TPU v7x, 128 devices: a whole 4x4x4 slice. The times are simulated.
128 devices in a mesh: rep: 2 (over core), tp: 32 (over y_lo, z, x), att: 2 (over y_hi).
Axes of the slice: x: 4, y: 4 (y_hi: 2, y_lo: 2; y = y_hi * 2 + y_lo), z: 4, core: 2. Of those that a mesh axis runs over, the one named last changes fastest.
Arguments:
- inputs: bfloat16 [2, 128, 12288], P(None, ('rep', 'tp', 'att')), may hold values from -6 to 6
- cotangent: bfloat16 [2, 128, 12288], P(None, ('rep', 'tp', 'att')), may hold values from -1.5 to 1.5
- gate_weight: bfloat16 [14336, 12288], P(('tp', 'att')), may hold values from -0.0546875 to 0.0546875
- up_weight: bfloat16 [14336, 12288], P(('tp', 'att')), may hold values from -0.0546875 to 0.0546875
- down_weight: bfloat16 [14336, 12288], P(('tp', 'att')), may hold values from -0.046875 to 0.046875
Outputs:
- input_grad: bfloat16 [2, 128, 12288], P(None, ('rep', 'tp', 'att'))
- gate_grad: bfloat16 [14336, 12288], P(('tp', 'att'), 'rep')
- up_grad: bfloat16 [14336, 12288], P(('tp', 'att'), 'rep')
- down_grad: bfloat16 [14336, 12288], P(('tp', 'att'), 'rep')
All inputs are finite; a program needn't handle non-finite values.
Results may differ from a plain program's by a relative error of at most 0.0054.
Values may be sent and summed in bfloat16 or wider, within the bound.
No kernel may reach another device: no remote copies, remote signals or barrier semaphores. Data moves between devices by JAX's collectives and lax.ppermute only.
A program may use at most 192 MiB of HBM per device.

v0:
```python
import jax
import jax.numpy as jnp
from jax import lax
from jax.sharding import PartitionSpec as P


def contract_last(left, right):
    return lax.dot_general(
        left, right, (((1,), (1,)), ((), ())), preferred_element_type=jnp.float32
    )


def contract_first(left, right):
    return lax.dot_general(
        left, right, (((0,), (0,)), ((), ())), preferred_element_type=jnp.float32
    )


def shards(inputs, cotangent, gate_weight, up_weight, down_weight):
    width = inputs.shape[2]
    local_ff = gate_weight.shape[0]
    gate_total = jnp.zeros((local_ff, width), jnp.float32)
    up_total = jnp.zeros((local_ff, width), jnp.float32)
    down_total = jnp.zeros((local_ff, width), jnp.float32)
    results = []
    for micro in range(inputs.shape[0]):
        stacked = jnp.stack([inputs[micro], cotangent[micro]])
        piece = lax.all_gather(stacked, ("tp", "att"), axis=1, tiled=True)
        rows_in = piece[0]
        rows_cot = piece[1]
        pre_gate = contract_last(rows_in, gate_weight)
        pre_up = contract_last(rows_in, up_weight)
        sig = jax.nn.sigmoid(pre_gate)
        act = pre_gate * sig
        hidden = (act * pre_up).astype(jnp.bfloat16)
        hidden_grad = contract_last(rows_cot, down_weight)
        recompute_gate_part = (hidden_grad * pre_up * sig * (1.0 + pre_gate * (1.0 - sig))).astype(
            jnp.bfloat16
        )
        recompute_up_part = (hidden_grad * act).astype(jnp.bfloat16)
        joined = jnp.concatenate(
            [rows_in, rows_cot, hidden, recompute_gate_part, recompute_up_part], axis=1
        )
        rows_in = joined[:, :width]
        rows_cot = joined[:, width : 2 * width]
        hidden = joined[:, 2 * width : 2 * width + local_ff]
        gate_part = joined[:, 2 * width + local_ff : 2 * width + 2 * local_ff]
        up_part = joined[:, 2 * width + 2 * local_ff :]
        summed = lax.psum_scatter(
            jnp.dot(gate_part, gate_weight, preferred_element_type=jnp.float32)
            + jnp.dot(up_part, up_weight, preferred_element_type=jnp.float32),
            ("tp", "att"),
            scatter_dimension=0,
            tiled=True,
        )
        results.append(summed.astype(jnp.bfloat16))
        gate_total = gate_total + contract_first(gate_part, rows_in)
        up_total = up_total + contract_first(up_part, rows_in)
        down_total = down_total + contract_first(hidden, rows_cot)
    gate_total, up_total, down_total = (
        lax.psum_scatter(gate_total, "rep", scatter_dimension=1, tiled=True),
        lax.psum_scatter(up_total, "rep", scatter_dimension=1, tiled=True),
        lax.psum_scatter(down_total, "rep", scatter_dimension=1, tiled=True),
    )
    input_grad = jnp.stack(results)
    return (
        input_grad,
        gate_total.astype(jnp.bfloat16),
        up_total.astype(jnp.bfloat16),
        down_total.astype(jnp.bfloat16),
    )


def solution(mesh):
    return jax.shard_map(
        shards,
        mesh=mesh,
        in_specs=(
            P(None, ("rep", "tp", "att"), None),
            P(None, ("rep", "tp", "att"), None),
            P(("tp", "att"), None),
            P(("tp", "att"), None),
            P(("tp", "att"), None),
        ),
        out_specs=(
            P(None, ("rep", "tp", "att"), None),
            P(("tp", "att"), "rep"),
            P(("tp", "att"), "rep"),
            P(("tp", "att"), "rep"),
        ),
        check_vma=False,
    )
```

profile of v0, /device:TPU:0, one launch (start us, length us, event | category | flops | bytes accessed | tf_op | source)
XLA Modules:
  0.0 1193.2 jit_solution(862975742515268396)
XLA Ops:
  7.2 0.0 all-gather.5.cloned.1.call-start
  7.2 1.1 fusion.13
  8.3 0.7 pad_maximum_fusion.1
  9.1 0.0 all-gather.5.cloned.1.call-update
  9.1 0.0 all-gather.3.cloned.1.call-start
  9.1 0.7 pad_maximum_fusion
  9.9 0.0 all-gather.3.cloned.1.call-update
  9.9 0.0 reduce-scatter.8.cloned.1.call-start
  9.9 337.9 %all-gather.5.cloned.1.call-done = bf16[2,64,12288]{2,0,1:T(2,128)(2,1)} async-done(((bf16[2,1,12288]{2,0,1:T(2,128)(2,1)}), bf16[2,64,12288]{2,0,1:T(2,128)(2,1)}) %all-gather.5.cloned.1.call-update) | async-done | bytes 3145744 | tf_op jit(solution)/shard_map/all_gather | solution.py:28
  347.9 9.2 fusion.12
  357.1 1.7 copy.33
  358.8 4.4 fusion.19
  363.2 4.4 fusion.18
  367.6 316.1 %all-gather.3.cloned.1.call-done = bf16[2,64,12288]{2,0,1:T(2,128)(2,1)} async-done(((bf16[2,1,12288]{2,0,1:T(2,128)(2,1)}), bf16[2,64,12288]{2,0,1:T(2,128)(2,1)}) %all-gather.3.cloned.1.call-update) | async-done | bytes 3145744 | tf_op jit(solution)/shard_map/all_gather | solution.py:28
  683.6 8.1 fusion.11
  691.7 1.7 copy.34
  693.4 4.4 fusion.16
  697.8 4.4 fusion.15
  702.2 0.0 copy-done.1
  702.2 0.0 copy-start
  702.2 2.7 fusion
  704.9 7.2 convolution_add_fusion
  712.1 0.0 reduce-scatter.8.cloned.1.call-update
  712.2 0.3 reduce-scatter.6.cloned.1.call-start
  712.4 6.1 multiply_convert_fusion.2
  718.6 6.1 multiply_convert_fusion.4
  724.7 1.6 fusion.22
  726.3 6.7 convolution_add_fusion.1
  732.9 0.0 reduce-scatter.6.cloned.1.call-update
  733.0 0.3 reduce-scatter.4.cloned.1.call-start
  733.3 1.6 fusion.21
  734.9 5.7 convolution_add_fusion.2
  740.6 0.0 reduce-scatter.4.cloned.1.call-update
  740.6 0.6 copy-done.3
  741.2 0.6 dynamic-slice
  741.8 3.8 fusion.20
  745.6 0.0 slice-start.1
  745.6 0.0 slice-start.3
  745.6 6.3 convolution_add_fusion.3
  751.9 1.1 fusion.17
  753.1 3.0 convolution_add_fusion.4
  756.0 413.2 %all-reduce.4 = (bf16[64,12288]{1,0:T(8,128)(2,1)}, bf16[64,12288]{1,0:T(8,128)(2,1)}) all-reduce(f32[64,12288]{1,0:T(8,128)S(1)} %convolution_add_fusion.3, f32[64,12288]{1,0:T(8,128)} %convolution_add_fusion.4), channel_id=3, replica_groups=mesh['rep'=2,'tp'=32,'att'=2] {'tp','att'}, use_global_device_ids=true, to_apply=%region_1.0.clone | all-reduce | flops 1572864 | bytes 9437184
  1169.3 1.6 fusion.5
  1170.9 1.6 fusion.6
  1172.5 0.7 pad_maximum_fusion.2
  1173.3 4.5 convert_element_type.43
  1177.7 4.5 convert_element_type.40
  1182.2 4.5 convert_element_type.39
  (16 shorter events, 0.0 us)
Async XLA Ops:
  7.2 340.7 %all-gather.5.cloned.1.call-start = ((), (), s32[]{:S(2)}) async-start(), calls=%async_computation.4 | async-start | bytes 3194880 | tf_op jit(solution)/shard_map/all_gather | solution.py:28
  9.1 674.6 %all-gather.3.cloned.1.call-start = ((), (), s32[]{:S(2)}) async-start(), calls=%async_computation.3 | async-start | bytes 3194880 | tf_op jit(solution)/shard_map/all_gather | solution.py:28
  9.9 1163.4 %reduce-scatter.8.cloned.1.call-start = ((), (), s32[]{:S(2)}) async-start(), calls=%async_computation.7 | async-start | bytes 16515072 | tf_op jit(solution)/shard_map/reduce_scatter | solution.py:63
  691.7 10.5 copy-start.1
  702.2 2.7 copy-start
  712.2 465.6 %reduce-scatter.6.cloned.1.call-start = ((), (), s32[]{:S(2)}) async-start(), calls=%async_computation.6 | async-start | bytes 16515072 | tf_op jit(solution)/shard_map/reduce_scatter | solution.py:62
  712.4 6.1 copy-start.2
  733.0 449.2 %reduce-scatter.4.cloned.1.call-start = ((), (), s32[]{:S(2)}) async-start(), calls=%async_computation.5 | async-start | bytes 16515072 | tf_op jit(solution)/shard_map/reduce_scatter | solution.py:61
  740.6 0.7 copy-start.3
  741.8 10.1 slice-start
  741.8 11.2 slice-start.2
  745.6 6.3 slice-start.1
  745.6 7.4 slice-start.3
Sparse Core Ops, SparseCore 0:
  10.2 337.6 all-gather.4
  350.1 333.5 all-gather.2
  712.3 20.4 reduce-scatter.7
  735.1 23.7 reduce-scatter.5
  761.1 23.7 reduce-scatter.3
where the time goes:
time: 1190 us
  waiting for transfers between devices  654 us (55%)
  blocking collectives  413 us (35%)
  matrix products  69.3 us (6%)
  local copies, waits for them, and re-layouts  26.3 us (2%)
  other arithmetic  15.6 us (1%)
  between operations  14 us (1%)
    all_gather x2, waiting for transfers between devices, shards(): piece = lax.all_gather(stacked, ('tp', 'att'), axis=1, tiled=True)  654 us
    unnamed x1, blocking collectives  413 us
    dot_general x6, matrix products, contract_last(): lax.dot_general(left, right, (((1,), (1,)), ((), ())), preferred_element_...  29.7 us
    dot_general x6, matrix products, contract_first(): lax.dot_general(left, right, (((0,), (0,)), ((), ())), preferred_element_...  25.5 us
  transfers between devices with their start and end apart: 5, of which 2 were waited for; matrix products, arithmetic and copies ran while one was open for 6% of the time, Pallas kernels for 0%

commit v1 on v0

v1 whole, which is shorter than its diff:
```python
import functools

import jax
import jax.numpy as jnp
import numpy as np
from jax import lax
from jax.experimental import pallas as pl
from jax.experimental.pallas import tpu as pltpu
from jax.sharding import PartitionSpec as P

AXES = ("rep", "tp", "att")
CHUNKS = (("x", "y", "z"), ("y", "z", "x"), ("z", "x", "y"))
GROUP = 32
VMEM_LIMIT = 56 * 1024 * 1024


def linear(core, x, y, z):
    return core * 64 + ((y % 2) * 16 + z * 4 + x) * 2 + y // 2


def pairs(moves, flip=0):
    result = []
    for core in range(2):
        dx, dy, dz = moves[core]
        for x in range(4):
            for y in range(4):
                for z in range(4):
                    result.append(
                        (linear(core, x, y, z), linear(core ^ flip, x ^ dx, y ^ dy, z ^ dz))
                    )
    return sorted(result)


def neighbour(axes, stage):
    moves = []
    for core in range(2):
        distance = 1 if core == stage else 3
        moves.append(tuple(distance if name in axes else 0 for name in "xyz"))
    return pairs(moves)


OTHER_CORE = pairs([(0, 0, 0)] * 2, flip=1)


def send(value, route):
    return lax.ppermute(value, AXES, route)


def label_order(axes):
    bit = {"x": 1, "y": 2, "z": 4}
    return [
        sum(bit[axis] for place, axis in enumerate(axes) if index >> place & 1)
        for index in range(8)
    ]


def forward_kernel(third, *refs):
    pieces, (gate_hbm, up_hbm, down_hbm), out_ref = refs[:24], refs[24:27], refs[27]
    rows_in, rows_cot, gate, up, down, sems, weight_sems = refs[28:]
    start = lax.axis_index("rep") * (3 * third)
    weight_copies = []
    for k in range(3):
        for i, (source, target) in enumerate(((gate_hbm, gate), (up_hbm, up), (down_hbm, down))):
            copy = pltpu.make_async_copy(
                source.at[:, pl.ds(pl.multiple_of(start + k * third, third), third)],
                target.at[:, pl.ds(k * third, third)],
                weight_sems.at[3 * k + i],
            )
            copy.start()
            weight_copies.append(copy)
    copies = []
    for k in range(3):
        for label in range(8):
            piece = pieces[8 * k + label]
            for i, target in enumerate((rows_in, rows_cot)):
                copy = pltpu.make_async_copy(
                    piece.at[i],
                    target.at[pl.ds(GROUP * label, GROUP), pl.ds(k * third, third)],
                    sems.at[16 * k + 2 * label + i],
                )
                copy.start()
                copies.append(copy)
    for k in range(3):
        columns = slice(k * third, (k + 1) * third)
        for copy in copies[16 * k : 16 * k + 16]:
            copy.wait()
        for i, (rows, weight) in enumerate(((rows_in, gate), (rows_in, up), (rows_cot, down))):
            weight_copies[3 * k + i].wait()
            product = lax.dot_general(
                rows[:, columns],
                weight[:, columns],
                (((1,), (1,)), ((), ())),
                preferred_element_type=jnp.float32,
            )
            if k == 0:
                out_ref[i] = product
            else:
                out_ref[i] += product


def forward(pieces, weights):
    local_ff, width = weights[0].shape
    half, third = width // 2, width // 6
    rows = 8 * GROUP
    any_spec = pl.BlockSpec(memory_space=pl.ANY)
    return pl.pallas_call(
        functools.partial(forward_kernel, third),
        out_shape=jax.ShapeDtypeStruct((3, rows, local_ff), jnp.float32),
        in_specs=[any_spec] * 27,
        out_specs=pl.BlockSpec(memory_space=pltpu.VMEM),
        scratch_shapes=[
            pltpu.VMEM((rows, half), jnp.bfloat16),
            pltpu.VMEM((rows, half), jnp.bfloat16),
            pltpu.VMEM((local_ff, half), jnp.bfloat16),
            pltpu.VMEM((local_ff, half), jnp.bfloat16),
            pltpu.VMEM((local_ff, half), jnp.bfloat16),
            pltpu.SemaphoreType.DMA((48,)),
            pltpu.SemaphoreType.DMA((9,)),
        ],
        compiler_params=pltpu.CompilerParams(vmem_limit_bytes=VMEM_LIMIT),
        cost_estimate=pl.CostEstimate(
            flops=6 * rows * local_ff * half, bytes_accessed=16 * 2**20, transcendentals=0
        ),
    )(*pieces, *weights)


def permuted(one_hot, value):
    high = value.astype(jnp.bfloat16)
    rest = value - high.astype(jnp.float32)
    middle = rest.astype(jnp.bfloat16)
    low = (rest - middle.astype(jnp.float32)).astype(jnp.bfloat16)
    return (
        jnp.dot(one_hot, high, preferred_element_type=jnp.float32)
        + jnp.dot(one_hot, middle, preferred_element_type=jnp.float32)
        + jnp.dot(one_hot, low, preferred_element_type=jnp.float32)
    )


def middle_kernel(third, *refs):
    part, other, one_hot, gate_hbm, up_hbm = refs[:5]
    sends, keeps, (gate_out, up_out, hidden_out) = refs[5:8], refs[8:11], refs[11:14]
    gate, up, weight_sems = refs[14:]
    start = lax.axis_index("rep") * (3 * third)
    copies = []
    for k in range(3):
        for i, (source, target) in enumerate(((gate_hbm, gate), (up_hbm, up))):
            copy = pltpu.make_async_copy(
                source.at[:, pl.ds(pl.multiple_of(start + k * third, third), third)],
                target.at[:, pl.ds(k * third, third)],
                weight_sems.at[2 * k + i],
            )
            copy.start()
            copies.append(copy)
    matrix = one_hot[...]
    pre_gate = part[0] + permuted(matrix, other[0])
    pre_up = part[1] + permuted(matrix, other[1])
    hidden_grad = part[2] + permuted(matrix, other[2])
    sig = jax.nn.sigmoid(pre_gate)
    act = pre_gate * sig
    hidden_out[...] = (act * pre_up).astype(jnp.bfloat16)
    gate_out[...] = (hidden_grad * pre_up * sig * (1.0 + pre_gate * (1.0 - sig))).astype(
        jnp.bfloat16
    )
    up_out[...] = (hidden_grad * act).astype(jnp.bfloat16)
    for k in range(3):
        columns = slice(k * third, (k + 1) * third)
        order = label_order(CHUNKS[k])
        copies[2 * k].wait()
        copies[2 * k + 1].wait()
        for first, target in ((4, sends[k]), (0, keeps[k])):
            picks = [slice(GROUP * b, GROUP * b + GROUP) for b in order[first : first + 4]]
            left = jnp.concatenate([gate_out[pick] for pick in picks], axis=0)
            right = jnp.concatenate([up_out[pick] for pick in picks], axis=0)
            target[...] = (
                jnp.dot(left, gate[:, columns], preferred_element_type=jnp.float32)
                + jnp.dot(right, up[:, columns], preferred_element_type=jnp.float32)
            ).astype(target.dtype)


def middle(part, other, one_hot, gate_weight, up_weight):
    local_ff, width = gate_weight.shape
    half, third = width // 2, width // 6
    rows = 8 * GROUP
    vmem_spec, any_spec = (pl.BlockSpec(memory_space=s) for s in (pltpu.VMEM, pl.ANY))
    small = jax.ShapeDtypeStruct((rows, local_ff), jnp.bfloat16)
    return pl.pallas_call(
        functools.partial(middle_kernel, third),
        out_shape=[jax.ShapeDtypeStruct((rows // 2, third), jnp.bfloat16)] * 3
        + [jax.ShapeDtypeStruct((rows // 2, third), jnp.float32)] * 3
        + [small] * 3,
        in_specs=[vmem_spec] * 3 + [any_spec] * 2,
        out_specs=[vmem_spec] * 9,
        scratch_shapes=[
            pltpu.VMEM((local_ff, half), jnp.bfloat16),
            pltpu.VMEM((local_ff, half), jnp.bfloat16),
            pltpu.SemaphoreType.DMA((6,)),
        ],
        compiler_params=pltpu.CompilerParams(vmem_limit_bytes=VMEM_LIMIT),
        cost_estimate=pl.CostEstimate(
            flops=4 * rows * local_ff * half, bytes_accessed=14 * 2**20, transcendentals=0
        ),
    )(part, other, one_hot, gate_weight, up_weight)


def weight_kernel(third, *refs):
    pieces, (gate_part, up_part, hidden) = refs[:24], refs[24:27]
    outs, (rows_in, rows_cot, results, sems, out_sems) = refs[27:30], refs[30:]
    copies = []
    for k in range(3):
        for label in range(8):
            piece = pieces[8 * k + label]
            for i, target in enumerate((rows_in, rows_cot)):
                copy = pltpu.make_async_copy(
                    piece.at[i],
                    target.at[pl.ds(GROUP * label, GROUP), pl.ds(k * third, third)],
                    sems.at[16 * k + 2 * label + i],
                )
                copy.start()
                copies.append(copy)
    out_copies = []
    for k in range(3):
        columns = slice(k * third, (k + 1) * third)
        for copy in copies[16 * k : 16 * k + 16]:
            copy.wait()
        for i, (left, rows) in enumerate(
            ((gate_part, rows_in), (up_part, rows_in), (hidden, rows_cot))
        ):
            results[i, :, columns] = lax.dot_general(
                left[...],
                rows[:, columns],
                (((0,), (0,)), ((), ())),
                preferred_element_type=jnp.float32,
            ).astype(jnp.bfloat16)
            copy = pltpu.make_async_copy(
                results.at[i, :, pl.ds(k * third, third)],
                outs[i].at[:, pl.ds(k * third, third)],
                out_sems.at[3 * k + i],
            )
            copy.start()
            out_copies.append(copy)
    for copy in out_copies:
        copy.wait()


def weight_grads(pieces, gate_part, up_part, hidden, third):
    rows, local_ff = gate_part.shape
    half = 3 * third
    vmem_spec, any_spec = (pl.BlockSpec(memory_space=s) for s in (pltpu.VMEM, pl.ANY))
    return pl.pallas_call(
        functools.partial(weight_kernel, third),
        out_shape=[jax.ShapeDtypeStruct((local_ff, half), jnp.bfloat16)] * 3,
        in_specs=[any_spec] * 24 + [vmem_spec] * 3,
        out_specs=[any_spec] * 3,
        scratch_shapes=[
            pltpu.VMEM((rows, half), jnp.bfloat16),
            pltpu.VMEM((rows, half), jnp.bfloat16),
            pltpu.VMEM((3, local_ff, half), jnp.bfloat16),
            pltpu.SemaphoreType.DMA((48,)),
            pltpu.SemaphoreType.DMA((9,)),
        ],
        compiler_params=pltpu.CompilerParams(vmem_limit_bytes=VMEM_LIMIT),
        cost_estimate=pl.CostEstimate(
            flops=6 * rows * local_ff * half, bytes_accessed=16 * 2**20, transcendentals=0
        ),
    )(*pieces, gate_part, up_part, hidden)


def cross_core_rows():
    matrix = np.zeros((8 * GROUP, 8 * GROUP), np.float32)
    for high in range(8):
        for low in range(8):
            for row in range(4):
                matrix[(high * 8 + low) * 4 + row, (low * 8 + high) * 4 + row] = 1.0
    return jnp.asarray(matrix, jnp.bfloat16)


def shards(inputs, cotangent, gate_weight, up_weight, down_weight):
    core = lax.axis_index("rep")
    width = inputs.shape[2]
    half, third = width // 2, width // 6
    micro = inputs.shape[0]

    rows = jnp.stack([inputs[:, 0], cotangent[:, 0]])
    low, high = rows[:, :, :half], rows[:, :, half:]
    mine = jnp.where(core == 0, low, high)
    theirs = send(jnp.where(core == 0, high, low), OTHER_CORE)
    block = jnp.concatenate(
        [jnp.where(core == 0, mine, theirs), jnp.where(core == 0, theirs, mine)], axis=1
    )
    block = jnp.concatenate(
        [block] + [send(block, neighbour(axes, 0)) for axes in ("x", "y", "xy")], axis=1
    )
    block = jnp.concatenate([block, send(block, neighbour("z", 0))], axis=1)
    pieces = []
    for k in range(3):
        held = [block[:, :, k * third : (k + 1) * third]]
        for axis in CHUNKS[k]:
            held = held + [send(piece, neighbour(axis, 1)) for piece in held]
        labelled = dict(zip(label_order(CHUNKS[k]), held))
        pieces += [labelled[label] for label in range(8)]

    part = forward(pieces, (gate_weight, up_weight, down_weight))
    other = send(part, OTHER_CORE)
    results = middle(part, other, cross_core_rows(), gate_weight, up_weight)
    outgoing, sums, (gate_part, up_part, hidden) = results[:3], results[3:6], results[6:]
    gate_grad, up_grad, down_grad = weight_grads(pieces, gate_part, up_part, hidden, third)

    for stage in (2, 1, 0):
        sums = [
            value + send(out, neighbour(CHUNKS[k][stage], 1)).astype(jnp.float32)
            for k, (value, out) in enumerate(zip(sums, outgoing))
        ]
        if stage:
            cut = sums[0].shape[0] // 2
            outgoing = [value[cut:].astype(jnp.bfloat16) for value in sums]
            sums = [value[:cut] for value in sums]
    value = jnp.concatenate(sums, axis=1)
    cut = value.shape[0] // 2
    value = value[:cut] + send(value[cut:].astype(jnp.bfloat16), neighbour("z", 0)).astype(
        jnp.float32
    )
    cut = value.shape[0] // 4
    value = value[:cut] + sum(
        send(value[i * cut : (i + 1) * cut].astype(jnp.bfloat16), neighbour(axes, 0)).astype(
            jnp.float32
        )
        for i, axes in ((1, "x"), (2, "y"), (3, "xy"))
    )
    value = value.astype(jnp.bfloat16)
    mine = jnp.where(core == 0, value[:micro], value[micro:])
    theirs = send(jnp.where(core == 0, value[micro:], value[:micro]), OTHER_CORE)
    input_grad = jnp.concatenate(
        [jnp.where(core == 0, mine, theirs), jnp.where(core == 0, theirs, mine)], axis=1
    )[:, None, :]
    return input_grad, gate_grad, up_grad, down_grad


def solution(mesh):
    return jax.shard_map(
        shards,
        mesh=mesh,
        in_specs=(
            P(None, ("rep", "tp", "att"), None),
            P(None, ("rep", "tp", "att"), None),
            P(("tp", "att"), None),
            P(("tp", "att"), None),
            P(("tp", "att"), None),
        ),
        out_specs=(
            P(None, ("rep", "tp", "att"), None),
            P(("tp", "att"), "rep"),
            P(("tp", "att"), "rep"),
            P(("tp", "att"), "rep"),
        ),
        check_vma=False,
    )
```

time: 1190 us -> 140 us (0.12)
  waiting for transfers between devices: 654 us -> 41.5 us
  blocking collectives: 413 us -> 0 us
  matrix products: 69.3 us -> 0 us
  starting transfers between devices: 0.69 us -> 61 us
  Pallas kernels: 0 us -> 24.2 us
  local copies, waits for them, and re-layouts: 26.3 us -> 4.65 us
  between operations: 14 us -> 1.14 us
    all_gather x2 -> x0, waiting for transfers between devices: 654 us -> none  [shards(): piece = lax.all_gather(stacked, ('tp', 'att'), axis=1, tiled=True)]
    unnamed x1 -> x0, blocking collectives: 413 us -> none
    dot_general x16 -> x0, matrix products: 69.3 us -> none  [the longest x6 29.7 us: contract_last(): lax.dot_general(left, right, (((1,), (1,)), ((), ())), preferred_element_...]
    ppermute x0 -> x41, starting transfers between devices: none -> 61 us  [send(): return lax.ppermute(value, AXES, route)]
    ppermute x0 -> x41, waiting for transfers between devices: none -> 41.5 us  [send(): return lax.ppermute(value, AXES, route)]
    pallas_call x0 -> x3, Pallas kernels: none -> 24.2 us  [the longest x1 10.6 us: forward(): pl.pallas_call(functools.partial(forward_kernel, third), out_shape=jax.Sh...]
    slice x3 -> x9, local copies, waits for them, and re-layouts: 18.4 us -> 0.29 us  [the longest x6 0.14 us: shards(): outgoing = [value[cut:].astype(jnp.bfloat16) for value in sums]]
    convert_element_type x3 -> x1, other arithmetic: 13.4 us -> 0.05 us  [shards(): value = value.astype(jnp.bfloat16)]
  transfers between devices with their start and end apart: 5 -> 41, of which waited for: 2 -> 22; matrix products, arithmetic and copies ran while one was open for 6% -> 2% of each run, Pallas kernels for 0% -> 5%
where the time goes in v1:
time: 140 us; the launch traced here: 138 us
  starting transfers between devices  61 us (44%)
  waiting for transfers between devices  41.5 us (30%)
  Pallas kernels  24.2 us (17%)
  other arithmetic  5.8 us (4%)
  local copies, waits for them, and re-layouts  4.65 us (3%)
    ppermute x41, starting transfers between devices, send(): return lax.ppermute(value, AXES, route)  61 us
    ppermute x41, waiting for transfers between devices, send(): return lax.ppermute(value, AXES, route)  41.5 us
    pallas_call x1, Pallas kernels, forward(): pl.pallas_call(functools.partial(forward_kernel, third), out_shape=jax.Sh...  10.6 us
    pallas_call x1, Pallas kernels, weight_grads(): pl.pallas_call(functools.partial(weight_kernel, third), out_shape=[jax.Sh...  6.94 us
    pallas_call x1, Pallas kernels, middle(): pl.pallas_call(functools.partial(middle_kernel, third), out_shape=[jax.Sh...  6.64 us
    add x9, other arithmetic, shards(): value + send(out, neighbour(CHUNKS[k][stage], 1)).astype(jnp.float32)  2.99 us
  transfers between devices with their start and end apart: 41, of which 22 were waited for; matrix products, arithmetic and copies ran while one was open for 2% of the time, Pallas kernels for 5%

profile of v1, /device:TPU:0, one launch (start us, length us, event | category | flops | bytes accessed | tf_op | source)
XLA Modules:
  0.0 138.2 jit_solution(5169364959272802725)
XLA Ops:
  1.6 1.2 collective-permute-done
  3.8 2.7 %collective-permute-start.3 = (bf16[2,4,6144]{2,1,0:T(4,128)(2,1)S(1)}, bf16[2,4,6144]{2,1,0:T(4,128)(2,1)S(1)}, u32[]{:S(2)}, u32[]{:S(2)}) collective-permute-start(bf16[2,4,6144]{2,1,0:T(4,128)(2,1)S(1)} %pad_maximum_fusion.1), channel_id=1, source_target_pairs={{0,34},{1,35},{2,32},{3,33},{4,38},{5,39},{6,36},{7,37},{8,42},{9,... | collective-permute-start | bytes 294920 | tf_op jit(solution)/shard_map/ppermute | solution.py:46
  7.4 2.0 %collective-permute-done.3 = bf16[2,4,6144]{2,1,0:T(4,128)(2,1)S(1)} collective-permute-done((bf16[2,4,6144]{2,1,0:T(4,128)(2,1)S(1)}, bf16[2,4,6144]{2,1,0:T(4,128)(2,1)S(1)}, u32[]{:S(2)}, u32[]{:S(2)}) %collective-permute-start.3) | collective-permute-done | bytes 98336 | tf_op jit(solution)/shard_map/ppermute | solution.py:46
  9.4 1.7 %collective-permute-done.2 = bf16[2,4,6144]{2,1,0:T(4,128)(2,1)S(1)} collective-permute-done((bf16[2,4,6144]{2,1,0:T(4,128)(2,1)S(1)}, bf16[2,4,6144]{2,1,0:T(4,128)(2,1)S(1)}, u32[]{:S(2)}, u32[]{:S(2)}) %collective-permute-start.2) | collective-permute-done | bytes 98336 | tf_op jit(solution)/shard_map/ppermute | solution.py:46
  12.0 2.0 %collective-permute-start.4 = (bf16[2,16,6144]{2,1,0:T(8,128)(2,1)S(1)}, bf16[2,16,6144]{2,1,0:T(8,128)(2,1)S(1)}, u32[]{:S(2)}, u32[]{:S(2)}) collective-permute-start(bf16[2,16,6144]{2,1,0:T(8,128)(2,1)S(1)} %concatenate.18), channel_id=1, source_target_pairs={{0,8},{1,9},{2,10},{3,11},{4,12},{5,13},{6,14},{7,15},{8,0},{9,1},... | collective-permute-start | bytes 1179656 | tf_op jit(solution)/shard_map/ppermute | solution.py:46
  14.0 5.9 %collective-permute-done.4 = bf16[2,16,6144]{2,1,0:T(8,128)(2,1)S(1)} collective-permute-done((bf16[2,16,6144]{2,1,0:T(8,128)(2,1)S(1)}, bf16[2,16,6144]{2,1,0:T(8,128)(2,1)S(1)}, u32[]{:S(2)}, u32[]{:S(2)}) %collective-permute-start.4) | collective-permute-done | bytes 393248 | tf_op jit(solution)/shard_map/ppermute | solution.py:46
  20.6 4.1 %collective-permute-start.22 = (bf16[2,32,2048]{2,1,0:T(8,128)(2,1)S(1)}, bf16[2,32,2048]{2,1,0:T(8,128)(2,1)S(1)}, u32[]{:S(2)}, u32[]{:S(2)}) collective-permute-start(bf16[2,32,2048]{2,1,0:T(8,128)(2,1)S(1)} %get-tuple-element.32.refs_16_), channel_id=1, source_target_pairs={{0,24},{1,25},{2,26},{3,27},{4,28},{5,29},{6,30},{7,31},{8,16},{9,... | collective-permute-start | bytes 786440 | tf_op jit(solution)/shard_map/ppermute | solution.py:46
  24.7 3.0 %collective-permute-start.20 = (bf16[2,32,2048]{2,1,0:T(8,128)(2,1)S(1)}, bf16[2,32,2048]{2,1,0:T(8,128)(2,1)S(1)}, u32[]{:S(2)}, u32[]{:S(2)}) collective-permute-start(bf16[2,32,2048]{2,1,0:T(8,128)(2,1)S(1)} %get-tuple-element.32.refs_16_), channel_id=1, source_target_pairs={{0,33},{1,32},{2,35},{3,34},{4,37},{5,36},{6,39},{7,38},{8,41},{9,... | collective-permute-start | bytes 786440 | tf_op jit(solution)/shard_map/ppermute | solution.py:46
  27.7 2.1 %collective-permute-start.19 = (bf16[2,32,2048]{2,1,0:T(8,128)(2,1)S(1)}, bf16[2,32,2048]{2,1,0:T(8,128)(2,1)S(1)}, u32[]{:S(2)}, u32[]{:S(2)}) collective-permute-start(bf16[2,32,2048]{2,1,0:T(8,128)(2,1)S(1)} %get-tuple-element.32.refs_16_), channel_id=1, source_target_pairs={{0,6},{1,7},{2,4},{3,5},{4,2},{5,3},{6,0},{7,1},{8,14},{9,15},{10,... | collective-permute-start | bytes 786440 | tf_op jit(solution)/shard_map/ppermute | solution.py:46
  30.1 1.1 collective-permute-start.12
  32.3 2.1 %collective-permute-start.8 = (bf16[2,32,2048]{2,1,0:T(8,128)(2,1)S(1)}, bf16[2,32,2048]{2,1,0:T(8,128)(2,1)S(1)}, u32[]{:S(2)}, u32[]{:S(2)}) collective-permute-start(bf16[2,32,2048]{2,1,0:T(8,128)(2,1)S(1)} %get-tuple-element.34.refs_0_), channel_id=1, source_target_pairs={{0,24},{1,25},{2,26},{3,27},{4,28},{5,29},{6,30},{7,31},{8,16},{9,... | collective-permute-start | bytes 786440 | tf_op jit(solution)/shard_map/ppermute | solution.py:46
  35.3 2.1 %collective-permute-start.6 = (bf16[2,32,2048]{2,1,0:T(8,128)(2,1)S(1)}, bf16[2,32,2048]{2,1,0:T(8,128)(2,1)S(1)}, u32[]{:S(2)}, u32[]{:S(2)}) collective-permute-start(bf16[2,32,2048]{2,1,0:T(8,128)(2,1)S(1)} %get-tuple-element.34.refs_0_), channel_id=1, source_target_pairs={{0,33},{1,32},{2,35},{3,34},{4,37},{5,36},{6,39},{7,38},{8,41},{9,... | collective-permute-start | bytes 786440 | tf_op jit(solution)/shard_map/ppermute | solution.py:46
  37.4 2.1 %collective-permute-start.5 = (bf16[2,32,2048]{2,1,0:T(8,128)(2,1)S(1)}, bf16[2,32,2048]{2,1,0:T(8,128)(2,1)S(1)}, u32[]{:S(2)}, u32[]{:S(2)}) collective-permute-start(bf16[2,32,2048]{2,1,0:T(8,128)(2,1)S(1)} %get-tuple-element.34.refs_0_), channel_id=1, source_target_pairs={{0,6},{1,7},{2,4},{3,5},{4,2},{5,3},{6,0},{7,1},{8,14},{9,15},{10,... | collective-permute-start | bytes 786440 | tf_op jit(solution)/shard_map/ppermute | solution.py:46
  41.8 2.1 %collective-permute-start.21 = (bf16[2,32,2048]{2,1,0:T(8,128)(2,1)S(1)}, bf16[2,32,2048]{2,1,0:T(8,128)(2,1)S(1)}, u32[]{:S(2)}, u32[]{:S(2)}) collective-permute-start(bf16[2,32,2048]{2,1,0:T(8,128)(2,1)S(1)} %collective-permute-done.19.refs_17_), channel_id=1, source_target_pairs={{0,33},{1,32},{2,35},{3,34},{4,37},{5,36},{6,39},{7,38},{8,41},{9,... | collective-permute-start | bytes 786440 | tf_op jit(solution)/shard_map/ppermute | solution.py:46
  43.9 2.1 %collective-permute-start.16 = (bf16[2,32,2048]{2,1,0:T(8,128)(2,1)S(1)}, bf16[2,32,2048]{2,1,0:T(8,128)(2,1)S(1)}, u32[]{:S(2)}, u32[]{:S(2)}) collective-permute-start(bf16[2,32,2048]{2,1,0:T(8,128)(2,1)S(1)} %collective-permute-done.15.refs_12_), channel_id=1, source_target_pairs={{0,6},{1,7},{2,4},{3,5},{4,2},{5,3},{6,0},{7,1},{8,14},{9,15},{10,... | collective-permute-start | bytes 786440 | tf_op jit(solution)/shard_map/ppermute | solution.py:46
  48.3 2.1 %collective-permute-start.7 = (bf16[2,32,2048]{2,1,0:T(8,128)(2,1)S(1)}, bf16[2,32,2048]{2,1,0:T(8,128)(2,1)S(1)}, u32[]{:S(2)}, u32[]{:S(2)}) collective-permute-start(bf16[2,32,2048]{2,1,0:T(8,128)(2,1)S(1)} %collective-permute-done.5.refs_1_), channel_id=1, source_target_pairs={{0,33},{1,32},{2,35},{3,34},{4,37},{5,36},{6,39},{7,38},{8,41},{9,... | collective-permute-start | bytes 786440 | tf_op jit(solution)/shard_map/ppermute | solution.py:46
  50.4 1.2 collective-permute-start.9
  51.5 2.1 %collective-permute-start.10 = (bf16[2,32,2048]{2,1,0:T(8,128)(2,1)S(1)}, bf16[2,32,2048]{2,1,0:T(8,128)(2,1)S(1)}, u32[]{:S(2)}, u32[]{:S(2)}) collective-permute-start(bf16[2,32,2048]{2,1,0:T(8,128)(2,1)S(1)} %collective-permute-done.6.refs_2_), channel_id=1, source_target_pairs={{0,24},{1,25},{2,26},{3,27},{4,28},{5,29},{6,30},{7,31},{8,16},{9,... | collective-permute-start | bytes 786440 | tf_op jit(solution)/shard_map/ppermute | solution.py:46
  53.6 1.2 collective-permute-start.25
  54.8 2.1 %collective-permute-start.18 = (bf16[2,32,2048]{2,1,0:T(8,128)(2,1)S(1)}, bf16[2,32,2048]{2,1,0:T(8,128)(2,1)S(1)}, u32[]{:S(2)}, u32[]{:S(2)}) collective-permute-start(bf16[2,32,2048]{2,1,0:T(8,128)(2,1)S(1)} %collective-permute-done.17.refs_14_), channel_id=1, source_target_pairs={{0,6},{1,7},{2,4},{3,5},{4,2},{5,3},{6,0},{7,1},{8,14},{9,15},{10,... | collective-permute-start | bytes 786440 | tf_op jit(solution)/shard_map/ppermute | solution.py:46
  56.9 2.1 %collective-permute-start.11 = (bf16[2,32,2048]{2,1,0:T(8,128)(2,1)S(1)}, bf16[2,32,2048]{2,1,0:T(8,128)(2,1)S(1)}, u32[]{:S(2)}, u32[]{:S(2)}) collective-permute-start(bf16[2,32,2048]{2,1,0:T(8,128)(2,1)S(1)} %collective-permute-done.7.refs_3_), channel_id=1, source_target_pairs={{0,24},{1,25},{2,26},{3,27},{4,28},{5,29},{6,30},{7,31},{8,16},{9,... | collective-permute-start | bytes 786440 | tf_op jit(solution)/shard_map/ppermute | solution.py:46
  59.0 1.7 %collective-permute-done.10.refs_6_ = bf16[2,32,2048]{2,1,0:T(8,128)(2,1)S(1)} collective-permute-done((bf16[2,32,2048]{2,1,0:T(8,128)(2,1)S(1)}, bf16[2,32,2048]{2,1,0:T(8,128)(2,1)S(1)}, u32[]{:S(2)}, u32[]{:S(2)}) %collective-permute-start.10) | collective-permute-done | bytes 262176 | tf_op jit(solution)/shard_map/ppermute | solution.py:46
  61.2 1.2 collective-permute-done.18.refs_15_
  62.4 2.1 %collective-permute-done.11.refs_7_ = bf16[2,32,2048]{2,1,0:T(8,128)(2,1)S(1)} collective-permute-done((bf16[2,32,2048]{2,1,0:T(8,128)(2,1)S(1)}, bf16[2,32,2048]{2,1,0:T(8,128)(2,1)S(1)}, u32[]{:S(2)}, u32[]{:S(2)}) %collective-permute-start.11) | collective-permute-done | bytes 262176 | tf_op jit(solution)/shard_map/ppermute | solution.py:46
  65.4 10.6 %shard_map.93.refs_0_ = f32[3,256,224]{2,1,0:T(8,128)} custom-call(bf16[2,32,2048]{2,1,0:T(8,128)(2,1)} %copy-done.2, bf16[2,32,2048]{2,1,0:T(8,128)(2,1)} %copy-done.12, bf16[2,32,2048]{2,1,0:T(8,128)(2,1)} %copy-done.11, bf16[2,32,2048]{2,1,0:T(8,128)(2,1)} %copy-done.19, bf16[2,32,2048]{2,1,0:T(8,128)(2,1)} %copy-done.10, ...), custom_call_target="tpu_custom_call" | custom-call | flops 2113929216 | bytes 16777216 | tf_op jit(solution)/shard_map/pallas_call | solution.py:106
  76.0 1.4 %copy.10 = f32[3,256,224]{1,2,0:T(8,128)S(1)} copy(f32[3,256,224]{2,1,0:T(8,128)} %shard_map.93.refs_0_) | data formatting | bytes 1376256 | tf_op jit(solution)/shard_map/pallas_call | solution.py:106
  77.7 2.1 %collective-permute-done.26 = f32[3,256,224]{1,2,0:T(8,128)S(1)} collective-permute-done((f32[3,256,224]{1,2,0:T(8,128)S(1)}, f32[3,256,224]{1,2,0:T(8,128)S(1)}, u32[]{:S(2)}, u32[]{:S(2)}) %collective-permute-start.26) | collective-permute-done | bytes 688160 | tf_op jit(solution)/shard_map/ppermute | solution.py:46
  79.8 1.2 copy.11.refs_1_
  81.0 6.6 %shard_map.94 = (bf16[128,2048]{1,0:T(8,128)(2,1)}, bf16[128,2048]{1,0:T(8,128)(2,1)}, bf16[128,2048]{1,0:T(8,128)(2,1)}, f32[128,2048]{1,0:T(8,128)}, f32[128,2...) custom-call(f32[3,256,224]{2,1,0:T(8,128)} %shard_map.93.refs_0_, ...), custom_call_target="tpu_custom_call" | custom-call | flops 1409286144 | bytes 14680064 | tf_op jit(solution)/shard_map/pallas_call | solution.py:186
  87.6 2.2 %collective-permute-start.27 = (bf16[128,2048]{1,0:T(8,128)(2,1)}, bf16[128,2048]{1,0:T(8,128)(2,1)S(1)}, u32[]{:S(2)}, u32[]{:S(2)}) collective-permute-start(bf16[128,2048]{1,0:T(8,128)(2,1)} %get-tuple-element.17), channel_id=1, source_target_pairs={{0,24},{1,25},{2,26},{3,27},{4,28},{5,29},{6,30},{7,31},{8,16},{9,... | collective-permute-start | bytes 1572872 | tf_op jit(solution)/shard_map/ppermute | solution.py:46
  89.8 1.2 collective-permute-start.30
  91.0 1.2 collective-permute-start.33
  92.2 6.1 %collective-permute-done.27 = bf16[128,2048]{1,0:T(8,128)(2,1)S(1)} collective-permute-done((bf16[128,2048]{1,0:T(8,128)(2,1)}, bf16[128,2048]{1,0:T(8,128)(2,1)S(1)}, u32[]{:S(2)}, u32[]{:S(2)}) %collective-permute-start.27) | collective-permute-done | bytes 524320 | tf_op jit(solution)/shard_map/ppermute | solution.py:46
  98.3 1.3 convert_add_fusion.2
  99.7 1.2 collective-permute-start.28
  100.9 1.3 convert_add_fusion.1
  102.3 2.2 %collective-permute-start.31 = (bf16[64,2048]{1,0:T(8,128)(2,1)S(1)}, bf16[64,2048]{1,0:T(8,128)(2,1)S(1)}, u32[]{:S(2)}, u32[]{:S(2)}) collective-permute-start(bf16[64,2048]{1,0:T(8,128)(2,1)S(1)} %slice.173), channel_id=1, source_target_pairs={{0,24},{1,25},{2,26},{3,27},{4,28},{5,29},{6,30},{7,31},{8,16},{9,... | collective-permute-start | bytes 786440 | tf_op jit(solution)/shard_map/ppermute | solution.py:46
  104.6 1.3 collective-permute-start.34
  105.9 1.4 %collective-permute-done.28 = bf16[64,2048]{1,0:T(8,128)(2,1)S(1)} collective-permute-done((bf16[64,2048]{1,0:T(8,128)(2,1)S(1)}, bf16[64,2048]{1,0:T(8,128)(2,1)S(1)}, u32[]{:S(2)}, u32[]{:S(2)}) %collective-permute-start.28) | collective-permute-done | bytes 262176 | tf_op jit(solution)/shard_map/ppermute | solution.py:46
  107.4 1.2 collective-permute-start.29
  108.6 1.3 collective-permute-done.31
  110.0 2.2 %collective-permute-start.32 = (bf16[32,2048]{1,0:T(8,128)(2,1)S(1)}, bf16[32,2048]{1,0:T(8,128)(2,1)S(1)}, u32[]{:S(2)}, u32[]{:S(2)}) collective-permute-start(bf16[32,2048]{1,0:T(8,128)(2,1)S(1)} %slice.177), channel_id=1, source_target_pairs={{0,33},{1,32},{2,35},{3,34},{4,37},{5,36},{6,39},{7,38},{8,41},{9,... | collective-permute-start | bytes 393224 | tf_op jit(solution)/shard_map/ppermute | solution.py:46
  112.4 2.1 %collective-permute-start.35 = (bf16[32,2048]{1,0:T(8,128)(2,1)S(1)}, bf16[32,2048]{1,0:T(8,128)(2,1)S(1)}, u32[]{:S(2)}, u32[]{:S(2)}) collective-permute-start(bf16[32,2048]{1,0:T(8,128)(2,1)S(1)} %slice.176), channel_id=1, source_target_pairs={{0,24},{1,25},{2,26},{3,27},{4,28},{5,29},{6,30},{7,31},{8,16},{9,... | collective-permute-start | bytes 393224 | tf_op jit(solution)/shard_map/ppermute | solution.py:46
  114.5 1.7 %collective-permute-done.32 = bf16[32,2048]{1,0:T(8,128)(2,1)S(1)} collective-permute-done((bf16[32,2048]{1,0:T(8,128)(2,1)S(1)}, bf16[32,2048]{1,0:T(8,128)(2,1)S(1)}, u32[]{:S(2)}, u32[]{:S(2)}) %collective-permute-start.32) | collective-permute-done | bytes 131104 | tf_op jit(solution)/shard_map/ppermute | solution.py:46
  116.3 2.3 %collective-permute-done.35 = bf16[32,2048]{1,0:T(8,128)(2,1)S(1)} collective-permute-done((bf16[32,2048]{1,0:T(8,128)(2,1)S(1)}, bf16[32,2048]{1,0:T(8,128)(2,1)S(1)}, u32[]{:S(2)}, u32[]{:S(2)}) %collective-permute-start.35) | collective-permute-done | bytes 131104 | tf_op jit(solution)/shard_map/ppermute | solution.py:46
  118.8 5.7 %collective-permute-done.36 = bf16[16,6144]{1,0:T(8,128)(2,1)S(1)} collective-permute-done((bf16[16,6144]{1,0:T(8,128)(2,1)S(1)}, bf16[16,6144]{1,0:T(8,128)(2,1)S(1)}, u32[]{:S(2)}, u32[]{:S(2)}) %collective-permute-start.36) | collective-permute-done | bytes 196640 | tf_op jit(solution)/shard_map/ppermute | solution.py:46
  125.7 2.4 %collective-permute-start.38 = (bf16[4,6144]{1,0:T(4,128)(2,1)S(1)}, bf16[4,6144]{1,0:T(4,128)(2,1)S(1)}, u32[]{:S(2)}, u32[]{:S(2)}) collective-permute-start(bf16[4,6144]{1,0:T(4,128)(2,1)S(1)} %get-tuple-element.37), channel_id=1, source_target_pairs={{0,32},{1,33},{2,34},{3,35},{4,36},{5,37},{6,38},{7,39},{8,40},{9,... | collective-permute-start | bytes 147464 | tf_op jit(solution)/shard_map/ppermute | solution.py:46
  130.5 6.9 %shard_map.95 = (bf16[224,6144]{1,0:T(8,128)(2,1)}, bf16[224,6144]{1,0:T(8,128)(2,1)}, bf16[224,6144]{1,0:T(8,128)(2,1)}) custom-call(bf16[2,32,2048]{2,1,0:T(8,128)(2,1)} %copy-done.2, bf16[2,32,2048]{2,1,0:T(8,128)(2,1)} %copy-done.12, bf16[2,32,2048]{2,1,0:T(8,128)(2,1)} %copy-done.11, bf16[2,32,2048]{2,1,0:T(8,128)(2,1)} %copy-done.19, ...), custom_call_target="tpu_custom_call" | custom-call | flops 2113929216 | bytes 16777216 | tf_op jit(solution)/shard_map/pallas_call | solution.py:249
  (118 shorter events, 17.6 us)
Async XLA Ops:
  1.5 1.3 collective-permute-start
  3.8 5.6 %collective-permute-start.3 = (bf16[2,4,6144]{2,1,0:T(4,128)(2,1)S(1)}, bf16[2,4,6144]{2,1,0:T(4,128)(2,1)S(1)}, u32[]{:S(2)}, u32[]{:S(2)}) collective-permute-start(bf16[2,4,6144]{2,1,0:T(4,128)(2,1)S(1)} %pad_maximum_fusion.1), channel_id=1, source_target_pairs={{0,34},{1,35},{2,32},{3,33},{4,38},{5,39},{6,36},{7,37},{8,42},{9,... | collective-permute-start | bytes 294920 | tf_op jit(solution)/shard_map/ppermute | solution.py:46
  6.5 4.6 %collective-permute-start.2 = (bf16[2,4,6144]{2,1,0:T(4,128)(2,1)S(1)}, bf16[2,4,6144]{2,1,0:T(4,128)(2,1)S(1)}, u32[]{:S(2)}, u32[]{:S(2)}) collective-permute-start(bf16[2,4,6144]{2,1,0:T(4,128)(2,1)S(1)} %pad_maximum_fusion.1), channel_id=1, source_target_pairs={{0,32},{1,33},{2,34},{3,35},{4,36},{5,37},{6,38},{7,39},{8,40},{9,... | collective-permute-start | bytes 294920 | tf_op jit(solution)/shard_map/ppermute | solution.py:46
  6.9 4.6 %collective-permute-start.1 = (bf16[2,4,6144]{2,1,0:T(4,128)(2,1)S(1)}, bf16[2,4,6144]{2,1,0:T(4,128)(2,1)S(1)}, u32[]{:S(2)}, u32[]{:S(2)}) collective-permute-start(bf16[2,4,6144]{2,1,0:T(4,128)(2,1)S(1)} %pad_maximum_fusion.1), channel_id=1, source_target_pairs={{0,2},{1,3},{2,0},{3,1},{4,6},{5,7},{6,4},{7,5},{8,10},{9,11},{10,... | collective-permute-start | bytes 294920 | tf_op jit(solution)/shard_map/ppermute | solution.py:46
  12.0 7.9 %collective-permute-start.4 = (bf16[2,16,6144]{2,1,0:T(8,128)(2,1)S(1)}, bf16[2,16,6144]{2,1,0:T(8,128)(2,1)S(1)}, u32[]{:S(2)}, u32[]{:S(2)}) collective-permute-start(bf16[2,16,6144]{2,1,0:T(8,128)(2,1)S(1)} %concatenate.18), channel_id=1, source_target_pairs={{0,8},{1,9},{2,10},{3,11},{4,12},{5,13},{6,14},{7,15},{8,0},{9,1},... | collective-permute-start | bytes 1179656 | tf_op jit(solution)/shard_map/ppermute | solution.py:46
  20.5 43.9 %copy-start = (bf16[2,32,2048]{2,1,0:T(8,128)(2,1)}, bf16[2,32,2048]{2,1,0:T(8,128)(2,1)S(1)}, u32[]{:S(2)}) copy-start(bf16[2,32,2048]{2,1,0:T(8,128)(2,1)S(1)} %get-tuple-element.32.refs_16_) | copy-start | bytes 786436
  20.6 43.9 %copy-start.1 = (bf16[2,32,2048]{2,1,0:T(8,128)(2,1)}, bf16[2,32,2048]{2,1,0:T(8,128)(2,1)S(1)}, u32[]{:S(2)}) copy-start(bf16[2,32,2048]{2,1,0:T(8,128)(2,1)S(1)} %get-tuple-element.33.refs_8_) | copy-start | bytes 786436
  20.6 43.9 %copy-start.2 = (bf16[2,32,2048]{2,1,0:T(8,128)(2,1)}, bf16[2,32,2048]{2,1,0:T(8,128)(2,1)S(1)}, u32[]{:S(2)}) copy-start(bf16[2,32,2048]{2,1,0:T(8,128)(2,1)S(1)} %get-tuple-element.34.refs_0_) | copy-start | bytes 786436
  20.6 9.5 %collective-permute-start.22 = (bf16[2,32,2048]{2,1,0:T(8,128)(2,1)S(1)}, bf16[2,32,2048]{2,1,0:T(8,128)(2,1)S(1)}, u32[]{:S(2)}, u32[]{:S(2)}) collective-permute-start(bf16[2,32,2048]{2,1,0:T(8,128)(2,1)S(1)} %get-tuple-element.32.refs_16_), channel_id=1, source_target_pairs={{0,24},{1,25},{2,26},{3,27},{4,28},{5,29},{6,30},{7,31},{8,16},{9,... | collective-permute-start | bytes 786440 | tf_op jit(solution)/shard_map/ppermute | solution.py:46
  24.7 7.6 %collective-permute-start.20 = (bf16[2,32,2048]{2,1,0:T(8,128)(2,1)S(1)}, bf16[2,32,2048]{2,1,0:T(8,128)(2,1)S(1)}, u32[]{:S(2)}, u32[]{:S(2)}) collective-permute-start(bf16[2,32,2048]{2,1,0:T(8,128)(2,1)S(1)} %get-tuple-element.32.refs_16_), channel_id=1, source_target_pairs={{0,33},{1,32},{2,35},{3,34},{4,37},{5,36},{6,39},{7,38},{8,41},{9,... | collective-permute-start | bytes 786440 | tf_op jit(solution)/shard_map/ppermute | solution.py:46
  27.7 7.6 %collective-permute-start.19 = (bf16[2,32,2048]{2,1,0:T(8,128)(2,1)S(1)}, bf16[2,32,2048]{2,1,0:T(8,128)(2,1)S(1)}, u32[]{:S(2)}, u32[]{:S(2)}) collective-permute-start(bf16[2,32,2048]{2,1,0:T(8,128)(2,1)S(1)} %get-tuple-element.32.refs_16_), channel_id=1, source_target_pairs={{0,6},{1,7},{2,4},{3,5},{4,2},{5,3},{6,0},{7,1},{8,14},{9,15},{10,... | collective-permute-start | bytes 786440 | tf_op jit(solution)/shard_map/ppermute | solution.py:46
  29.8 7.6 %collective-permute-start.15 = (bf16[2,32,2048]{2,1,0:T(8,128)(2,1)S(1)}, bf16[2,32,2048]{2,1,0:T(8,128)(2,1)S(1)}, u32[]{:S(2)}, u32[]{:S(2)}) collective-permute-start(bf16[2,32,2048]{2,1,0:T(8,128)(2,1)S(1)} %get-tuple-element.33.refs_8_), channel_id=1, source_target_pairs={{0,24},{1,25},{2,26},{3,27},{4,28},{5,29},{6,30},{7,31},{8,16},{9,... | collective-permute-start | bytes 786440 | tf_op jit(solution)/shard_map/ppermute | solution.py:46
  29.9 9.6 %collective-permute-start.13 = (bf16[2,32,2048]{2,1,0:T(8,128)(2,1)S(1)}, bf16[2,32,2048]{2,1,0:T(8,128)(2,1)S(1)}, u32[]{:S(2)}, u32[]{:S(2)}) collective-permute-start(bf16[2,32,2048]{2,1,0:T(8,128)(2,1)S(1)} %get-tuple-element.33.refs_8_), channel_id=1, source_target_pairs={{0,33},{1,32},{2,35},{3,34},{4,37},{5,36},{6,39},{7,38},{8,41},{9,... | collective-permute-start | bytes 786440 | tf_op jit(solution)/shard_map/ppermute | solution.py:46
  30.1 34.4 %copy-start.4 = (bf16[2,32,2048]{2,1,0:T(8,128)(2,1)}, bf16[2,32,2048]{2,1,0:T(8,128)(2,1)S(1)}, u32[]{:S(2)}) copy-start(bf16[2,32,2048]{2,1,0:T(8,128)(2,1)S(1)} %collective-permute-done.22.refs_20_) | copy-start | bytes 786436
  30.1 10.5 %collective-permute-start.12 = (bf16[2,32,2048]{2,1,0:T(8,128)(2,1)S(1)}, bf16[2,32,2048]{2,1,0:T(8,128)(2,1)S(1)}, u32[]{:S(2)}, u32[]{:S(2)}) collective-permute-start(bf16[2,32,2048]{2,1,0:T(8,128)(2,1)S(1)} %get-tuple-element.33.refs_8_), channel_id=1, source_target_pairs={{0,6},{1,7},{2,4},{3,5},{4,2},{5,3},{6,0},{7,1},{8,14},{9,15},{10,... | collective-permute-start | bytes 786440 | tf_op jit(solution)/shard_map/ppermute | solution.py:46
  32.3 32.2 %copy-start.5 = (bf16[2,32,2048]{2,1,0:T(8,128)(2,1)}, bf16[2,32,2048]{2,1,0:T(8,128)(2,1)S(1)}, u32[]{:S(2)}) copy-start(bf16[2,32,2048]{2,1,0:T(8,128)(2,1)S(1)} %collective-permute-done.20.refs_18_) | copy-start | bytes 786436
  32.3 9.5 %collective-permute-start.8 = (bf16[2,32,2048]{2,1,0:T(8,128)(2,1)S(1)}, bf16[2,32,2048]{2,1,0:T(8,128)(2,1)S(1)}, u32[]{:S(2)}, u32[]{:S(2)}) collective-permute-start(bf16[2,32,2048]{2,1,0:T(8,128)(2,1)S(1)} %get-tuple-element.34.refs_0_), channel_id=1, source_target_pairs={{0,24},{1,25},{2,26},{3,27},{4,28},{5,29},{6,30},{7,31},{8,16},{9,... | collective-permute-start | bytes 786440 | tf_op jit(solution)/shard_map/ppermute | solution.py:46
  35.3 29.2 %copy-start.6 = (bf16[2,32,2048]{2,1,0:T(8,128)(2,1)}, bf16[2,32,2048]{2,1,0:T(8,128)(2,1)S(1)}, u32[]{:S(2)}) copy-start(bf16[2,32,2048]{2,1,0:T(8,128)(2,1)S(1)} %collective-permute-done.19.refs_17_) | copy-start | bytes 786436
  35.3 8.6 %collective-permute-start.6 = (bf16[2,32,2048]{2,1,0:T(8,128)(2,1)S(1)}, bf16[2,32,2048]{2,1,0:T(8,128)(2,1)S(1)}, u32[]{:S(2)}, u32[]{:S(2)}) collective-permute-start(bf16[2,32,2048]{2,1,0:T(8,128)(2,1)S(1)} %get-tuple-element.34.refs_0_), channel_id=1, source_target_pairs={{0,33},{1,32},{2,35},{3,34},{4,37},{5,36},{6,39},{7,38},{8,41},{9,... | collective-permute-start | bytes 786440 | tf_op jit(solution)/shard_map/ppermute | solution.py:46
  37.4 27.1 %copy-start.7 = (bf16[2,32,2048]{2,1,0:T(8,128)(2,1)}, bf16[2,32,2048]{2,1,0:T(8,128)(2,1)S(1)}, u32[]{:S(2)}) copy-start(bf16[2,32,2048]{2,1,0:T(8,128)(2,1)S(1)} %collective-permute-done.15.refs_12_) | copy-start | bytes 786436
  37.4 8.6 %collective-permute-start.5 = (bf16[2,32,2048]{2,1,0:T(8,128)(2,1)S(1)}, bf16[2,32,2048]{2,1,0:T(8,128)(2,1)S(1)}, u32[]{:S(2)}, u32[]{:S(2)}) collective-permute-start(bf16[2,32,2048]{2,1,0:T(8,128)(2,1)S(1)} %get-tuple-element.34.refs_0_), channel_id=1, source_target_pairs={{0,6},{1,7},{2,4},{3,5},{4,2},{5,3},{6,0},{7,1},{8,14},{9,15},{10,... | collective-permute-start | bytes 786440 | tf_op jit(solution)/shard_map/ppermute | solution.py:46
  39.5 7.6 %collective-permute-start.24 = (bf16[2,32,2048]{2,1,0:T(8,128)(2,1)S(1)}, bf16[2,32,2048]{2,1,0:T(8,128)(2,1)S(1)}, u32[]{:S(2)}, u32[]{:S(2)}) collective-permute-start(bf16[2,32,2048]{2,1,0:T(8,128)(2,1)S(1)} %collective-permute-done.22.refs_20_), channel_id=1, source_target_pairs={{0,33},{1,32},{2,35},{3,34},{4,37},{5,36},{6,39},{7,38},{8,41},{9,... | collective-permute-start | bytes 786440 | tf_op jit(solution)/shard_map/ppermute | solution.py:46
  40.6 7.6 %collective-permute-start.23 = (bf16[2,32,2048]{2,1,0:T(8,128)(2,1)S(1)}, bf16[2,32,2048]{2,1,0:T(8,128)(2,1)S(1)}, u32[]{:S(2)}, u32[]{:S(2)}) collective-permute-start(bf16[2,32,2048]{2,1,0:T(8,128)(2,1)S(1)} %collective-permute-done.22.refs_20_), channel_id=1, source_target_pairs={{0,6},{1,7},{2,4},{3,5},{4,2},{5,3},{6,0},{7,1},{8,14},{9,15},{10,... | collective-permute-start | bytes 786440 | tf_op jit(solution)/shard_map/ppermute | solution.py:46
  41.8 8.6 %collective-permute-start.21 = (bf16[2,32,2048]{2,1,0:T(8,128)(2,1)S(1)}, bf16[2,32,2048]{2,1,0:T(8,128)(2,1)S(1)}, u32[]{:S(2)}, u32[]{:S(2)}) collective-permute-start(bf16[2,32,2048]{2,1,0:T(8,128)(2,1)S(1)} %collective-permute-done.19.refs_17_), channel_id=1, source_target_pairs={{0,33},{1,32},{2,35},{3,34},{4,37},{5,36},{6,39},{7,38},{8,41},{9,... | collective-permute-start | bytes 786440 | tf_op jit(solution)/shard_map/ppermute | solution.py:46
  43.9 7.6 %collective-permute-start.16 = (bf16[2,32,2048]{2,1,0:T(8,128)(2,1)S(1)}, bf16[2,32,2048]{2,1,0:T(8,128)(2,1)S(1)}, u32[]{:S(2)}, u32[]{:S(2)}) collective-permute-start(bf16[2,32,2048]{2,1,0:T(8,128)(2,1)S(1)} %collective-permute-done.15.refs_12_), channel_id=1, source_target_pairs={{0,6},{1,7},{2,4},{3,5},{4,2},{5,3},{6,0},{7,1},{8,14},{9,15},{10,... | collective-permute-start | bytes 786440 | tf_op jit(solution)/shard_map/ppermute | solution.py:46
  46.0 7.6 %collective-permute-start.17 = (bf16[2,32,2048]{2,1,0:T(8,128)(2,1)S(1)}, bf16[2,32,2048]{2,1,0:T(8,128)(2,1)S(1)}, u32[]{:S(2)}, u32[]{:S(2)}) collective-permute-start(bf16[2,32,2048]{2,1,0:T(8,128)(2,1)S(1)} %collective-permute-done.13.refs_10_), channel_id=1, source_target_pairs={{0,24},{1,25},{2,26},{3,27},{4,28},{5,29},{6,30},{7,31},{8,16},{9,... | collective-permute-start | bytes 786440 | tf_op jit(solution)/shard_map/ppermute | solution.py:46
  47.1 7.6 %collective-permute-start.14 = (bf16[2,32,2048]{2,1,0:T(8,128)(2,1)S(1)}, bf16[2,32,2048]{2,1,0:T(8,128)(2,1)S(1)}, u32[]{:S(2)}, u32[]{:S(2)}) collective-permute-start(bf16[2,32,2048]{2,1,0:T(8,128)(2,1)S(1)} %collective-permute-done.13.refs_10_), channel_id=1, source_target_pairs={{0,6},{1,7},{2,4},{3,5},{4,2},{5,3},{6,0},{7,1},{8,14},{9,15},{10,... | collective-permute-start | bytes 786440 | tf_op jit(solution)/shard_map/ppermute | solution.py:46
  48.3 8.6 %collective-permute-start.7 = (bf16[2,32,2048]{2,1,0:T(8,128)(2,1)S(1)}, bf16[2,32,2048]{2,1,0:T(8,128)(2,1)S(1)}, u32[]{:S(2)}, u32[]{:S(2)}) collective-permute-start(bf16[2,32,2048]{2,1,0:T(8,128)(2,1)S(1)} %collective-permute-done.5.refs_1_), channel_id=1, source_target_pairs={{0,33},{1,32},{2,35},{3,34},{4,37},{5,36},{6,39},{7,38},{8,41},{9,... | collective-permute-start | bytes 786440 | tf_op jit(solution)/shard_map/ppermute | solution.py:46
  50.4 10.4 %collective-permute-start.9 = (bf16[2,32,2048]{2,1,0:T(8,128)(2,1)S(1)}, bf16[2,32,2048]{2,1,0:T(8,128)(2,1)S(1)}, u32[]{:S(2)}, u32[]{:S(2)}) collective-permute-start(bf16[2,32,2048]{2,1,0:T(8,128)(2,1)S(1)} %collective-permute-done.5.refs_1_), channel_id=1, source_target_pairs={{0,24},{1,25},{2,26},{3,27},{4,28},{5,29},{6,30},{7,31},{8,16},{9,... | collective-permute-start | bytes 786440 | tf_op jit(solution)/shard_map/ppermute | solution.py:46
  51.5 9.2 %collective-permute-start.10 = (bf16[2,32,2048]{2,1,0:T(8,128)(2,1)S(1)}, bf16[2,32,2048]{2,1,0:T(8,128)(2,1)S(1)}, u32[]{:S(2)}, u32[]{:S(2)}) collective-permute-start(bf16[2,32,2048]{2,1,0:T(8,128)(2,1)S(1)} %collective-permute-done.6.refs_2_), channel_id=1, source_target_pairs={{0,24},{1,25},{2,26},{3,27},{4,28},{5,29},{6,30},{7,31},{8,16},{9,... | collective-permute-start | bytes 786440 | tf_op jit(solution)/shard_map/ppermute | solution.py:46
  53.6 7.6 %collective-permute-start.25 = (bf16[2,32,2048]{2,1,0:T(8,128)(2,1)S(1)}, bf16[2,32,2048]{2,1,0:T(8,128)(2,1)S(1)}, u32[]{:S(2)}, u32[]{:S(2)}) collective-permute-start(bf16[2,32,2048]{2,1,0:T(8,128)(2,1)S(1)} %collective-permute-done.23.refs_21_), channel_id=1, source_target_pairs={{0,33},{1,32},{2,35},{3,34},{4,37},{5,36},{6,39},{7,38},{8,41},{9,... | collective-permute-start | bytes 786440 | tf_op jit(solution)/shard_map/ppermute | solution.py:46
  54.8 7.6 %collective-permute-start.18 = (bf16[2,32,2048]{2,1,0:T(8,128)(2,1)S(1)}, bf16[2,32,2048]{2,1,0:T(8,128)(2,1)S(1)}, u32[]{:S(2)}, u32[]{:S(2)}) collective-permute-start(bf16[2,32,2048]{2,1,0:T(8,128)(2,1)S(1)} %collective-permute-done.17.refs_14_), channel_id=1, source_target_pairs={{0,6},{1,7},{2,4},{3,5},{4,2},{5,3},{6,0},{7,1},{8,14},{9,15},{10,... | collective-permute-start | bytes 786440 | tf_op jit(solution)/shard_map/ppermute | solution.py:46
  56.9 7.6 %collective-permute-start.11 = (bf16[2,32,2048]{2,1,0:T(8,128)(2,1)S(1)}, bf16[2,32,2048]{2,1,0:T(8,128)(2,1)S(1)}, u32[]{:S(2)}, u32[]{:S(2)}) collective-permute-start(bf16[2,32,2048]{2,1,0:T(8,128)(2,1)S(1)} %collective-permute-done.7.refs_3_), channel_id=1, source_target_pairs={{0,24},{1,25},{2,26},{3,27},{4,28},{5,29},{6,30},{7,31},{8,16},{9,... | collective-permute-start | bytes 786440 | tf_op jit(solution)/shard_map/ppermute | solution.py:46
  77.4 2.4 %collective-permute-start.26 = (f32[3,256,224]{1,2,0:T(8,128)S(1)}, f32[3,256,224]{1,2,0:T(8,128)S(1)}, u32[]{:S(2)}, u32[]{:S(2)}) collective-permute-start(f32[3,256,224]{1,2,0:T(8,128)S(1)} %copy.10), channel_id=1, source_target_pairs={{0,64},{1,65},{2,66},{3,67},{4,68},{5,69},{6,70},{7,71},{8,72},{9,... | collective-permute-start | bytes 2064392 | tf_op jit(solution)/shard_map/ppermute | solution.py:46
  87.6 10.7 %collective-permute-start.27 = (bf16[128,2048]{1,0:T(8,128)(2,1)}, bf16[128,2048]{1,0:T(8,128)(2,1)S(1)}, u32[]{:S(2)}, u32[]{:S(2)}) collective-permute-start(bf16[128,2048]{1,0:T(8,128)(2,1)} %get-tuple-element.17), channel_id=1, source_target_pairs={{0,24},{1,25},{2,26},{3,27},{4,28},{5,29},{6,30},{7,31},{8,16},{9,... | collective-permute-start | bytes 1572872 | tf_op jit(solution)/shard_map/ppermute | solution.py:46
  89.8 11.1 %collective-permute-start.30 = (bf16[128,2048]{1,0:T(8,128)(2,1)}, bf16[128,2048]{1,0:T(8,128)(2,1)S(1)}, u32[]{:S(2)}, u32[]{:S(2)}) collective-permute-start(bf16[128,2048]{1,0:T(8,128)(2,1)} %get-tuple-element.19), channel_id=1, source_target_pairs={{0,6},{1,7},{2,4},{3,5},{4,2},{5,3},{6,0},{7,1},{8,14},{9,15},{10,... | collective-permute-start | bytes 1572872 | tf_op jit(solution)/shard_map/ppermute | solution.py:46
  91.0 13.5 %collective-permute-start.33 = (bf16[128,2048]{1,0:T(8,128)(2,1)}, bf16[128,2048]{1,0:T(8,128)(2,1)S(1)}, u32[]{:S(2)}, u32[]{:S(2)}) collective-permute-start(bf16[128,2048]{1,0:T(8,128)(2,1)} %get-tuple-element.21), channel_id=1, source_target_pairs={{0,33},{1,32},{2,35},{3,34},{4,37},{5,36},{6,39},{7,38},{8,41},{9,... | collective-permute-start | bytes 1572872 | tf_op jit(solution)/shard_map/ppermute | solution.py:46
  99.7 7.7 %collective-permute-start.28 = (bf16[64,2048]{1,0:T(8,128)(2,1)S(1)}, bf16[64,2048]{1,0:T(8,128)(2,1)S(1)}, u32[]{:S(2)}, u32[]{:S(2)}) collective-permute-start(bf16[64,2048]{1,0:T(8,128)(2,1)S(1)} %slice.174), channel_id=1, source_target_pairs={{0,33},{1,32},{2,35},{3,34},{4,37},{5,36},{6,39},{7,38},{8,41},{9,... | collective-permute-start | bytes 786440 | tf_op jit(solution)/shard_map/ppermute | solution.py:46
  102.3 7.7 %collective-permute-start.31 = (bf16[64,2048]{1,0:T(8,128)(2,1)S(1)}, bf16[64,2048]{1,0:T(8,128)(2,1)S(1)}, u32[]{:S(2)}, u32[]{:S(2)}) collective-permute-start(bf16[64,2048]{1,0:T(8,128)(2,1)S(1)} %slice.173), channel_id=1, source_target_pairs={{0,24},{1,25},{2,26},{3,27},{4,28},{5,29},{6,30},{7,31},{8,16},{9,... | collective-permute-start | bytes 786440 | tf_op jit(solution)/shard_map/ppermute | solution.py:46
  104.6 7.7 %collective-permute-start.34 = (bf16[64,2048]{1,0:T(8,128)(2,1)S(1)}, bf16[64,2048]{1,0:T(8,128)(2,1)S(1)}, u32[]{:S(2)}, u32[]{:S(2)}) collective-permute-start(bf16[64,2048]{1,0:T(8,128)(2,1)S(1)} %slice.172), channel_id=1, source_target_pairs={{0,6},{1,7},{2,4},{3,5},{4,2},{5,3},{6,0},{7,1},{8,14},{9,15},{10,... | collective-permute-start | bytes 786440 | tf_op jit(solution)/shard_map/ppermute | solution.py:46
  107.4 7.1 %collective-permute-start.29 = (bf16[32,2048]{1,0:T(8,128)(2,1)S(1)}, bf16[32,2048]{1,0:T(8,128)(2,1)S(1)}, u32[]{:S(2)}, u32[]{:S(2)}) collective-permute-start(bf16[32,2048]{1,0:T(8,128)(2,1)S(1)} %slice.178), channel_id=1, source_target_pairs={{0,6},{1,7},{2,4},{3,5},{4,2},{5,3},{6,0},{7,1},{8,14},{9,15},{10,... | collective-permute-start | bytes 393224 | tf_op jit(solution)/shard_map/ppermute | solution.py:46
  110.0 6.3 %collective-permute-start.32 = (bf16[32,2048]{1,0:T(8,128)(2,1)S(1)}, bf16[32,2048]{1,0:T(8,128)(2,1)S(1)}, u32[]{:S(2)}, u32[]{:S(2)}) collective-permute-start(bf16[32,2048]{1,0:T(8,128)(2,1)S(1)} %slice.177), channel_id=1, source_target_pairs={{0,33},{1,32},{2,35},{3,34},{4,37},{5,36},{6,39},{7,38},{8,41},{9,... | collective-permute-start | bytes 393224 | tf_op jit(solution)/shard_map/ppermute | solution.py:46
  112.4 6.3 %collective-permute-start.35 = (bf16[32,2048]{1,0:T(8,128)(2,1)S(1)}, bf16[32,2048]{1,0:T(8,128)(2,1)S(1)}, u32[]{:S(2)}, u32[]{:S(2)}) collective-permute-start(bf16[32,2048]{1,0:T(8,128)(2,1)S(1)} %slice.176), channel_id=1, source_target_pairs={{0,24},{1,25},{2,26},{3,27},{4,28},{5,29},{6,30},{7,31},{8,16},{9,... | collective-permute-start | bytes 393224 | tf_op jit(solution)/shard_map/ppermute | solution.py:46
  118.7 5.8 %collective-permute-start.36 = (bf16[16,6144]{1,0:T(8,128)(2,1)S(1)}, bf16[16,6144]{1,0:T(8,128)(2,1)S(1)}, u32[]{:S(2)}, u32[]{:S(2)}) collective-permute-start(bf16[16,6144]{1,0:T(8,128)(2,1)S(1)} %slice.175), channel_id=1, source_target_pairs={{0,8},{1,9},{2,10},{3,11},{4,12},{5,13},{6,14},{7,15},{8,0},{9,1},... | collective-permute-start | bytes 589832 | tf_op jit(solution)/shard_map/ppermute | solution.py:46
  124.6 4.2 %collective-permute-start.37 = (bf16[4,6144]{1,0:T(4,128)(2,1)S(1)}, bf16[4,6144]{1,0:T(4,128)(2,1)S(1)}, u32[]{:S(2)}, u32[]{:S(2)}) collective-permute-start(bf16[4,6144]{1,0:T(4,128)(2,1)S(1)} %get-tuple-element.35), channel_id=1, source_target_pairs={{0,2},{1,3},{2,0},{3,1},{4,6},{5,7},{6,4},{7,5},{8,10},{9,11},{10,... | collective-permute-start | bytes 147464 | tf_op jit(solution)/shard_map/ppermute | solution.py:46
  124.7 5.1 %collective-permute-start.39 = (bf16[4,6144]{1,0:T(4,128)(2,1)S(1)}, bf16[4,6144]{1,0:T(4,128)(2,1)S(1)}, u32[]{:S(2)}, u32[]{:S(2)}) collective-permute-start(bf16[4,6144]{1,0:T(4,128)(2,1)S(1)} %get-tuple-element.36), channel_id=1, source_target_pairs={{0,34},{1,35},{2,32},{3,33},{4,38},{5,39},{6,36},{7,37},{8,42},{9,... | collective-permute-start | bytes 147464 | tf_op jit(solution)/shard_map/ppermute | solution.py:46
  125.7 4.6 %collective-permute-start.38 = (bf16[4,6144]{1,0:T(4,128)(2,1)S(1)}, bf16[4,6144]{1,0:T(4,128)(2,1)S(1)}, u32[]{:S(2)}, u32[]{:S(2)}) collective-permute-start(bf16[4,6144]{1,0:T(4,128)(2,1)S(1)} %get-tuple-element.37), channel_id=1, source_target_pairs={{0,32},{1,33},{2,34},{3,35},{4,36},{5,37},{6,38},{7,39},{8,40},{9,... | collective-permute-start | bytes 147464 | tf_op jit(solution)/shard_map/ppermute | solution.py:46
  130.4 7.0 %collective-permute-start.40 = (bf16[2,6144]{1,0:T(2,128)(2,1)S(1)}, bf16[2,6144]{1,0:T(2,128)(2,1)S(1)}, u32[]{:S(2)}, u32[]{:S(2)}) collective-permute-start(bf16[2,6144]{1,0:T(2,128)(2,1)S(1)} %broadcast_select_fusion.6), channel_id=1, source_target_pairs={{0,64},{1,65},{2,66},{3,67},{4,68},{5,69},{6,70},{7,71},{8,72},{9,... | collective-permute-start | bytes 73736 | tf_op jit(solution)/shard_map/ppermute | solution.py:46
  (18 other events, 231.5 us)

commit v2 on v0

v2 whole, which is shorter than its diff:
```python
import functools

import jax
import jax.numpy as jnp
import numpy as np
from jax import lax
from jax.experimental import pallas as pl
from jax.experimental.pallas import tpu as pltpu
from jax.sharding import PartitionSpec as P

AXES = ("rep", "tp", "att")
CHUNKS = (("x", "y", "z"), ("y", "z", "x"), ("z", "x", "y"))
CUBE = ("x", "y", "xy", "z", "xz", "yz", "xyz")
GROUP = 32
LANES = 256


def linear(core, x, y, z):
    return core * 64 + ((y % 2) * 16 + z * 4 + x) * 2 + y // 2


def pairs(moves, flip=0):
    result = []
    for core in range(2):
        dx, dy, dz = moves[core]
        for x in range(4):
            for y in range(4):
                for z in range(4):
                    result.append(
                        (linear(core, x, y, z), linear(core ^ flip, x ^ dx, y ^ dy, z ^ dz))
                    )
    return sorted(result)


def neighbour(axes, stage):
    moves = []
    for core in range(2):
        moves.append(
            tuple(
                (1 if core == stage else 3) if name in axes else 0
                for name in "xyz"
            )
        )
    return pairs(moves)


OTHER_CORE = pairs([(0, 0, 0)] * 2, flip=1)


def send(value, route):
    return lax.ppermute(value, AXES, route)


def label_order(axes):
    bit = {"x": 1, "y": 2, "z": 4}
    return [
        sum(bit[axis] for place, axis in enumerate(axes) if index >> place & 1)
        for index in range(8)
    ]


def call(kernel, operands, outs, scratch=(), limit=16, flops=0, megabytes=0):
    places = [place for place, _ in operands]
    values = [
        pltpu.with_memory_space_constraint(value, pltpu.VMEM if place == "vmem" else pltpu.HBM)
        for place, value in operands
    ]
    spec = {
        "vmem": pl.BlockSpec(memory_space=pltpu.VMEM),
        "hbm": pl.BlockSpec(memory_space=pltpu.HBM),
    }
    return pl.pallas_call(
        kernel,
        out_shape=[
            pltpu.VMEM(shape, dtype) if place == "vmem" else jax.ShapeDtypeStruct(shape, dtype)
            for place, shape, dtype in outs
        ],
        in_specs=[spec[place] for place in places],
        out_specs=[spec[place] for place, _, _ in outs],
        scratch_shapes=list(scratch),
        compiler_params=pltpu.CompilerParams(vmem_limit_bytes=limit * 2**20),
        cost_estimate=pl.CostEstimate(
            flops=flops, bytes_accessed=megabytes * 2**20, transcendentals=0
        ),
    )(*values)


def join_kernel(first, second, out):
    rows = first.shape[1]
    out[:, :rows] = first[...]
    out[:, rows:] = second[...]


def join(first, second):
    shape = (first.shape[0], 2 * first.shape[1], first.shape[2])
    return call(
        join_kernel,
        [("vmem", first), ("vmem", second)],
        [("vmem", shape, first.dtype)],
        megabytes=2,
    )[0]


def add_products(third, k, first, piece, weights, acc):
    columns = slice(k * third, (k + 1) * third)
    order = label_order(CHUNKS[k])[first : first + 4]
    for i, source in enumerate((0, 0, 1)):
        product = lax.dot_general(
            piece[source],
            weights[i][:, columns],
            (((1,), (1,)), ((), ())),
            preferred_element_type=jnp.float32,
        )
        local_ff = product.shape[1]
        for place, label in enumerate(order):
            rows = slice(GROUP * label, GROUP * label + GROUP)
            acc[rows, i * LANES : i * LANES + local_ff] += product[
                GROUP * place : GROUP * place + GROUP
            ]


def load_kernel(third, *refs):
    hbm, weights, sems = refs[:3], refs[3:6], refs[6]
    start = lax.axis_index("rep") * (3 * third)
    copies = []
    for i in range(3):
        copy = pltpu.make_async_copy(
            hbm[i].at[:, pl.ds(pl.multiple_of(start, third), 3 * third)], weights[i], sems.at[i]
        )
        copy.start()
        copies.append(copy)
    for copy in copies:
        copy.wait()


def early_kernel(third, *refs):
    pieces, weights, acc = refs[:3], refs[3:6], refs[6]
    acc[...] = jnp.zeros_like(acc)
    for k in range(3):
        add_products(third, k, 0, pieces[k], weights, acc)


def late_kernel(third, k, *refs):
    piece, weights, acc, out = refs[0], refs[1:4], refs[4], refs[5]
    out[...] = acc[...]
    add_products(third, k, 4, piece, weights, out)


def permuted(one_hot, value):
    high = value.astype(jnp.bfloat16)
    rest = value - high.astype(jnp.float32)
    middle = rest.astype(jnp.bfloat16)
    low = (rest - middle.astype(jnp.float32)).astype(jnp.bfloat16)
    return (
        jnp.dot(one_hot, high, preferred_element_type=jnp.float32)
        + jnp.dot(one_hot, middle, preferred_element_type=jnp.float32)
        + jnp.dot(one_hot, low, preferred_element_type=jnp.float32)
    )


def input_products(third, first, gate_part, up_part, gate, up, targets):
    for k in range(3):
        columns = slice(k * third, (k + 1) * third)
        picks = [
            slice(GROUP * label, GROUP * label + GROUP)
            for label in label_order(CHUNKS[k])[first : first + 4]
        ]
        left = jnp.concatenate([gate_part[pick] for pick in picks], axis=0)
        right = jnp.concatenate([up_part[pick] for pick in picks], axis=0)
        targets[k][...] = (
            jnp.dot(left, gate[:, columns], preferred_element_type=jnp.float32)
            + jnp.dot(right, up[:, columns], preferred_element_type=jnp.float32)
        ).astype(targets[k].dtype)


def middle_kernel(third, *refs):
    part, other, one_hot, gate, up = refs[:5]
    sends, (gate_out, up_out, hidden_out) = refs[5:8], refs[8:11]
    local_ff = gate.shape[0]
    matrix = one_hot[...]
    total = [
        part[:, i * LANES : (i + 1) * LANES]
        + permuted(matrix, other[:, i * LANES : (i + 1) * LANES])
        for i in range(3)
    ]
    pre_gate, pre_up, hidden_grad = (value[:, :local_ff] for value in total)
    sig = jax.nn.sigmoid(pre_gate)
    act = pre_gate * sig
    hidden_out[...] = (act * pre_up).astype(jnp.bfloat16)
    gate_out[...] = (hidden_grad * pre_up * sig * (1.0 + pre_gate * (1.0 - sig))).astype(
        jnp.bfloat16
    )
    up_out[...] = (hidden_grad * act).astype(jnp.bfloat16)
    input_products(third, 4, gate_out, up_out, gate, up, sends)


def rest_kernel(third, *refs):
    pieces, (gate, up, gate_part, up_part, hidden) = refs[:6], refs[6:11]
    keeps, outs, (results, sems) = refs[11:14], refs[14:17], refs[17:]
    input_products(third, 0, gate_part, up_part, gate, up, keeps)
    copies = []
    for k in range(3):
        order = label_order(CHUNKS[k])
        for i, (left, source) in enumerate(((gate_part, 0), (up_part, 0), (hidden, 1))):
            groups = [
                piece[source, i * GROUP : (i + 1) * GROUP]
                for piece in pieces[2 * k : 2 * k + 2]
                for i in range(4)
            ]
            rows = jnp.concatenate([groups[order.index(label)] for label in range(8)], axis=0)
            results[i, :, k * third : (k + 1) * third] = lax.dot_general(
                left[...], rows, (((0,), (0,)), ((), ())), preferred_element_type=jnp.float32
            ).astype(jnp.bfloat16)
            copy = pltpu.make_async_copy(
                results.at[i, :, pl.ds(k * third, third)],
                outs[i].at[:, pl.ds(k * third, third)],
                sems.at[3 * k + i],
            )
            copy.start()
            copies.append(copy)
    for copy in copies:
        copy.wait()


def cross_core_rows():
    matrix = np.zeros((8 * GROUP, 8 * GROUP), np.float32)
    for high in range(8):
        for low in range(8):
            for row in range(4):
                matrix[(high * 8 + low) * 4 + row, (low * 8 + high) * 4 + row] = 1.0
    return jnp.asarray(matrix, jnp.bfloat16)


def shards(inputs, cotangent, gate_weight, up_weight, down_weight):
    core = lax.axis_index("rep")
    width = inputs.shape[2]
    half, third = width // 2, width // 6
    micro = inputs.shape[0]

    rows = jnp.stack([inputs[:, 0], cotangent[:, 0]])
    low, high = rows[:, :, :half], rows[:, :, half:]
    mine = jnp.where(core == 0, low, high)
    theirs = send(jnp.where(core == 0, high, low), OTHER_CORE)
    block = jnp.concatenate(
        [jnp.where(core == 0, mine, theirs), jnp.where(core == 0, theirs, mine)], axis=1
    )
    block = jnp.concatenate(
        [block] + [send(block, neighbour(axes, 0)) for axes in CUBE], axis=1
    )
    local_ff = gate_weight.shape[0]
    rows = 8 * GROUP
    vmem, hbm = (lambda value: ("vmem", value)), (lambda value: ("hbm", value))
    fourth = [
        send(block[:, :, k * third : (k + 1) * third], neighbour(CHUNKS[k][0], 1))
        for k in range(3)
    ]
    weights = call(
        functools.partial(load_kernel, third),
        [hbm(gate_weight), hbm(up_weight), hbm(down_weight)],
        [("vmem", (local_ff, half), jnp.bfloat16)] * 3,
        [pltpu.SemaphoreType.DMA((3,))],
        megabytes=16,
    )
    fourth, weights = lax.optimization_barrier((fourth, weights))
    held, last = [], []
    for k in range(3):
        own = block[:, :, k * third : (k + 1) * third]
        for stage, axis in enumerate(CHUNKS[k]):
            new = fourth[k] if stage == 0 else send(own, neighbour(axis, 1))
            if stage < 2:
                own = join(own, new)
        held.append(own)
        last.append(new)
    (part,) = call(
        functools.partial(early_kernel, third),
        [vmem(value) for value in (*held, *weights)],
        [("vmem", (rows, 3 * LANES), jnp.float32)],
        flops=3 * rows * local_ff * half,
        megabytes=14,
    )
    for k in range(3):
        (part,) = call(
            functools.partial(late_kernel, third, k),
            [vmem(value) for value in (last[k], *weights, part)],
            [("vmem", (rows, 3 * LANES), jnp.float32)],
            flops=rows * local_ff * half,
            megabytes=5,
        )
    other = send(part, OTHER_CORE)
    small = ("vmem", (rows, local_ff), jnp.bfloat16)
    results = call(
        functools.partial(middle_kernel, third),
        [vmem(value) for value in (part, other, cross_core_rows(), weights[0], weights[1])],
        [("vmem", (rows // 2, third), jnp.bfloat16)] * 3 + [small] * 3,
        flops=2 * rows * local_ff * half,
        megabytes=8,
    )
    outgoing, parts = results[:3], results[3:]
    received = [send(out, neighbour(CHUNKS[k][2], 1)) for k, out in enumerate(outgoing)]
    results = call(
        functools.partial(rest_kernel, third),
        [vmem(piece) for k in range(3) for piece in (held[k], last[k])]
        + [vmem(value) for value in (weights[0], weights[1], *parts)],
        [("vmem", (rows // 2, third), jnp.float32)] * 3
        + [("hbm", (local_ff, half), jnp.bfloat16)] * 3,
        [pltpu.VMEM((3, local_ff, half), jnp.bfloat16), pltpu.SemaphoreType.DMA((9,))],
        limit=24,
        flops=8 * rows * local_ff * half,
        megabytes=24,
    )
    sums, (gate_grad, up_grad, down_grad) = results[:3], results[3:]

    for stage in (2, 1, 0):
        sums = [value + new.astype(jnp.float32) for value, new in zip(sums, received)]
        if stage:
            cut = sums[0].shape[0] // 2
            received = [
                send(value[cut:].astype(jnp.bfloat16), neighbour(CHUNKS[k][stage - 1], 1))
                for k, value in enumerate(sums)
            ]
            sums = [value[:cut] for value in sums]
    value = jnp.concatenate(sums, axis=1)
    cut = value.shape[0] // 8
    value = value[:cut] + sum(
        send(value[i * cut : (i + 1) * cut].astype(jnp.bfloat16), neighbour(axes, 0)).astype(
            jnp.float32
        )
        for i, axes in enumerate(CUBE, 1)
    )
    value = value.astype(jnp.bfloat16)
    mine = jnp.where(core == 0, value[:micro], value[micro:])
    theirs = send(jnp.where(core == 0, value[micro:], value[:micro]), OTHER_CORE)
    input_grad = jnp.concatenate(
        [jnp.where(core == 0, mine, theirs), jnp.where(core == 0, theirs, mine)], axis=1
    )[:, None, :]
    return input_grad, gate_grad, up_grad, down_grad


def solution(mesh):
    return jax.shard_map(
        shards,
        mesh=mesh,
        in_specs=(
            P(None, ("rep", "tp", "att"), None),
            P(None, ("rep", "tp", "att"), None),
            P(("tp", "att"), None),
            P(("tp", "att"), None),
            P(("tp", "att"), None),
        ),
        out_specs=(
            P(None, ("rep", "tp", "att"), None),
            P(("tp", "att"), "rep"),
            P(("tp", "att"), "rep"),
            P(("tp", "att"), "rep"),
        ),
        check_vma=False,
    )
```

time: 1190 us -> 112 us (0.09)
  waiting for transfers between devices: 654 us -> 36.6 us
  blocking collectives: 413 us -> 0 us
  matrix products: 69.3 us -> 0 us
  starting transfers between devices: 0.69 us -> 52.3 us
  local copies, waits for them, and re-layouts: 26.3 us -> 1.14 us
  Pallas kernels: 0 us -> 16.3 us
  between operations: 14 us -> 0.99 us
  other arithmetic: 15.6 us -> 3.41 us
    all_gather x2 -> x0, waiting for transfers between devices: 654 us -> none  [shards(): piece = lax.all_gather(stacked, ('tp', 'att'), axis=1, tiled=True)]
    unnamed x1 -> x0, blocking collectives: 413 us -> none
    dot_general x16 -> x0, matrix products: 69.3 us -> none  [the longest x6 29.7 us: contract_last(): lax.dot_general(left, right, (((1,), (1,)), ((), ())), preferred_element_...]
    ppermute x0 -> x35, starting transfers between devices: none -> 52.3 us  [send(): return lax.ppermute(value, AXES, route)]
    ppermute x0 -> x35, waiting for transfers between devices: none -> 36.6 us  [send(): return lax.ppermute(value, AXES, route)]
    slice x3 -> x8, local copies, waits for them, and re-layouts: 18.4 us -> 0.32 us  [the longest x6 0.14 us: shards(): value[cut:].astype(jnp.bfloat16)]
    pallas_call x0 -> x13, Pallas kernels: none -> 16.3 us  [call(): pl.pallas_call(kernel, out_shape=[pltpu.VMEM(shape, dtype) if place == 'v...]
    convert_element_type x3 -> x1, other arithmetic: 13.4 us -> 0.1 us  [shards(): value = value.astype(jnp.bfloat16)]
  transfers between devices with their start and end apart: 5 -> 35, of which waited for: 2 -> 21; matrix products, arithmetic and copies ran while one was open for 6% -> 1% of each run, Pallas kernels for 0% -> 12%
where the time goes in v2:
time: 112 us; the launch traced here: 111 us
  starting transfers between devices  52.3 us (47%)
  waiting for transfers between devices  36.6 us (33%)
  Pallas kernels  16.3 us (15%)
  other arithmetic  3.41 us (3%)
  local copies, waits for them, and re-layouts  1.14 us (1%)
    ppermute x35, starting transfers between devices, send(): return lax.ppermute(value, AXES, route)  52.3 us
    ppermute x35, waiting for transfers between devices, send(): return lax.ppermute(value, AXES, route)  36.6 us
    pallas_call x13, Pallas kernels, call(): pl.pallas_call(kernel, out_shape=[pltpu.VMEM(shape, dtype) if place == 'v...  16.3 us
  transfers between devices with their start and end apart: 35, of which 21 were waited for; matrix products, arithmetic and copies ran while one was open for 1% of the time, Pallas kernels for 12%

profile of v2, /device:TPU:0, one launch (start us, length us, event | category | flops | bytes accessed | tf_op | source)
XLA Modules:
  0.0 110.7 jit_solution(11239270569674185698)
XLA Ops:
  0.6 0.9 broadcast_select_fusion.2
  1.6 1.2 %collective-permute-done = bf16[2,2,6144]{2,1,0:T(2,128)(2,1)S(1)} collective-permute-done((bf16[2,2,6144]{2,1,0:T(2,128)(2,1)S(1)}, bf16[2,2,6144]{2,1,0:T(2,128)(2,1)S(1)}, u32[]{:S(2)}, u32[]{:S(2)}) %collective-permute-start) | collective-permute-done | bytes 49184 | tf_op jit(solution)/shard_map/ppermute | solution.py:51
  2.8 0.9 broadcast_select_fusion
  3.8 4.0 %collective-permute-start.7 = (bf16[2,4,6144]{2,1,0:T(4,128)(2,1)S(1)}, bf16[2,4,6144]{2,1,0:T(4,128)(2,1)S(1)}, u32[]{:S(2)}, u32[]{:S(2)}) collective-permute-start(bf16[2,4,6144]{2,1,0:T(4,128)(2,1)S(1)} %pad_maximum_fusion.1), channel_id=1, source_target_pairs={{0,42},{1,43},{2,40},{3,41},{4,46},{5,47},{6,44},{7,45},{8,34},{9,... | collective-permute-start | bytes 294920 | tf_op jit(solution)/shard_map/ppermute | solution.py:51
  7.9 1.9 %collective-permute-start.5 = (bf16[2,4,6144]{2,1,0:T(4,128)(2,1)S(1)}, bf16[2,4,6144]{2,1,0:T(4,128)(2,1)S(1)}, u32[]{:S(2)}, u32[]{:S(2)}) collective-permute-start(bf16[2,4,6144]{2,1,0:T(4,128)(2,1)S(1)} %pad_maximum_fusion.1), channel_id=1, source_target_pairs={{0,10},{1,11},{2,8},{3,9},{4,14},{5,15},{6,12},{7,13},{8,2},{9,3},... | collective-permute-start | bytes 294920 | tf_op jit(solution)/shard_map/ppermute | solution.py:51
  10.0 2.4 %collective-permute-start.3 = (bf16[2,4,6144]{2,1,0:T(4,128)(2,1)S(1)}, bf16[2,4,6144]{2,1,0:T(4,128)(2,1)S(1)}, u32[]{:S(2)}, u32[]{:S(2)}) collective-permute-start(bf16[2,4,6144]{2,1,0:T(4,128)(2,1)S(1)} %pad_maximum_fusion.1), channel_id=1, source_target_pairs={{0,34},{1,35},{2,32},{3,33},{4,38},{5,39},{6,36},{7,37},{8,42},{9,... | collective-permute-start | bytes 294920 | tf_op jit(solution)/shard_map/ppermute | solution.py:51
  12.8 1.7 %collective-permute-done.6 = bf16[2,4,6144]{2,1,0:T(4,128)(2,1)S(1)} collective-permute-done((bf16[2,4,6144]{2,1,0:T(4,128)(2,1)S(1)}, bf16[2,4,6144]{2,1,0:T(4,128)(2,1)S(1)}, u32[]{:S(2)}, u32[]{:S(2)}) %collective-permute-start.6) | collective-permute-done | bytes 98336 | tf_op jit(solution)/shard_map/ppermute | solution.py:51
  14.8 0.6 collective-permute-done.4
  15.9 1.1 collective-permute-done.2
  17.0 2.1 %collective-permute-done.1 = bf16[2,4,6144]{2,1,0:T(4,128)(2,1)S(1)} collective-permute-done((bf16[2,4,6144]{2,1,0:T(4,128)(2,1)S(1)}, bf16[2,4,6144]{2,1,0:T(4,128)(2,1)S(1)}, u32[]{:S(2)}, u32[]{:S(2)}) %collective-permute-start.1) | collective-permute-done | bytes 98336 | tf_op jit(solution)/shard_map/ppermute | solution.py:51
  19.1 0.8 concatenate.14
  20.0 2.4 %collective-permute-start.10 = (bf16[2,32,2048]{2,1,0:T(8,128)(2,1)S(1)}, bf16[2,32,2048]{2,1,0:T(8,128)(2,1)S(1)}, u32[]{:S(2)}, u32[]{:S(2)}) collective-permute-start(bf16[2,32,2048]{2,1,0:T(8,128)(2,1)S(1)} %get-tuple-element.48.first), channel_id=1, source_target_pairs={{0,24},{1,25},{2,26},{3,27},{4,28},{5,29},{6,30},{7,31},{8,16},{9,... | collective-permute-start | bytes 786440 | tf_op jit(solution)/shard_map/ppermute | solution.py:51
  22.4 3.0 %collective-permute-start.9 = (bf16[2,32,2048]{2,1,0:T(8,128)(2,1)S(1)}, bf16[2,32,2048]{2,1,0:T(8,128)(2,1)S(1)}, u32[]{:S(2)}, u32[]{:S(2)}) collective-permute-start(bf16[2,32,2048]{2,1,0:T(8,128)(2,1)S(1)} %get-tuple-element.49.first), channel_id=1, source_target_pairs={{0,33},{1,32},{2,35},{3,34},{4,37},{5,36},{6,39},{7,38},{8,41},{9,... | collective-permute-start | bytes 786440 | tf_op jit(solution)/shard_map/ppermute | solution.py:51
  25.4 2.1 %collective-permute-start.8 = (bf16[2,32,2048]{2,1,0:T(8,128)(2,1)S(1)}, bf16[2,32,2048]{2,1,0:T(8,128)(2,1)S(1)}, u32[]{:S(2)}, u32[]{:S(2)}) collective-permute-start(bf16[2,32,2048]{2,1,0:T(8,128)(2,1)S(1)} %get-tuple-element.50.first), channel_id=1, source_target_pairs={{0,6},{1,7},{2,4},{3,5},{4,2},{5,3},{6,0},{7,1},{8,14},{9,15},{10,... | collective-permute-start | bytes 786440 | tf_op jit(solution)/shard_map/ppermute | solution.py:51
  27.5 3.5 %shard_map.93 = (bf16[224,6144]{1,0:T(8,128)(2,1)S(1)}, bf16[224,6144]{1,0:T(8,128)(2,1)S(1)}, bf16[224,6144]{1,0:T(8,128)(2,1)S(1)}) custom-call(bf16[224,12288]{1,0:T(8,128)(2,1)} %refs_0_.1, bf16[224,12288]{1,0:T(8,128)(2,1)} %refs_1_.1, bf16[224,12288]{1,0:T(8,128)(2,1)} %refs_2_.2), custom_call_target="tpu_custom_call" | custom-call | bytes 16777216 | tf_op jit(solution)/shard_map/pallas_call | solution.py:72
  31.0 2.0 %collective-permute-done.8.second = bf16[2,32,2048]{2,1,0:T(8,128)(2,1)S(1)} collective-permute-done((bf16[2,32,2048]{2,1,0:T(8,128)(2,1)S(1)}, bf16[2,32,2048]{2,1,0:T(8,128)(2,1)S(1)}, u32[]{:S(2)}, u32[]{:S(2)}) %collective-permute-start.8) | collective-permute-done | bytes 262176 | tf_op jit(solution)/shard_map/ppermute | solution.py:51
  33.4 1.0 collective-permute-start.13
  34.4 2.1 %collective-permute-start.15 = (bf16[2,64,2048]{2,1,0:T(8,128)(2,1)S(1)}, bf16[2,64,2048]{2,1,0:T(8,128)(2,1)S(1)}, u32[]{:S(2)}, u32[]{:S(2)}) collective-permute-start(bf16[2,64,2048]{2,1,0:T(8,128)(2,1)S(1)} %shard_map.98.first), channel_id=1, source_target_pairs={{0,6},{1,7},{2,4},{3,5},{4,2},{5,3},{6,0},{7,1},{8,14},{9,15},{10,... | collective-permute-start | bytes 1572872 | tf_op jit(solution)/shard_map/ppermute | solution.py:51
  36.5 7.0 %collective-permute-done.11.second = bf16[2,64,2048]{2,1,0:T(8,128)(2,1)S(1)} collective-permute-done((bf16[2,64,2048]{2,1,0:T(8,128)(2,1)S(1)}, bf16[2,64,2048]{2,1,0:T(8,128)(2,1)S(1)}, u32[]{:S(2)}, u32[]{:S(2)}) %collective-permute-start.11) | collective-permute-done | bytes 524320 | tf_op jit(solution)/shard_map/ppermute | solution.py:51
  43.9 2.2 %collective-permute-start.14 = (bf16[2,128,2048]{2,1,0:T(8,128)(2,1)S(1)}, bf16[2,128,2048]{2,1,0:T(8,128)(2,1)S(1)}, u32[]{:S(2)}, u32[]{:S(2)}) collective-permute-start(bf16[2,128,2048]{2,1,0:T(8,128)(2,1)S(1)} %shard_map.97.refs_1_.refs_2_), channel_id=1, source_target_pairs={{0,6},{1,7},{2,4},{3,5},{4,2},{5,3},{6,0},{7,1},{8,14},{9,15},{10,... | collective-permute-start | bytes 3145736 | tf_op jit(solution)/shard_map/ppermute | solution.py:51
  46.2 3.1 %collective-permute-start.16 = (bf16[2,128,2048]{2,1,0:T(8,128)(2,1)S(1)}, bf16[2,128,2048]{2,1,0:T(8,128)(2,1)S(1)}, u32[]{:S(2)}, u32[]{:S(2)}) collective-permute-start(bf16[2,128,2048]{2,1,0:T(8,128)(2,1)S(1)} %shard_map.99.refs_2_.refs_4_), channel_id=1, source_target_pairs={{0,33},{1,32},{2,35},{3,34},{4,37},{5,36},{6,39},{7,38},{8,41},{9,... | collective-permute-start | bytes 3145736 | tf_op jit(solution)/shard_map/ppermute | solution.py:51
  49.3 2.9 %shard_map.100.refs_4_ = f32[256,768]{1,0:T(8,128)S(1)} custom-call(bf16[2,128,2048]{2,1,0:T(8,128)(2,1)S(1)} %shard_map.95.refs_0_, bf16[2,128,2048]{2,1,0:T(8,128)(2,1)S(1)} %shard_map.97.refs_1_.refs_2_, bf16[2,128,2048]{2,1,0:T(8,128)(2,1)S(1)} %shard_map.99.refs_2_.refs_4_, bf16[224,6144]{1,0:T(8,128)(2,1)S(1)} %get-tuple-element.31.refs_3_.refs_1_.refs_6_, ...), custom_call_target="tpu_custom_call" | custom-call | flops 1056964608 | bytes 14680064 | tf_op jit(solution)/shard_map/pallas_call | solution.py:72
  52.2 7.5 %collective-permute-done.12.refs_0_.refs_1_ = bf16[2,128,2048]{2,1,0:T(8,128)(2,1)S(1)} collective-permute-done((bf16[2,128,2048]{2,1,0:T(8,128)(2,1)S(1)}, bf16[2,128,2048]{2,1,0:T(8,128)(2,1)S(1)}, u32[]{:S(2)}, u32[]{:S(2)}) %collective-permute-start.12) | collective-permute-done | bytes 1048608 | tf_op jit(solution)/shard_map/ppermute | solution.py:51
  59.7 1.1 shard_map.101.refs_4_
  60.8 1.1 shard_map.102.refs_4_
  62.3 1.1 shard_map.103.refs_0_
  63.4 2.3 %collective-permute-done.17.refs_1_ = f32[256,768]{1,0:T(8,128)S(1)} collective-permute-done((f32[256,768]{1,0:T(8,128)S(1)}, f32[256,768]{1,0:T(8,128)S(1)}, u32[]{:S(2)}, u32[]{:S(2)}) %collective-permute-start.17) | collective-permute-done | bytes 786464 | tf_op jit(solution)/shard_map/ppermute | solution.py:51
  65.7 1.9 %shard_map.104 = (bf16[128,2048]{1,0:T(8,128)(2,1)S(1)}, bf16[128,2048]{1,0:T(8,128)(2,1)S(1)}, bf16[128,2048]{1,0:T(8,128)(2,1)S(1)}, bf16[256,224]{1,0:T(8,128...) custom-call(f32[256,768]{1,0:T(8,128)S(1)} %shard_map.103.refs_0_, ...), custom_call_target="tpu_custom_call" | custom-call | flops 704643072 | bytes 8388608 | tf_op jit(solution)/shard_map/pallas_call | solution.py:72
  67.6 3.1 %collective-permute-start.18 = (bf16[128,2048]{1,0:T(8,128)(2,1)S(1)}, bf16[128,2048]{1,0:T(8,128)(2,1)S(1)}, u32[]{:S(2)}, u32[]{:S(2)}) collective-permute-start(bf16[128,2048]{1,0:T(8,128)(2,1)S(1)} %get-tuple-element.38), channel_id=1, source_target_pairs={{0,24},{1,25},{2,26},{3,27},{4,28},{5,29},{6,30},{7,31},{8,16},{9,... | collective-permute-start | bytes 1572872 | tf_op jit(solution)/shard_map/ppermute | solution.py:51
  70.7 1.1 %collective-permute-start.21 = (bf16[128,2048]{1,0:T(8,128)(2,1)S(1)}, bf16[128,2048]{1,0:T(8,128)(2,1)S(1)}, u32[]{:S(2)}, u32[]{:S(2)}) collective-permute-start(bf16[128,2048]{1,0:T(8,128)(2,1)S(1)} %get-tuple-element.40), channel_id=1, source_target_pairs={{0,6},{1,7},{2,4},{3,5},{4,2},{5,3},{6,0},{7,1},{8,14},{9,15},{10,... | collective-permute-start | bytes 1572872 | tf_op jit(solution)/shard_map/ppermute | solution.py:51
  71.9 2.0 %collective-permute-start.24 = (bf16[128,2048]{1,0:T(8,128)(2,1)S(1)}, bf16[128,2048]{1,0:T(8,128)(2,1)S(1)}, u32[]{:S(2)}, u32[]{:S(2)}) collective-permute-start(bf16[128,2048]{1,0:T(8,128)(2,1)S(1)} %get-tuple-element.42), channel_id=1, source_target_pairs={{0,33},{1,32},{2,35},{3,34},{4,37},{5,36},{6,39},{7,38},{8,41},{9,... | collective-permute-start | bytes 1572872 | tf_op jit(solution)/shard_map/ppermute | solution.py:51
  73.9 4.6 %shard_map.105 = (f32[128,2048]{1,0:T(8,128)S(1)}, f32[128,2048]{1,0:T(8,128)S(1)}, f32[128,2048]{1,0:T(8,128)S(1)}, bf16[224,6144]{1,0:T(8,128)(2,1)}, bf16[224...) custom-call(bf16[2,128,2048]{2,1,0:T(8,128)(2,1)S(1)} %shard_map.95.refs_0_, ...), custom_call_target="tpu_custom_call" | custom-call | flops 2818572288 | bytes 25165824 | tf_op jit(solution)/shard_map/pallas_call | solution.py:72
  78.6 2.7 %collective-permute-start.19 = (bf16[64,2048]{1,0:T(8,128)(2,1)S(1)}, bf16[64,2048]{1,0:T(8,128)(2,1)S(1)}, u32[]{:S(2)}, u32[]{:S(2)}) collective-permute-start(bf16[64,2048]{1,0:T(8,128)(2,1)S(1)} %slice.188), channel_id=1, source_target_pairs={{0,33},{1,32},{2,35},{3,34},{4,37},{5,36},{6,39},{7,38},{8,41},{9,... | collective-permute-start | bytes 786440 | tf_op jit(solution)/shard_map/ppermute | solution.py:51
  81.5 1.2 %collective-permute-start.22 = (bf16[64,2048]{1,0:T(8,128)(2,1)S(1)}, bf16[64,2048]{1,0:T(8,128)(2,1)S(1)}, u32[]{:S(2)}, u32[]{:S(2)}) collective-permute-start(bf16[64,2048]{1,0:T(8,128)(2,1)S(1)} %slice.187), channel_id=1, source_target_pairs={{0,24},{1,25},{2,26},{3,27},{4,28},{5,29},{6,30},{7,31},{8,16},{9,... | collective-permute-start | bytes 786440 | tf_op jit(solution)/shard_map/ppermute | solution.py:51
  82.8 2.2 %collective-permute-start.25 = (bf16[64,2048]{1,0:T(8,128)(2,1)S(1)}, bf16[64,2048]{1,0:T(8,128)(2,1)S(1)}, u32[]{:S(2)}, u32[]{:S(2)}) collective-permute-start(bf16[64,2048]{1,0:T(8,128)(2,1)S(1)} %slice.186), channel_id=1, source_target_pairs={{0,6},{1,7},{2,4},{3,5},{4,2},{5,3},{6,0},{7,1},{8,14},{9,15},{10,... | collective-permute-start | bytes 786440 | tf_op jit(solution)/shard_map/ppermute | solution.py:51
  85.0 1.3 %collective-permute-done.19 = bf16[64,2048]{1,0:T(8,128)(2,1)S(1)} collective-permute-done((bf16[64,2048]{1,0:T(8,128)(2,1)S(1)}, bf16[64,2048]{1,0:T(8,128)(2,1)S(1)}, u32[]{:S(2)}, u32[]{:S(2)}) %collective-permute-start.19) | collective-permute-done | bytes 262176 | tf_op jit(solution)/shard_map/ppermute | solution.py:51
  86.4 1.3 %collective-permute-start.20 = (bf16[32,2048]{1,0:T(8,128)(2,1)S(1)}, bf16[32,2048]{1,0:T(8,128)(2,1)S(1)}, u32[]{:S(2)}, u32[]{:S(2)}) collective-permute-start(bf16[32,2048]{1,0:T(8,128)(2,1)S(1)} %slice.191), channel_id=1, source_target_pairs={{0,6},{1,7},{2,4},{3,5},{4,2},{5,3},{6,0},{7,1},{8,14},{9,15},{10,... | collective-permute-start | bytes 393224 | tf_op jit(solution)/shard_map/ppermute | solution.py:51
  87.7 1.4 %collective-permute-done.22 = bf16[64,2048]{1,0:T(8,128)(2,1)S(1)} collective-permute-done((bf16[64,2048]{1,0:T(8,128)(2,1)S(1)}, bf16[64,2048]{1,0:T(8,128)(2,1)S(1)}, u32[]{:S(2)}, u32[]{:S(2)}) %collective-permute-start.22) | collective-permute-done | bytes 262176 | tf_op jit(solution)/shard_map/ppermute | solution.py:51
  89.2 1.1 %collective-permute-start.23 = (bf16[32,2048]{1,0:T(8,128)(2,1)S(1)}, bf16[32,2048]{1,0:T(8,128)(2,1)S(1)}, u32[]{:S(2)}, u32[]{:S(2)}) collective-permute-start(bf16[32,2048]{1,0:T(8,128)(2,1)S(1)} %slice.190), channel_id=1, source_target_pairs={{0,33},{1,32},{2,35},{3,34},{4,37},{5,36},{6,39},{7,38},{8,41},{9,... | collective-permute-start | bytes 393224 | tf_op jit(solution)/shard_map/ppermute | solution.py:51
  90.5 2.2 %collective-permute-start.26 = (bf16[32,2048]{1,0:T(8,128)(2,1)S(1)}, bf16[32,2048]{1,0:T(8,128)(2,1)S(1)}, u32[]{:S(2)}, u32[]{:S(2)}) collective-permute-start(bf16[32,2048]{1,0:T(8,128)(2,1)S(1)} %slice.189), channel_id=1, source_target_pairs={{0,24},{1,25},{2,26},{3,27},{4,28},{5,29},{6,30},{7,31},{8,16},{9,... | collective-permute-start | bytes 393224 | tf_op jit(solution)/shard_map/ppermute | solution.py:51
  93.2 2.3 %collective-permute-done.23 = bf16[32,2048]{1,0:T(8,128)(2,1)S(1)} collective-permute-done((bf16[32,2048]{1,0:T(8,128)(2,1)S(1)}, bf16[32,2048]{1,0:T(8,128)(2,1)S(1)}, u32[]{:S(2)}, u32[]{:S(2)}) %collective-permute-start.23) | collective-permute-done | bytes 131104 | tf_op jit(solution)/shard_map/ppermute | solution.py:51
  95.5 1.3 %collective-permute-done.26 = bf16[32,2048]{1,0:T(8,128)(2,1)S(1)} collective-permute-done((bf16[32,2048]{1,0:T(8,128)(2,1)S(1)}, bf16[32,2048]{1,0:T(8,128)(2,1)S(1)}, u32[]{:S(2)}, u32[]{:S(2)}) %collective-permute-start.26) | collective-permute-done | bytes 131104 | tf_op jit(solution)/shard_map/ppermute | solution.py:51
  97.2 4.3 %collective-permute-start.32 = (bf16[4,6144]{1,0:T(4,128)(2,1)S(1)}, bf16[4,6144]{1,0:T(4,128)(2,1)S(1)}, u32[]{:S(2)}, u32[]{:S(2)}) collective-permute-start(bf16[4,6144]{1,0:T(4,128)(2,1)S(1)} %get-tuple-element.53), channel_id=1, source_target_pairs={{0,40},{1,41},{2,42},{3,43},{4,44},{5,45},{6,46},{7,47},{8,32},{9,... | collective-permute-start | bytes 147464 | tf_op jit(solution)/shard_map/ppermute | solution.py:51
  101.5 1.6 %collective-permute-start.30 = (bf16[4,6144]{1,0:T(4,128)(2,1)S(1)}, bf16[4,6144]{1,0:T(4,128)(2,1)S(1)}, u32[]{:S(2)}, u32[]{:S(2)}) collective-permute-start(bf16[4,6144]{1,0:T(4,128)(2,1)S(1)} %get-tuple-element.55), channel_id=1, source_target_pairs={{0,8},{1,9},{2,10},{3,11},{4,12},{5,13},{6,14},{7,15},{8,0},{9,1},... | collective-permute-start | bytes 147464 | tf_op jit(solution)/shard_map/ppermute | solution.py:51
  103.1 3.4 %collective-permute-start.28 = (bf16[4,6144]{1,0:T(4,128)(2,1)S(1)}, bf16[4,6144]{1,0:T(4,128)(2,1)S(1)}, u32[]{:S(2)}, u32[]{:S(2)}) collective-permute-start(bf16[4,6144]{1,0:T(4,128)(2,1)S(1)} %get-tuple-element.57), channel_id=1, source_target_pairs={{0,32},{1,33},{2,34},{3,35},{4,36},{5,37},{6,38},{7,39},{8,40},{9,... | collective-permute-start | bytes 147464 | tf_op jit(solution)/shard_map/ppermute | solution.py:51
  106.5 1.5 %collective-permute-done.29 = bf16[4,6144]{1,0:T(4,128)(2,1)S(1)} collective-permute-done((bf16[4,6144]{1,0:T(4,128)(2,1)S(1)}, bf16[4,6144]{1,0:T(4,128)(2,1)S(1)}, u32[]{:S(2)}, u32[]{:S(2)}) %collective-permute-start.29) | collective-permute-done | bytes 49184 | tf_op jit(solution)/shard_map/ppermute | solution.py:51
  108.8 1.2 %collective-permute-done.34 = bf16[2,6144]{1,0:T(2,128)(2,1)S(1)} collective-permute-done((bf16[2,6144]{1,0:T(2,128)(2,1)S(1)}, bf16[2,6144]{1,0:T(2,128)(2,1)S(1)}, u32[]{:S(2)}, u32[]{:S(2)}) %collective-permute-start.34) | collective-permute-done | bytes 24608 | tf_op jit(solution)/shard_map/ppermute | solution.py:51
  110.1 0.7 maximum_bitcast_fusion
  (64 shorter events, 5.6 us)
Async XLA Ops:
  1.5 1.3 %collective-permute-start = (bf16[2,2,6144]{2,1,0:T(2,128)(2,1)S(1)}, bf16[2,2,6144]{2,1,0:T(2,128)(2,1)S(1)}, u32[]{:S(2)}, u32[]{:S(2)}) collective-permute-start(bf16[2,2,6144]{2,1,0:T(2,128)(2,1)S(1)} %get-tuple-element.46), channel_id=1, source_target_pairs={{0,64},{1,65},{2,66},{3,67},{4,68},{5,69},{6,70},{7,71},{8,72},{9,... | collective-permute-start | bytes 147464 | tf_op jit(solution)/shard_map/ppermute | solution.py:51
  3.8 8.5 %collective-permute-start.7 = (bf16[2,4,6144]{2,1,0:T(4,128)(2,1)S(1)}, bf16[2,4,6144]{2,1,0:T(4,128)(2,1)S(1)}, u32[]{:S(2)}, u32[]{:S(2)}) collective-permute-start(bf16[2,4,6144]{2,1,0:T(4,128)(2,1)S(1)} %pad_maximum_fusion.1), channel_id=1, source_target_pairs={{0,42},{1,43},{2,40},{3,41},{4,46},{5,47},{6,44},{7,45},{8,34},{9,... | collective-permute-start | bytes 294920 | tf_op jit(solution)/shard_map/ppermute | solution.py:51
  7.8 6.7 %collective-permute-start.6 = (bf16[2,4,6144]{2,1,0:T(4,128)(2,1)S(1)}, bf16[2,4,6144]{2,1,0:T(4,128)(2,1)S(1)}, u32[]{:S(2)}, u32[]{:S(2)}) collective-permute-start(bf16[2,4,6144]{2,1,0:T(4,128)(2,1)S(1)} %pad_maximum_fusion.1), channel_id=1, source_target_pairs={{0,40},{1,41},{2,42},{3,43},{4,44},{5,45},{6,46},{7,47},{8,32},{9,... | collective-permute-start | bytes 294920 | tf_op jit(solution)/shard_map/ppermute | solution.py:51
  7.9 7.0 %collective-permute-start.5 = (bf16[2,4,6144]{2,1,0:T(4,128)(2,1)S(1)}, bf16[2,4,6144]{2,1,0:T(4,128)(2,1)S(1)}, u32[]{:S(2)}, u32[]{:S(2)}) collective-permute-start(bf16[2,4,6144]{2,1,0:T(4,128)(2,1)S(1)} %pad_maximum_fusion.1), channel_id=1, source_target_pairs={{0,10},{1,11},{2,8},{3,9},{4,14},{5,15},{6,12},{7,13},{8,2},{9,3},... | collective-permute-start | bytes 294920 | tf_op jit(solution)/shard_map/ppermute | solution.py:51
  9.7 5.7 %collective-permute-start.4 = (bf16[2,4,6144]{2,1,0:T(4,128)(2,1)S(1)}, bf16[2,4,6144]{2,1,0:T(4,128)(2,1)S(1)}, u32[]{:S(2)}, u32[]{:S(2)}) collective-permute-start(bf16[2,4,6144]{2,1,0:T(4,128)(2,1)S(1)} %pad_maximum_fusion.1), channel_id=1, source_target_pairs={{0,8},{1,9},{2,10},{3,11},{4,12},{5,13},{6,14},{7,15},{8,0},{9,1},... | collective-permute-start | bytes 294920 | tf_op jit(solution)/shard_map/ppermute | solution.py:51
  10.0 6.0 %collective-permute-start.3 = (bf16[2,4,6144]{2,1,0:T(4,128)(2,1)S(1)}, bf16[2,4,6144]{2,1,0:T(4,128)(2,1)S(1)}, u32[]{:S(2)}, u32[]{:S(2)}) collective-permute-start(bf16[2,4,6144]{2,1,0:T(4,128)(2,1)S(1)} %pad_maximum_fusion.1), channel_id=1, source_target_pairs={{0,34},{1,35},{2,32},{3,33},{4,38},{5,39},{6,36},{7,37},{8,42},{9,... | collective-permute-start | bytes 294920 | tf_op jit(solution)/shard_map/ppermute | solution.py:51
  12.4 4.6 %collective-permute-start.2 = (bf16[2,4,6144]{2,1,0:T(4,128)(2,1)S(1)}, bf16[2,4,6144]{2,1,0:T(4,128)(2,1)S(1)}, u32[]{:S(2)}, u32[]{:S(2)}) collective-permute-start(bf16[2,4,6144]{2,1,0:T(4,128)(2,1)S(1)} %pad_maximum_fusion.1), channel_id=1, source_target_pairs={{0,32},{1,33},{2,34},{3,35},{4,36},{5,37},{6,38},{7,39},{8,40},{9,... | collective-permute-start | bytes 294920 | tf_op jit(solution)/shard_map/ppermute | solution.py:51
  14.5 4.6 %collective-permute-start.1 = (bf16[2,4,6144]{2,1,0:T(4,128)(2,1)S(1)}, bf16[2,4,6144]{2,1,0:T(4,128)(2,1)S(1)}, u32[]{:S(2)}, u32[]{:S(2)}) collective-permute-start(bf16[2,4,6144]{2,1,0:T(4,128)(2,1)S(1)} %pad_maximum_fusion.1), channel_id=1, source_target_pairs={{0,2},{1,3},{2,0},{3,1},{4,6},{5,7},{6,4},{7,5},{8,10},{9,11},{10,... | collective-permute-start | bytes 294920 | tf_op jit(solution)/shard_map/ppermute | solution.py:51
  20.0 11.0 %collective-permute-start.10 = (bf16[2,32,2048]{2,1,0:T(8,128)(2,1)S(1)}, bf16[2,32,2048]{2,1,0:T(8,128)(2,1)S(1)}, u32[]{:S(2)}, u32[]{:S(2)}) collective-permute-start(bf16[2,32,2048]{2,1,0:T(8,128)(2,1)S(1)} %get-tuple-element.48.first), channel_id=1, source_target_pairs={{0,24},{1,25},{2,26},{3,27},{4,28},{5,29},{6,30},{7,31},{8,16},{9,... | collective-permute-start | bytes 786440 | tf_op jit(solution)/shard_map/ppermute | solution.py:51
  22.4 8.6 %collective-permute-start.9 = (bf16[2,32,2048]{2,1,0:T(8,128)(2,1)S(1)}, bf16[2,32,2048]{2,1,0:T(8,128)(2,1)S(1)}, u32[]{:S(2)}, u32[]{:S(2)}) collective-permute-start(bf16[2,32,2048]{2,1,0:T(8,128)(2,1)S(1)} %get-tuple-element.49.first), channel_id=1, source_target_pairs={{0,33},{1,32},{2,35},{3,34},{4,37},{5,36},{6,39},{7,38},{8,41},{9,... | collective-permute-start | bytes 786440 | tf_op jit(solution)/shard_map/ppermute | solution.py:51
  25.4 7.6 %collective-permute-start.8 = (bf16[2,32,2048]{2,1,0:T(8,128)(2,1)S(1)}, bf16[2,32,2048]{2,1,0:T(8,128)(2,1)S(1)}, u32[]{:S(2)}, u32[]{:S(2)}) collective-permute-start(bf16[2,32,2048]{2,1,0:T(8,128)(2,1)S(1)} %get-tuple-element.50.first), channel_id=1, source_target_pairs={{0,6},{1,7},{2,4},{3,5},{4,2},{5,3},{6,0},{7,1},{8,14},{9,15},{10,... | collective-permute-start | bytes 786440 | tf_op jit(solution)/shard_map/ppermute | solution.py:51
  33.1 10.5 %collective-permute-start.11 = (bf16[2,64,2048]{2,1,0:T(8,128)(2,1)S(1)}, bf16[2,64,2048]{2,1,0:T(8,128)(2,1)S(1)}, u32[]{:S(2)}, u32[]{:S(2)}) collective-permute-start(bf16[2,64,2048]{2,1,0:T(8,128)(2,1)S(1)} %shard_map.94.first), channel_id=1, source_target_pairs={{0,33},{1,32},{2,35},{3,34},{4,37},{5,36},{6,39},{7,38},{8,41},{9,... | collective-permute-start | bytes 1572872 | tf_op jit(solution)/shard_map/ppermute | solution.py:51
  33.4 10.5 %collective-permute-start.13 = (bf16[2,64,2048]{2,1,0:T(8,128)(2,1)S(1)}, bf16[2,64,2048]{2,1,0:T(8,128)(2,1)S(1)}, u32[]{:S(2)}, u32[]{:S(2)}) collective-permute-start(bf16[2,64,2048]{2,1,0:T(8,128)(2,1)S(1)} %shard_map.96.first), channel_id=1, source_target_pairs={{0,24},{1,25},{2,26},{3,27},{4,28},{5,29},{6,30},{7,31},{8,16},{9,... | collective-permute-start | bytes 1572872 | tf_op jit(solution)/shard_map/ppermute | solution.py:51
  34.4 11.7 %collective-permute-start.15 = (bf16[2,64,2048]{2,1,0:T(8,128)(2,1)S(1)}, bf16[2,64,2048]{2,1,0:T(8,128)(2,1)S(1)}, u32[]{:S(2)}, u32[]{:S(2)}) collective-permute-start(bf16[2,64,2048]{2,1,0:T(8,128)(2,1)S(1)} %shard_map.98.first), channel_id=1, source_target_pairs={{0,6},{1,7},{2,4},{3,5},{4,2},{5,3},{6,0},{7,1},{8,14},{9,15},{10,... | collective-permute-start | bytes 1572872 | tf_op jit(solution)/shard_map/ppermute | solution.py:51
  43.6 16.1 %collective-permute-start.12 = (bf16[2,128,2048]{2,1,0:T(8,128)(2,1)S(1)}, bf16[2,128,2048]{2,1,0:T(8,128)(2,1)S(1)}, u32[]{:S(2)}, u32[]{:S(2)}) collective-permute-start(bf16[2,128,2048]{2,1,0:T(8,128)(2,1)S(1)} %shard_map.95.refs_0_), channel_id=1, source_target_pairs={{0,24},{1,25},{2,26},{3,27},{4,28},{5,29},{6,30},{7,31},{8,16},{9,... | collective-permute-start | bytes 3145736 | tf_op jit(solution)/shard_map/ppermute | solution.py:51
  43.9 16.8 %collective-permute-start.14 = (bf16[2,128,2048]{2,1,0:T(8,128)(2,1)S(1)}, bf16[2,128,2048]{2,1,0:T(8,128)(2,1)S(1)}, u32[]{:S(2)}, u32[]{:S(2)}) collective-permute-start(bf16[2,128,2048]{2,1,0:T(8,128)(2,1)S(1)} %shard_map.97.refs_1_.refs_2_), channel_id=1, source_target_pairs={{0,6},{1,7},{2,4},{3,5},{4,2},{5,3},{6,0},{7,1},{8,14},{9,15},{10,... | collective-permute-start | bytes 3145736 | tf_op jit(solution)/shard_map/ppermute | solution.py:51
  46.2 16.1 %collective-permute-start.16 = (bf16[2,128,2048]{2,1,0:T(8,128)(2,1)S(1)}, bf16[2,128,2048]{2,1,0:T(8,128)(2,1)S(1)}, u32[]{:S(2)}, u32[]{:S(2)}) collective-permute-start(bf16[2,128,2048]{2,1,0:T(8,128)(2,1)S(1)} %shard_map.99.refs_2_.refs_4_), channel_id=1, source_target_pairs={{0,33},{1,32},{2,35},{3,34},{4,37},{5,36},{6,39},{7,38},{8,41},{9,... | collective-permute-start | bytes 3145736 | tf_op jit(solution)/shard_map/ppermute | solution.py:51
  61.8 3.9 %copy-start = (bf16[256,256]{1,0:T(8,128)(2,1)S(1)}, bf16[256,256]{1,0:T(8,128)(2,1)}, u32[]{:S(2)}) copy-start(bf16[256,256]{1,0:T(8,128)(2,1)} %constant.10.clone.refs_2_) | copy-start | bytes 393220
  63.3 2.4 %collective-permute-start.17 = (f32[256,768]{1,0:T(8,128)S(1)}, f32[256,768]{1,0:T(8,128)S(1)}, u32[]{:S(2)}, u32[]{:S(2)}) collective-permute-start(f32[256,768]{1,0:T(8,128)S(1)} %shard_map.103.refs_0_), channel_id=1, source_target_pairs={{0,64},{1,65},{2,66},{3,67},{4,68},{5,69},{6,70},{7,71},{8,72},{9,... | collective-permute-start | bytes 2359304 | tf_op jit(solution)/shard_map/ppermute | solution.py:51
  67.6 10.9 %collective-permute-start.18 = (bf16[128,2048]{1,0:T(8,128)(2,1)S(1)}, bf16[128,2048]{1,0:T(8,128)(2,1)S(1)}, u32[]{:S(2)}, u32[]{:S(2)}) collective-permute-start(bf16[128,2048]{1,0:T(8,128)(2,1)S(1)} %get-tuple-element.38), channel_id=1, source_target_pairs={{0,24},{1,25},{2,26},{3,27},{4,28},{5,29},{6,30},{7,31},{8,16},{9,... | collective-permute-start | bytes 1572872 | tf_op jit(solution)/shard_map/ppermute | solution.py:51
  70.7 10.6 %collective-permute-start.21 = (bf16[128,2048]{1,0:T(8,128)(2,1)S(1)}, bf16[128,2048]{1,0:T(8,128)(2,1)S(1)}, u32[]{:S(2)}, u32[]{:S(2)}) collective-permute-start(bf16[128,2048]{1,0:T(8,128)(2,1)S(1)} %get-tuple-element.40), channel_id=1, source_target_pairs={{0,6},{1,7},{2,4},{3,5},{4,2},{5,3},{6,0},{7,1},{8,14},{9,15},{10,... | collective-permute-start | bytes 1572872 | tf_op jit(solution)/shard_map/ppermute | solution.py:51
  71.9 10.8 %collective-permute-start.24 = (bf16[128,2048]{1,0:T(8,128)(2,1)S(1)}, bf16[128,2048]{1,0:T(8,128)(2,1)S(1)}, u32[]{:S(2)}, u32[]{:S(2)}) collective-permute-start(bf16[128,2048]{1,0:T(8,128)(2,1)S(1)} %get-tuple-element.42), channel_id=1, source_target_pairs={{0,33},{1,32},{2,35},{3,34},{4,37},{5,36},{6,39},{7,38},{8,41},{9,... | collective-permute-start | bytes 1572872 | tf_op jit(solution)/shard_map/ppermute | solution.py:51
  78.6 7.7 %collective-permute-start.19 = (bf16[64,2048]{1,0:T(8,128)(2,1)S(1)}, bf16[64,2048]{1,0:T(8,128)(2,1)S(1)}, u32[]{:S(2)}, u32[]{:S(2)}) collective-permute-start(bf16[64,2048]{1,0:T(8,128)(2,1)S(1)} %slice.188), channel_id=1, source_target_pairs={{0,33},{1,32},{2,35},{3,34},{4,37},{5,36},{6,39},{7,38},{8,41},{9,... | collective-permute-start | bytes 786440 | tf_op jit(solution)/shard_map/ppermute | solution.py:51
  81.5 7.7 %collective-permute-start.22 = (bf16[64,2048]{1,0:T(8,128)(2,1)S(1)}, bf16[64,2048]{1,0:T(8,128)(2,1)S(1)}, u32[]{:S(2)}, u32[]{:S(2)}) collective-permute-start(bf16[64,2048]{1,0:T(8,128)(2,1)S(1)} %slice.187), channel_id=1, source_target_pairs={{0,24},{1,25},{2,26},{3,27},{4,28},{5,29},{6,30},{7,31},{8,16},{9,... | collective-permute-start | bytes 786440 | tf_op jit(solution)/shard_map/ppermute | solution.py:51
  82.8 7.7 %collective-permute-start.25 = (bf16[64,2048]{1,0:T(8,128)(2,1)S(1)}, bf16[64,2048]{1,0:T(8,128)(2,1)S(1)}, u32[]{:S(2)}, u32[]{:S(2)}) collective-permute-start(bf16[64,2048]{1,0:T(8,128)(2,1)S(1)} %slice.186), channel_id=1, source_target_pairs={{0,6},{1,7},{2,4},{3,5},{4,2},{5,3},{6,0},{7,1},{8,14},{9,15},{10,... | collective-permute-start | bytes 786440 | tf_op jit(solution)/shard_map/ppermute | solution.py:51
  86.4 6.8 %collective-permute-start.20 = (bf16[32,2048]{1,0:T(8,128)(2,1)S(1)}, bf16[32,2048]{1,0:T(8,128)(2,1)S(1)}, u32[]{:S(2)}, u32[]{:S(2)}) collective-permute-start(bf16[32,2048]{1,0:T(8,128)(2,1)S(1)} %slice.191), channel_id=1, source_target_pairs={{0,6},{1,7},{2,4},{3,5},{4,2},{5,3},{6,0},{7,1},{8,14},{9,15},{10,... | collective-permute-start | bytes 393224 | tf_op jit(solution)/shard_map/ppermute | solution.py:51
  89.2 6.3 %collective-permute-start.23 = (bf16[32,2048]{1,0:T(8,128)(2,1)S(1)}, bf16[32,2048]{1,0:T(8,128)(2,1)S(1)}, u32[]{:S(2)}, u32[]{:S(2)}) collective-permute-start(bf16[32,2048]{1,0:T(8,128)(2,1)S(1)} %slice.190), channel_id=1, source_target_pairs={{0,33},{1,32},{2,35},{3,34},{4,37},{5,36},{6,39},{7,38},{8,41},{9,... | collective-permute-start | bytes 393224 | tf_op jit(solution)/shard_map/ppermute | solution.py:51
  90.5 6.3 %collective-permute-start.26 = (bf16[32,2048]{1,0:T(8,128)(2,1)S(1)}, bf16[32,2048]{1,0:T(8,128)(2,1)S(1)}, u32[]{:S(2)}, u32[]{:S(2)}) collective-permute-start(bf16[32,2048]{1,0:T(8,128)(2,1)S(1)} %slice.189), channel_id=1, source_target_pairs={{0,24},{1,25},{2,26},{3,27},{4,28},{5,29},{6,30},{7,31},{8,16},{9,... | collective-permute-start | bytes 393224 | tf_op jit(solution)/shard_map/ppermute | solution.py:51
  97.0 6.0 %collective-permute-start.27 = (bf16[4,6144]{1,0:T(4,128)(2,1)S(1)}, bf16[4,6144]{1,0:T(4,128)(2,1)S(1)}, u32[]{:S(2)}, u32[]{:S(2)}) collective-permute-start(bf16[4,6144]{1,0:T(4,128)(2,1)S(1)} %get-tuple-element.51), channel_id=1, source_target_pairs={{0,2},{1,3},{2,0},{3,1},{4,6},{5,7},{6,4},{7,5},{8,10},{9,11},{10,... | collective-permute-start | bytes 147464 | tf_op jit(solution)/shard_map/ppermute | solution.py:51
  97.1 6.0 %collective-permute-start.33 = (bf16[4,6144]{1,0:T(4,128)(2,1)S(1)}, bf16[4,6144]{1,0:T(4,128)(2,1)S(1)}, u32[]{:S(2)}, u32[]{:S(2)}) collective-permute-start(bf16[4,6144]{1,0:T(4,128)(2,1)S(1)} %get-tuple-element.52), channel_id=1, source_target_pairs={{0,42},{1,43},{2,40},{3,41},{4,46},{5,47},{6,44},{7,45},{8,34},{9,... | collective-permute-start | bytes 147464 | tf_op jit(solution)/shard_map/ppermute | solution.py:51
  97.2 9.3 %collective-permute-start.32 = (bf16[4,6144]{1,0:T(4,128)(2,1)S(1)}, bf16[4,6144]{1,0:T(4,128)(2,1)S(1)}, u32[]{:S(2)}, u32[]{:S(2)}) collective-permute-start(bf16[4,6144]{1,0:T(4,128)(2,1)S(1)} %get-tuple-element.53), channel_id=1, source_target_pairs={{0,40},{1,41},{2,42},{3,43},{4,44},{5,45},{6,46},{7,47},{8,32},{9,... | collective-permute-start | bytes 147464 | tf_op jit(solution)/shard_map/ppermute | solution.py:51
  101.5 5.0 %collective-permute-start.31 = (bf16[4,6144]{1,0:T(4,128)(2,1)S(1)}, bf16[4,6144]{1,0:T(4,128)(2,1)S(1)}, u32[]{:S(2)}, u32[]{:S(2)}) collective-permute-start(bf16[4,6144]{1,0:T(4,128)(2,1)S(1)} %get-tuple-element.54), channel_id=1, source_target_pairs={{0,10},{1,11},{2,8},{3,9},{4,14},{5,15},{6,12},{7,13},{8,2},{9,3},... | collective-permute-start | bytes 147464 | tf_op jit(solution)/shard_map/ppermute | solution.py:51
  101.5 5.0 %collective-permute-start.30 = (bf16[4,6144]{1,0:T(4,128)(2,1)S(1)}, bf16[4,6144]{1,0:T(4,128)(2,1)S(1)}, u32[]{:S(2)}, u32[]{:S(2)}) collective-permute-start(bf16[4,6144]{1,0:T(4,128)(2,1)S(1)} %get-tuple-element.55), channel_id=1, source_target_pairs={{0,8},{1,9},{2,10},{3,11},{4,12},{5,13},{6,14},{7,15},{8,0},{9,1},... | collective-permute-start | bytes 147464 | tf_op jit(solution)/shard_map/ppermute | solution.py:51
  103.0 5.0 %collective-permute-start.29 = (bf16[4,6144]{1,0:T(4,128)(2,1)S(1)}, bf16[4,6144]{1,0:T(4,128)(2,1)S(1)}, u32[]{:S(2)}, u32[]{:S(2)}) collective-permute-start(bf16[4,6144]{1,0:T(4,128)(2,1)S(1)} %get-tuple-element.56), channel_id=1, source_target_pairs={{0,34},{1,35},{2,32},{3,33},{4,38},{5,39},{6,36},{7,37},{8,42},{9,... | collective-permute-start | bytes 147464 | tf_op jit(solution)/shard_map/ppermute | solution.py:51
  103.1 5.5 %collective-permute-start.28 = (bf16[4,6144]{1,0:T(4,128)(2,1)S(1)}, bf16[4,6144]{1,0:T(4,128)(2,1)S(1)}, u32[]{:S(2)}, u32[]{:S(2)}) collective-permute-start(bf16[4,6144]{1,0:T(4,128)(2,1)S(1)} %get-tuple-element.57), channel_id=1, source_target_pairs={{0,32},{1,33},{2,34},{3,35},{4,36},{5,37},{6,38},{7,39},{8,40},{9,... | collective-permute-start | bytes 147464 | tf_op jit(solution)/shard_map/ppermute | solution.py:51
  108.7 1.3 %collective-permute-start.34 = (bf16[2,6144]{1,0:T(2,128)(2,1)S(1)}, bf16[2,6144]{1,0:T(2,128)(2,1)S(1)}, u32[]{:S(2)}, u32[]{:S(2)}) collective-permute-start(bf16[2,6144]{1,0:T(2,128)(2,1)S(1)} %broadcast_select_fusion.6), channel_id=1, source_target_pairs={{0,64},{1,65},{2,66},{3,67},{4,68},{5,69},{6,70},{7,71},{8,72},{9,... | collective-permute-start | bytes 73736 | tf_op jit(solution)/shard_map/ppermute | solution.py:51

commit v3 on v2

--- a/solution.py
+++ b/solution.py
@@ -10,6 +10,7 @@
 
 AXES = ("rep", "tp", "att")
 CHUNKS = (("x", "y", "z"), ("y", "z", "x"), ("z", "x", "y"))
+SCATTER_NEARER = "xy"
 CUBE = ("x", "y", "xy", "z", "xz", "yz", "xyz")
 GROUP = 32
 LANES = 256
@@ -32,12 +33,12 @@
     return sorted(result)
 
 
-def neighbour(axes, stage):
+def neighbour(axes, stage, nearer="xyz"):
     moves = []
     for core in range(2):
         moves.append(
             tuple(
-                (1 if core == stage else 3) if name in axes else 0
+                (1 if core == stage ^ (name not in nearer) else 3) if name in axes else 0
                 for name in "xyz"
             )
         )
@@ -174,10 +175,10 @@
 
 
 def middle_kernel(third, *refs):
-    part, other, one_hot, gate, up = refs[:5]
-    sends, (gate_out, up_out, hidden_out) = refs[5:8], refs[8:11]
+    part, other, cross_core, scatter, gate, up = refs[:6]
+    sends, (gate_out, up_out, hidden_out, gate_sums, up_sums) = refs[6:9], refs[9:14]
     local_ff = gate.shape[0]
-    matrix = one_hot[...]
+    matrix = cross_core[...]
     total = [
         part[:, i * LANES : (i + 1) * LANES]
         + permuted(matrix, other[:, i * LANES : (i + 1) * LANES])
@@ -191,13 +192,20 @@
         jnp.bfloat16
     )
     up_out[...] = (hidden_grad * act).astype(jnp.bfloat16)
-    input_products(third, 4, gate_out, up_out, gate, up, sends)
-
-
-def rest_kernel(third, *refs):
-    pieces, (gate, up, gate_part, up_part, hidden) = refs[:6], refs[6:11]
-    keeps, outs, (results, sems) = refs[11:14], refs[14:17], refs[17:]
-    input_products(third, 0, gate_part, up_part, gate, up, keeps)
+    for source, target in ((gate_out, gate_sums), (up_out, up_sums)):
+        target[...] = jnp.dot(
+            scatter[...], source[...], preferred_element_type=jnp.float32
+        ).astype(jnp.bfloat16)
+    input_products(third, 4, gate_sums, up_sums, gate, up, sends)
+
+
+def keep_kernel(third, gate_sums, up_sums, gate, up, *keeps):
+    input_products(third, 0, gate_sums, up_sums, gate, up, keeps)
+
+
+def weight_kernel(third, *refs):
+    pieces, (gate_part, up_part, hidden) = refs[:6], refs[6:9]
+    outs, (results, sems) = refs[9:12], refs[12:]
     copies = []
     for k in range(3):
         order = label_order(CHUNKS[k])
@@ -222,12 +230,14 @@
         copy.wait()
 
 
-def cross_core_rows():
+def exchanged_rows(axes):
+    mask = sum({"x": 1, "y": 2, "z": 4}[axis] for axis in axes)
     matrix = np.zeros((8 * GROUP, 8 * GROUP), np.float32)
     for high in range(8):
         for low in range(8):
+            new_high, new_low = high & ~mask | low & mask, low & ~mask | high & mask
             for row in range(4):
-                matrix[(high * 8 + low) * 4 + row, (low * 8 + high) * 4 + row] = 1.0
+                matrix[(high * 8 + low) * 4 + row, (new_high * 8 + new_low) * 4 + row] = 1.0
     return jnp.asarray(matrix, jnp.bfloat16)
 
 
@@ -250,10 +260,6 @@
     local_ff = gate_weight.shape[0]
     rows = 8 * GROUP
     vmem, hbm = (lambda value: ("vmem", value)), (lambda value: ("hbm", value))
-    fourth = [
-        send(block[:, :, k * third : (k + 1) * third], neighbour(CHUNKS[k][0], 1))
-        for k in range(3)
-    ]
     weights = call(
         functools.partial(load_kernel, third),
         [hbm(gate_weight), hbm(up_weight), hbm(down_weight)],
@@ -261,16 +267,13 @@
         [pltpu.SemaphoreType.DMA((3,))],
         megabytes=16,
     )
-    fourth, weights = lax.optimization_barrier((fourth, weights))
-    held, last = [], []
-    for k in range(3):
-        own = block[:, :, k * third : (k + 1) * third]
-        for stage, axis in enumerate(CHUNKS[k]):
-            new = fourth[k] if stage == 0 else send(own, neighbour(axis, 1))
-            if stage < 2:
-                own = join(own, new)
-        held.append(own)
-        last.append(new)
+    held = [block[:, :, k * third : (k + 1) * third] for k in range(3)]
+    for stage in range(3):
+        last = [send(held[k], neighbour(CHUNKS[k][stage], 1)) for k in range(3)]
+        if stage == 1:
+            last[0], weights = lax.optimization_barrier((last[0], weights))
+        if stage < 2:
+            held = [join(own, new) for own, new in zip(held, last)]
     (part,) = call(
         functools.partial(early_kernel, third),
         [vmem(value) for value in (*held, *weights)],
@@ -288,44 +291,63 @@
         )
     other = send(part, OTHER_CORE)
     small = ("vmem", (rows, local_ff), jnp.bfloat16)
+    scattered = "".join(axis for axis in "xyz" if axis not in SCATTER_NEARER)
+    operands = (
+        part,
+        other,
+        exchanged_rows("xyz"),
+        exchanged_rows(scattered),
+        weights[0],
+        weights[1],
+    )
     results = call(
         functools.partial(middle_kernel, third),
-        [vmem(value) for value in (part, other, cross_core_rows(), weights[0], weights[1])],
-        [("vmem", (rows // 2, third), jnp.bfloat16)] * 3 + [small] * 3,
+        [vmem(value) for value in operands],
+        [("vmem", (rows // 2, third), jnp.bfloat16)] * 3 + [small] * 5,
         flops=2 * rows * local_ff * half,
         megabytes=8,
     )
     outgoing, parts = results[:3], results[3:]
-    received = [send(out, neighbour(CHUNKS[k][2], 1)) for k, out in enumerate(outgoing)]
-    results = call(
-        functools.partial(rest_kernel, third),
-        [vmem(piece) for k in range(3) for piece in (held[k], last[k])]
-        + [vmem(value) for value in (weights[0], weights[1], *parts)],
-        [("vmem", (rows // 2, third), jnp.float32)] * 3
-        + [("hbm", (local_ff, half), jnp.bfloat16)] * 3,
-        [pltpu.VMEM((3, local_ff, half), jnp.bfloat16), pltpu.SemaphoreType.DMA((9,))],
-        limit=24,
-        flops=8 * rows * local_ff * half,
-        megabytes=24,
-    )
-    sums, (gate_grad, up_grad, down_grad) = results[:3], results[3:]
+    received = [send(out, neighbour(CHUNKS[k][2], 1, SCATTER_NEARER)) for k, out in enumerate(outgoing)]
+    sums = call(
+        functools.partial(keep_kernel, third),
+        [vmem(value) for value in (*parts[3:], weights[0], weights[1])],
+        [("vmem", (rows // 2, third), jnp.float32)] * 3,
+        flops=2 * rows * local_ff * half,
+        megabytes=8,
+    )
 
     for stage in (2, 1, 0):
         sums = [value + new.astype(jnp.float32) for value, new in zip(sums, received)]
         if stage:
             cut = sums[0].shape[0] // 2
             received = [
-                send(value[cut:].astype(jnp.bfloat16), neighbour(CHUNKS[k][stage - 1], 1))
+                send(value[cut:].astype(jnp.bfloat16), neighbour(CHUNKS[k][stage - 1], 1, SCATTER_NEARER))
                 for k, value in enumerate(sums)
             ]
             sums = [value[:cut] for value in sums]
     value = jnp.concatenate(sums, axis=1)
-    cut = value.shape[0] // 8
+    cut = value.shape[0] // 2
+    leaving, parts = lax.optimization_barrier((value[cut:].astype(jnp.bfloat16), parts))
+    arriving = send(leaving, neighbour("z", 0, SCATTER_NEARER))
+    grads = call(
+        functools.partial(weight_kernel, third),
+        [vmem(piece) for k in range(3) for piece in (held[k], last[k])]
+        + [vmem(value) for value in parts[:3]],
+        [("hbm", (local_ff, half), jnp.bfloat16)] * 3,
+        [pltpu.VMEM((3, local_ff, half), jnp.bfloat16), pltpu.SemaphoreType.DMA((9,))],
+        limit=24,
+        flops=6 * rows * local_ff * half,
+        megabytes=24,
+    )
+    arriving, (gate_grad, up_grad, down_grad) = lax.optimization_barrier((arriving, grads))
+    value = value[:cut] + arriving.astype(jnp.float32)
+    cut = value.shape[0] // 4
     value = value[:cut] + sum(
-        send(value[i * cut : (i + 1) * cut].astype(jnp.bfloat16), neighbour(axes, 0)).astype(
+        send(value[i * cut : (i + 1) * cut].astype(jnp.bfloat16), neighbour(axes, 0, SCATTER_NEARER)).astype(
             jnp.float32
         )
-        for i, axes in enumerate(CUBE, 1)
+        for i, axes in ((1, "x"), (2, "y"), (3, "xy"))
     )
     value = value.astype(jnp.bfloat16)
     mine = jnp.where(core == 0, value[:micro], value[micro:])

time: 112 us -> 108 us (0.964)
  starting transfers between devices: 52.3 us -> 48.9 us
    ppermute x35 -> x32, starting transfers between devices: 52.3 us -> 48.9 us  [send(): return lax.ppermute(value, AXES, route)]
    ppermute x35 -> x32, waiting for transfers between devices: 36.6 us -> 35.6 us  [send(): return lax.ppermute(value, AXES, route)]
    pallas_call x13 -> x14, Pallas kernels: 16.3 us -> 16.5 us  [call(): pl.pallas_call(kernel, out_shape=[pltpu.VMEM(shape, dtype) if place == 'v...]
  transfers between devices with their start and end apart: 35 -> 32, of which waited for: 21 -> 22; matrix products, arithmetic and copies ran while one was open for 1% -> 1% of each run, Pallas kernels for 12% -> 13%
where the time goes in v3:
time: 108 us; the launch traced here: 106 us
  starting transfers between devices  48.9 us (45%)
  waiting for transfers between devices  35.6 us (33%)
  Pallas kernels  16.5 us (15%)
  other arithmetic  3.34 us (3%)
  local copies, waits for them, and re-layouts  1.1 us (1%)
    ppermute x32, starting transfers between devices, send(): return lax.ppermute(value, AXES, route)  48.9 us
    ppermute x32, waiting for transfers between devices, send(): return lax.ppermute(value, AXES, route)  35.6 us
    pallas_call x14, Pallas kernels, call(): pl.pallas_call(kernel, out_shape=[pltpu.VMEM(shape, dtype) if place == 'v...  16.5 us
  transfers between devices with their start and end apart: 32, of which 22 were waited for; matrix products, arithmetic and copies ran while one was open for 1% of the time, Pallas kernels for 13%

profile of v3, /device:TPU:0, one launch (start us, length us, event | category | flops | bytes accessed | tf_op | source)
XLA Modules:
  0.0 106.4 jit_solution(14219384811816826946)
XLA Ops:
  0.6 0.9 broadcast_select_fusion.2
  1.6 1.2 %collective-permute-done = bf16[2,2,6144]{2,1,0:T(2,128)(2,1)S(1)} collective-permute-done((bf16[2,2,6144]{2,1,0:T(2,128)(2,1)S(1)}, bf16[2,2,6144]{2,1,0:T(2,128)(2,1)S(1)}, u32[]{:S(2)}, u32[]{:S(2)}) %collective-permute-start) | collective-permute-done | bytes 49184 | tf_op jit(solution)/shard_map/ppermute | solution.py:52
  2.8 0.9 broadcast_select_fusion
  3.8 4.0 %collective-permute-start.7 = (bf16[2,4,6144]{2,1,0:T(4,128)(2,1)S(1)}, bf16[2,4,6144]{2,1,0:T(4,128)(2,1)S(1)}, u32[]{:S(2)}, u32[]{:S(2)}) collective-permute-start(bf16[2,4,6144]{2,1,0:T(4,128)(2,1)S(1)} %pad_maximum_fusion.1), channel_id=1, source_target_pairs={{0,42},{1,43},{2,40},{3,41},{4,46},{5,47},{6,44},{7,45},{8,34},{9,... | collective-permute-start | bytes 294920 | tf_op jit(solution)/shard_map/ppermute | solution.py:52
  7.9 1.9 %collective-permute-start.5 = (bf16[2,4,6144]{2,1,0:T(4,128)(2,1)S(1)}, bf16[2,4,6144]{2,1,0:T(4,128)(2,1)S(1)}, u32[]{:S(2)}, u32[]{:S(2)}) collective-permute-start(bf16[2,4,6144]{2,1,0:T(4,128)(2,1)S(1)} %pad_maximum_fusion.1), channel_id=1, source_target_pairs={{0,10},{1,11},{2,8},{3,9},{4,14},{5,15},{6,12},{7,13},{8,2},{9,3},... | collective-permute-start | bytes 294920 | tf_op jit(solution)/shard_map/ppermute | solution.py:52
  10.0 2.4 %collective-permute-start.3 = (bf16[2,4,6144]{2,1,0:T(4,128)(2,1)S(1)}, bf16[2,4,6144]{2,1,0:T(4,128)(2,1)S(1)}, u32[]{:S(2)}, u32[]{:S(2)}) collective-permute-start(bf16[2,4,6144]{2,1,0:T(4,128)(2,1)S(1)} %pad_maximum_fusion.1), channel_id=1, source_target_pairs={{0,34},{1,35},{2,32},{3,33},{4,38},{5,39},{6,36},{7,37},{8,42},{9,... | collective-permute-start | bytes 294920 | tf_op jit(solution)/shard_map/ppermute | solution.py:52
  12.8 1.7 %collective-permute-done.6 = bf16[2,4,6144]{2,1,0:T(4,128)(2,1)S(1)} collective-permute-done((bf16[2,4,6144]{2,1,0:T(4,128)(2,1)S(1)}, bf16[2,4,6144]{2,1,0:T(4,128)(2,1)S(1)}, u32[]{:S(2)}, u32[]{:S(2)}) %collective-permute-start.6) | collective-permute-done | bytes 98336 | tf_op jit(solution)/shard_map/ppermute | solution.py:52
  15.9 1.1 collective-permute-done.2
  17.0 2.1 %collective-permute-done.1 = bf16[2,4,6144]{2,1,0:T(4,128)(2,1)S(1)} collective-permute-done((bf16[2,4,6144]{2,1,0:T(4,128)(2,1)S(1)}, bf16[2,4,6144]{2,1,0:T(4,128)(2,1)S(1)}, u32[]{:S(2)}, u32[]{:S(2)}) %collective-permute-start.1) | collective-permute-done | bytes 98336 | tf_op jit(solution)/shard_map/ppermute | solution.py:52
  20.0 2.1 %collective-permute-start.11 = (bf16[2,32,2048]{2,1,0:T(8,128)(2,1)S(1)}, bf16[2,32,2048]{2,1,0:T(8,128)(2,1)S(1)}, u32[]{:S(2)}, u32[]{:S(2)}) collective-permute-start(bf16[2,32,2048]{2,1,0:T(8,128)(2,1)S(1)} %get-tuple-element.67.first), channel_id=1, source_target_pairs={{0,6},{1,7},{2,4},{3,5},{4,2},{5,3},{6,0},{7,1},{8,14},{9,15},{10,... | collective-permute-start | bytes 786440 | tf_op jit(solution)/shard_map/ppermute | solution.py:52
  22.1 1.4 %collective-permute-start.13 = (bf16[2,32,2048]{2,1,0:T(8,128)(2,1)S(1)}, bf16[2,32,2048]{2,1,0:T(8,128)(2,1)S(1)}, u32[]{:S(2)}, u32[]{:S(2)}) collective-permute-start(bf16[2,32,2048]{2,1,0:T(8,128)(2,1)S(1)} %get-tuple-element.66.first), channel_id=1, source_target_pairs={{0,33},{1,32},{2,35},{3,34},{4,37},{5,36},{6,39},{7,38},{8,41},{9,... | collective-permute-start | bytes 786440 | tf_op jit(solution)/shard_map/ppermute | solution.py:52
  23.5 4.0 %collective-permute-start.8 = (bf16[2,32,2048]{2,1,0:T(8,128)(2,1)S(1)}, bf16[2,32,2048]{2,1,0:T(8,128)(2,1)S(1)}, u32[]{:S(2)}, u32[]{:S(2)}) collective-permute-start(bf16[2,32,2048]{2,1,0:T(8,128)(2,1)S(1)} %get-tuple-element.68.first), channel_id=1, source_target_pairs={{0,24},{1,25},{2,26},{3,27},{4,28},{5,29},{6,30},{7,31},{8,16},{9,... | collective-permute-start | bytes 786440 | tf_op jit(solution)/shard_map/ppermute | solution.py:52
  28.2 1.9 %collective-permute-start.12 = (bf16[2,64,2048]{2,1,0:T(8,128)(2,1)S(1)}, bf16[2,64,2048]{2,1,0:T(8,128)(2,1)S(1)}, u32[]{:S(2)}, u32[]{:S(2)}) collective-permute-start(bf16[2,64,2048]{2,1,0:T(8,128)(2,1)S(1)} %shard_map.104.first), channel_id=1, source_target_pairs={{0,33},{1,32},{2,35},{3,34},{4,37},{5,36},{6,39},{7,38},{8,41},{9,... | collective-permute-start | bytes 1572872 | tf_op jit(solution)/shard_map/ppermute | solution.py:52
  30.2 3.4 %collective-permute-start.14 = (bf16[2,64,2048]{2,1,0:T(8,128)(2,1)S(1)}, bf16[2,64,2048]{2,1,0:T(8,128)(2,1)S(1)}, u32[]{:S(2)}, u32[]{:S(2)}) collective-permute-start(bf16[2,64,2048]{2,1,0:T(8,128)(2,1)S(1)} %shard_map.106.first), channel_id=1, source_target_pairs={{0,24},{1,25},{2,26},{3,27},{4,28},{5,29},{6,30},{7,31},{8,16},{9,... | collective-permute-start | bytes 1572872 | tf_op jit(solution)/shard_map/ppermute | solution.py:52
  33.6 1.9 %collective-permute-start.9 = (bf16[2,64,2048]{2,1,0:T(8,128)(2,1)S(1)}, bf16[2,64,2048]{2,1,0:T(8,128)(2,1)S(1)}, u32[]{:S(2)}, u32[]{:S(2)}) collective-permute-start(bf16[2,64,2048]{2,1,0:T(8,128)(2,1)S(1)} %shard_map.102.first), channel_id=1, source_target_pairs={{0,6},{1,7},{2,4},{3,5},{4,2},{5,3},{6,0},{7,1},{8,14},{9,15},{10,... | collective-permute-start | bytes 1572872 | tf_op jit(solution)/shard_map/ppermute | solution.py:52
  35.5 3.5 %shard_map.105 = (bf16[224,6144]{1,0:T(8,128)(2,1)S(1)}, bf16[224,6144]{1,0:T(8,128)(2,1)S(1)}, bf16[224,6144]{1,0:T(8,128)(2,1)S(1)}) custom-call(bf16[224,12288]{1,0:T(8,128)(2,1)} %refs_0_.1, bf16[224,12288]{1,0:T(8,128)(2,1)} %refs_1_.1, bf16[224,12288]{1,0:T(8,128)(2,1)} %refs_2_.2), custom_call_target="tpu_custom_call" | custom-call | bytes 16777216 | tf_op jit(solution)/shard_map/pallas_call | solution.py:73
  39.0 2.1 %collective-permute-start.16 = (bf16[2,128,2048]{2,1,0:T(8,128)(2,1)S(1)}, bf16[2,128,2048]{2,1,0:T(8,128)(2,1)S(1)}, u32[]{:S(2)}, u32[]{:S(2)}) collective-permute-start(bf16[2,128,2048]{2,1,0:T(8,128)(2,1)S(1)} %shard_map.108.refs_0_), channel_id=1, source_target_pairs={{0,24},{1,25},{2,26},{3,27},{4,28},{5,29},{6,30},{7,31},{8,16},{9,... | collective-permute-start | bytes 3145736 | tf_op jit(solution)/shard_map/ppermute | solution.py:52
  41.2 1.7 %collective-permute-start.15 = (bf16[2,128,2048]{2,1,0:T(8,128)(2,1)S(1)}, bf16[2,128,2048]{2,1,0:T(8,128)(2,1)S(1)}, u32[]{:S(2)}, u32[]{:S(2)}) collective-permute-start(bf16[2,128,2048]{2,1,0:T(8,128)(2,1)S(1)} %shard_map.107.refs_1_.refs_2_), channel_id=1, source_target_pairs={{0,6},{1,7},{2,4},{3,5},{4,2},{5,3},{6,0},{7,1},{8,14},{9,15},{10,... | collective-permute-start | bytes 3145736 | tf_op jit(solution)/shard_map/ppermute | solution.py:52
  42.9 1.2 %collective-permute-done.9.second = bf16[2,64,2048]{2,1,0:T(8,128)(2,1)S(1)} collective-permute-done((bf16[2,64,2048]{2,1,0:T(8,128)(2,1)S(1)}, bf16[2,64,2048]{2,1,0:T(8,128)(2,1)S(1)}, u32[]{:S(2)}, u32[]{:S(2)}) %collective-permute-start.9) | collective-permute-done | bytes 524320 | tf_op jit(solution)/shard_map/ppermute | solution.py:52
  44.1 1.9 %collective-permute-start.10 = (bf16[2,128,2048]{2,1,0:T(8,128)(2,1)S(1)}, bf16[2,128,2048]{2,1,0:T(8,128)(2,1)S(1)}, u32[]{:S(2)}, u32[]{:S(2)}) collective-permute-start(bf16[2,128,2048]{2,1,0:T(8,128)(2,1)S(1)} %shard_map.103.refs_2_.refs_4_), channel_id=1, source_target_pairs={{0,33},{1,32},{2,35},{3,34},{4,37},{5,36},{6,39},{7,38},{8,41},{9,... | collective-permute-start | bytes 3145736 | tf_op jit(solution)/shard_map/ppermute | solution.py:52
  46.1 2.9 %shard_map.109.refs_4_ = f32[256,768]{1,0:T(8,128)S(1)} custom-call(bf16[2,128,2048]{2,1,0:T(8,128)(2,1)S(1)} %shard_map.108.refs_0_, bf16[2,128,2048]{2,1,0:T(8,128)(2,1)S(1)} %shard_map.107.refs_1_.refs_2_, bf16[2,128,2048]{2,1,0:T(8,128)(2,1)S(1)} %shard_map.103.refs_2_.refs_4_, bf16[224,6144]{1,0:T(8,128)(2,1)S(1)} %get-tuple-element.36.refs_3_.refs_1_.refs_4_.gate, ...), custom_call_target="tpu_custom_call" | custom-call | flops 1056964608 | bytes 14680064 | tf_op jit(solution)/shard_map/pallas_call | solution.py:73
  49.0 6.1 %collective-permute-done.16.refs_0_.refs_1_ = bf16[2,128,2048]{2,1,0:T(8,128)(2,1)S(1)} collective-permute-done((bf16[2,128,2048]{2,1,0:T(8,128)(2,1)S(1)}, bf16[2,128,2048]{2,1,0:T(8,128)(2,1)S(1)}, u32[]{:S(2)}, u32[]{:S(2)}) %collective-permute-start.16) | collective-permute-done | bytes 1048608 | tf_op jit(solution)/shard_map/ppermute | solution.py:52
  55.1 1.1 shard_map.110.refs_4_
  56.2 1.1 %collective-permute-done.15.refs_0_.refs_3_ = bf16[2,128,2048]{2,1,0:T(8,128)(2,1)S(1)} collective-permute-done((bf16[2,128,2048]{2,1,0:T(8,128)(2,1)S(1)}, bf16[2,128,2048]{2,1,0:T(8,128)(2,1)S(1)}, u32[]{:S(2)}, u32[]{:S(2)}) %collective-permute-start.15) | collective-permute-done | bytes 1048608 | tf_op jit(solution)/shard_map/ppermute | solution.py:52
  57.3 1.1 shard_map.111.refs_4_
  58.4 1.9 %collective-permute-done.10.refs_0_.refs_5_ = bf16[2,128,2048]{2,1,0:T(8,128)(2,1)S(1)} collective-permute-done((bf16[2,128,2048]{2,1,0:T(8,128)(2,1)S(1)}, bf16[2,128,2048]{2,1,0:T(8,128)(2,1)S(1)}, u32[]{:S(2)}, u32[]{:S(2)}) %collective-permute-start.10) | collective-permute-done | bytes 1048608 | tf_op jit(solution)/shard_map/ppermute | solution.py:52
  60.2 1.1 shard_map.112.refs_0_
  61.4 2.3 %collective-permute-done.17.refs_1_ = f32[256,768]{1,0:T(8,128)S(1)} collective-permute-done((f32[256,768]{1,0:T(8,128)S(1)}, f32[256,768]{1,0:T(8,128)S(1)}, u32[]{:S(2)}, u32[]{:S(2)}) %collective-permute-start.17) | collective-permute-done | bytes 786464 | tf_op jit(solution)/shard_map/ppermute | solution.py:52
  63.7 1.9 %shard_map.113 = (bf16[128,2048]{1,0:T(8,128)(2,1)S(1)}, bf16[128,2048]{1,0:T(8,128)(2,1)S(1)}, bf16[128,2048]{1,0:T(8,128)(2,1)S(1)}, bf16[256,224]{1,0:T(8,128...) custom-call(f32[256,768]{1,0:T(8,128)S(1)} %shard_map.112.refs_0_, ...), custom_call_target="tpu_custom_call" | custom-call | flops 704643072 | bytes 8388608 | tf_op jit(solution)/shard_map/pallas_call | solution.py:73
  65.7 2.1 %collective-permute-start.21 = (bf16[128,2048]{1,0:T(8,128)(2,1)S(1)}, bf16[128,2048]{1,0:T(8,128)(2,1)S(1)}, u32[]{:S(2)}, u32[]{:S(2)}) collective-permute-start(bf16[128,2048]{1,0:T(8,128)(2,1)S(1)} %get-tuple-element.45), channel_id=1, source_target_pairs={{0,6},{1,7},{2,4},{3,5},{4,2},{5,3},{6,0},{7,1},{8,14},{9,15},{10,... | collective-permute-start | bytes 1572872 | tf_op jit(solution)/shard_map/ppermute | solution.py:52
  67.8 1.5 %collective-permute-start.24 = (bf16[128,2048]{1,0:T(8,128)(2,1)S(1)}, bf16[128,2048]{1,0:T(8,128)(2,1)S(1)}, u32[]{:S(2)}, u32[]{:S(2)}) collective-permute-start(bf16[128,2048]{1,0:T(8,128)(2,1)S(1)} %get-tuple-element.47), channel_id=1, source_target_pairs={{0,33},{1,32},{2,35},{3,34},{4,37},{5,36},{6,39},{7,38},{8,41},{9,... | collective-permute-start | bytes 1572872 | tf_op jit(solution)/shard_map/ppermute | solution.py:52
  69.3 1.0 shard_map.114
  70.2 4.6 %collective-permute-done.18 = bf16[128,2048]{1,0:T(8,128)(2,1)S(1)} collective-permute-done((bf16[128,2048]{1,0:T(8,128)(2,1)S(1)}, bf16[128,2048]{1,0:T(8,128)(2,1)S(1)}, u32[]{:S(2)}, u32[]{:S(2)}) %collective-permute-start.18) | collective-permute-done | bytes 524320 | tf_op jit(solution)/shard_map/ppermute | solution.py:52
  75.0 1.9 %collective-permute-start.19 = (bf16[64,2048]{1,0:T(8,128)(2,1)S(1)}, bf16[64,2048]{1,0:T(8,128)(2,1)S(1)}, u32[]{:S(2)}, u32[]{:S(2)}) collective-permute-start(bf16[64,2048]{1,0:T(8,128)(2,1)S(1)} %slice.174), channel_id=1, source_target_pairs={{0,33},{1,32},{2,35},{3,34},{4,37},{5,36},{6,39},{7,38},{8,41},{9,... | collective-permute-start | bytes 786440 | tf_op jit(solution)/shard_map/ppermute | solution.py:52
  77.1 1.2 %collective-permute-start.22 = (bf16[64,2048]{1,0:T(8,128)(2,1)S(1)}, bf16[64,2048]{1,0:T(8,128)(2,1)S(1)}, u32[]{:S(2)}, u32[]{:S(2)}) collective-permute-start(bf16[64,2048]{1,0:T(8,128)(2,1)S(1)} %slice.173), channel_id=1, source_target_pairs={{0,8},{1,9},{2,10},{3,11},{4,12},{5,13},{6,14},{7,15},{8,0},{9,1},... | collective-permute-start | bytes 786440 | tf_op jit(solution)/shard_map/ppermute | solution.py:52
  78.5 1.9 %collective-permute-start.25 = (bf16[64,2048]{1,0:T(8,128)(2,1)S(1)}, bf16[64,2048]{1,0:T(8,128)(2,1)S(1)}, u32[]{:S(2)}, u32[]{:S(2)}) collective-permute-start(bf16[64,2048]{1,0:T(8,128)(2,1)S(1)} %slice.172), channel_id=1, source_target_pairs={{0,6},{1,7},{2,4},{3,5},{4,2},{5,3},{6,0},{7,1},{8,14},{9,15},{10,... | collective-permute-start | bytes 786440 | tf_op jit(solution)/shard_map/ppermute | solution.py:52
  80.4 2.3 %collective-permute-done.19 = bf16[64,2048]{1,0:T(8,128)(2,1)S(1)} collective-permute-done((bf16[64,2048]{1,0:T(8,128)(2,1)S(1)}, bf16[64,2048]{1,0:T(8,128)(2,1)S(1)}, u32[]{:S(2)}, u32[]{:S(2)}) %collective-permute-start.19) | collective-permute-done | bytes 262176 | tf_op jit(solution)/shard_map/ppermute | solution.py:52
  82.8 1.9 %collective-permute-start.20 = (bf16[32,2048]{1,0:T(8,128)(2,1)S(1)}, bf16[32,2048]{1,0:T(8,128)(2,1)S(1)}, u32[]{:S(2)}, u32[]{:S(2)}) collective-permute-start(bf16[32,2048]{1,0:T(8,128)(2,1)S(1)} %slice.178), channel_id=1, source_target_pairs={{0,6},{1,7},{2,4},{3,5},{4,2},{5,3},{6,0},{7,1},{8,14},{9,15},{10,... | collective-permute-start | bytes 393224 | tf_op jit(solution)/shard_map/ppermute | solution.py:52
  84.7 1.6 %collective-permute-start.23 = (bf16[32,2048]{1,0:T(8,128)(2,1)S(1)}, bf16[32,2048]{1,0:T(8,128)(2,1)S(1)}, u32[]{:S(2)}, u32[]{:S(2)}) collective-permute-start(bf16[32,2048]{1,0:T(8,128)(2,1)S(1)} %slice.177), channel_id=1, source_target_pairs={{0,33},{1,32},{2,35},{3,34},{4,37},{5,36},{6,39},{7,38},{8,41},{9,... | collective-permute-start | bytes 393224 | tf_op jit(solution)/shard_map/ppermute | solution.py:52
  86.4 1.5 %collective-permute-start.26 = (bf16[32,2048]{1,0:T(8,128)(2,1)S(1)}, bf16[32,2048]{1,0:T(8,128)(2,1)S(1)}, u32[]{:S(2)}, u32[]{:S(2)}) collective-permute-start(bf16[32,2048]{1,0:T(8,128)(2,1)S(1)} %slice.176), channel_id=1, source_target_pairs={{0,8},{1,9},{2,10},{3,11},{4,12},{5,13},{6,14},{7,15},{8,0},{9,1},... | collective-permute-start | bytes 393224 | tf_op jit(solution)/shard_map/ppermute | solution.py:52
  87.9 1.1 %collective-permute-done.20 = bf16[32,2048]{1,0:T(8,128)(2,1)S(1)} collective-permute-done((bf16[32,2048]{1,0:T(8,128)(2,1)S(1)}, bf16[32,2048]{1,0:T(8,128)(2,1)S(1)}, u32[]{:S(2)}, u32[]{:S(2)}) %collective-permute-start.20) | collective-permute-done | bytes 131104 | tf_op jit(solution)/shard_map/ppermute | solution.py:52
  89.1 1.9 %collective-permute-done.23 = bf16[32,2048]{1,0:T(8,128)(2,1)S(1)} collective-permute-done((bf16[32,2048]{1,0:T(8,128)(2,1)S(1)}, bf16[32,2048]{1,0:T(8,128)(2,1)S(1)}, u32[]{:S(2)}, u32[]{:S(2)}) %collective-permute-start.23) | collective-permute-done | bytes 131104 | tf_op jit(solution)/shard_map/ppermute | solution.py:52
  91.5 1.8 %collective-permute-start.27 = (bf16[16,6144]{1,0:T(8,128)(2,1)S(1)}, bf16[16,6144]{1,0:T(8,128)(2,1)S(1)}, u32[]{:S(2)}, u32[]{:S(2)}) collective-permute-start(bf16[16,6144]{1,0:T(8,128)(2,1)S(1)} %slice.175), channel_id=1, source_target_pairs={{0,24},{1,25},{2,26},{3,27},{4,28},{5,29},{6,30},{7,31},{8,16},{9,... | collective-permute-start | bytes 589832 | tf_op jit(solution)/shard_map/ppermute | solution.py:52
  93.3 3.8 %shard_map.115 = (bf16[224,6144]{1,0:T(8,128)(2,1)}, bf16[224,6144]{1,0:T(8,128)(2,1)}, bf16[224,6144]{1,0:T(8,128)(2,1)}) custom-call(bf16[2,128,2048]{2,1,0:T(8,128)(2,1)S(1)} %shard_map.108.refs_0_, bf16[2,128,2048]{2,1,0:T(8,128)(2,1)S(1)} %collective-permute-done.16.refs_0_.refs_1_, bf16[2,128,2048]{2,1,0:T(8,128)(2,1)S(1)} %shard_map.107.refs_1_.refs_2_, ...), custom_call_target="tpu_custom_call" | custom-call | flops 2113929216 | bytes 25165824 | tf_op jit(solution)/shard_map/pallas_call | solution.py:73
  97.1 1.4 %collective-permute-done.27 = bf16[16,6144]{1,0:T(8,128)(2,1)S(1)} collective-permute-done((bf16[16,6144]{1,0:T(8,128)(2,1)S(1)}, bf16[16,6144]{1,0:T(8,128)(2,1)S(1)}, u32[]{:S(2)}, u32[]{:S(2)}) %collective-permute-start.27) | collective-permute-done | bytes 196640 | tf_op jit(solution)/shard_map/ppermute | solution.py:52
  98.8 3.4 %collective-permute-start.29 = (bf16[4,6144]{1,0:T(4,128)(2,1)S(1)}, bf16[4,6144]{1,0:T(4,128)(2,1)S(1)}, u32[]{:S(2)}, u32[]{:S(2)}) collective-permute-start(bf16[4,6144]{1,0:T(4,128)(2,1)S(1)} %get-tuple-element.71), channel_id=1, source_target_pairs={{0,32},{1,33},{2,34},{3,35},{4,36},{5,37},{6,38},{7,39},{8,40},{9,... | collective-permute-start | bytes 147464 | tf_op jit(solution)/shard_map/ppermute | solution.py:52
  102.8 1.0 collective-permute-done.30
  104.5 1.2 %collective-permute-done.31 = bf16[2,6144]{1,0:T(2,128)(2,1)S(1)} collective-permute-done((bf16[2,6144]{1,0:T(2,128)(2,1)S(1)}, bf16[2,6144]{1,0:T(2,128)(2,1)S(1)}, u32[]{:S(2)}, u32[]{:S(2)}) %collective-permute-start.31) | collective-permute-done | bytes 24608 | tf_op jit(solution)/shard_map/ppermute | solution.py:52
  (62 shorter events, 7.8 us)
Async XLA Ops:
  1.5 1.3 %collective-permute-start = (bf16[2,2,6144]{2,1,0:T(2,128)(2,1)S(1)}, bf16[2,2,6144]{2,1,0:T(2,128)(2,1)S(1)}, u32[]{:S(2)}, u32[]{:S(2)}) collective-permute-start(bf16[2,2,6144]{2,1,0:T(2,128)(2,1)S(1)} %get-tuple-element.64), channel_id=1, source_target_pairs={{0,64},{1,65},{2,66},{3,67},{4,68},{5,69},{6,70},{7,71},{8,72},{9,... | collective-permute-start | bytes 147464 | tf_op jit(solution)/shard_map/ppermute | solution.py:52
  3.8 8.5 %collective-permute-start.7 = (bf16[2,4,6144]{2,1,0:T(4,128)(2,1)S(1)}, bf16[2,4,6144]{2,1,0:T(4,128)(2,1)S(1)}, u32[]{:S(2)}, u32[]{:S(2)}) collective-permute-start(bf16[2,4,6144]{2,1,0:T(4,128)(2,1)S(1)} %pad_maximum_fusion.1), channel_id=1, source_target_pairs={{0,42},{1,43},{2,40},{3,41},{4,46},{5,47},{6,44},{7,45},{8,34},{9,... | collective-permute-start | bytes 294920 | tf_op jit(solution)/shard_map/ppermute | solution.py:52
  7.8 6.7 %collective-permute-start.6 = (bf16[2,4,6144]{2,1,0:T(4,128)(2,1)S(1)}, bf16[2,4,6144]{2,1,0:T(4,128)(2,1)S(1)}, u32[]{:S(2)}, u32[]{:S(2)}) collective-permute-start(bf16[2,4,6144]{2,1,0:T(4,128)(2,1)S(1)} %pad_maximum_fusion.1), channel_id=1, source_target_pairs={{0,40},{1,41},{2,42},{3,43},{4,44},{5,45},{6,46},{7,47},{8,32},{9,... | collective-permute-start | bytes 294920 | tf_op jit(solution)/shard_map/ppermute | solution.py:52
  7.9 7.0 %collective-permute-start.5 = (bf16[2,4,6144]{2,1,0:T(4,128)(2,1)S(1)}, bf16[2,4,6144]{2,1,0:T(4,128)(2,1)S(1)}, u32[]{:S(2)}, u32[]{:S(2)}) collective-permute-start(bf16[2,4,6144]{2,1,0:T(4,128)(2,1)S(1)} %pad_maximum_fusion.1), channel_id=1, source_target_pairs={{0,10},{1,11},{2,8},{3,9},{4,14},{5,15},{6,12},{7,13},{8,2},{9,3},... | collective-permute-start | bytes 294920 | tf_op jit(solution)/shard_map/ppermute | solution.py:52
  9.7 5.7 %collective-permute-start.4 = (bf16[2,4,6144]{2,1,0:T(4,128)(2,1)S(1)}, bf16[2,4,6144]{2,1,0:T(4,128)(2,1)S(1)}, u32[]{:S(2)}, u32[]{:S(2)}) collective-permute-start(bf16[2,4,6144]{2,1,0:T(4,128)(2,1)S(1)} %pad_maximum_fusion.1), channel_id=1, source_target_pairs={{0,8},{1,9},{2,10},{3,11},{4,12},{5,13},{6,14},{7,15},{8,0},{9,1},... | collective-permute-start | bytes 294920 | tf_op jit(solution)/shard_map/ppermute | solution.py:52
  10.0 6.0 %collective-permute-start.3 = (bf16[2,4,6144]{2,1,0:T(4,128)(2,1)S(1)}, bf16[2,4,6144]{2,1,0:T(4,128)(2,1)S(1)}, u32[]{:S(2)}, u32[]{:S(2)}) collective-permute-start(bf16[2,4,6144]{2,1,0:T(4,128)(2,1)S(1)} %pad_maximum_fusion.1), channel_id=1, source_target_pairs={{0,34},{1,35},{2,32},{3,33},{4,38},{5,39},{6,36},{7,37},{8,42},{9,... | collective-permute-start | bytes 294920 | tf_op jit(solution)/shard_map/ppermute | solution.py:52
  12.4 4.6 %collective-permute-start.2 = (bf16[2,4,6144]{2,1,0:T(4,128)(2,1)S(1)}, bf16[2,4,6144]{2,1,0:T(4,128)(2,1)S(1)}, u32[]{:S(2)}, u32[]{:S(2)}) collective-permute-start(bf16[2,4,6144]{2,1,0:T(4,128)(2,1)S(1)} %pad_maximum_fusion.1), channel_id=1, source_target_pairs={{0,32},{1,33},{2,34},{3,35},{4,36},{5,37},{6,38},{7,39},{8,40},{9,... | collective-permute-start | bytes 294920 | tf_op jit(solution)/shard_map/ppermute | solution.py:52
  14.5 4.6 %collective-permute-start.1 = (bf16[2,4,6144]{2,1,0:T(4,128)(2,1)S(1)}, bf16[2,4,6144]{2,1,0:T(4,128)(2,1)S(1)}, u32[]{:S(2)}, u32[]{:S(2)}) collective-permute-start(bf16[2,4,6144]{2,1,0:T(4,128)(2,1)S(1)} %pad_maximum_fusion.1), channel_id=1, source_target_pairs={{0,2},{1,3},{2,0},{3,1},{4,6},{5,7},{6,4},{7,5},{8,10},{9,11},{10,... | collective-permute-start | bytes 294920 | tf_op jit(solution)/shard_map/ppermute | solution.py:52
  20.0 8.2 %collective-permute-start.11 = (bf16[2,32,2048]{2,1,0:T(8,128)(2,1)S(1)}, bf16[2,32,2048]{2,1,0:T(8,128)(2,1)S(1)}, u32[]{:S(2)}, u32[]{:S(2)}) collective-permute-start(bf16[2,32,2048]{2,1,0:T(8,128)(2,1)S(1)} %get-tuple-element.67.first), channel_id=1, source_target_pairs={{0,6},{1,7},{2,4},{3,5},{4,2},{5,3},{6,0},{7,1},{8,14},{9,15},{10,... | collective-permute-start | bytes 786440 | tf_op jit(solution)/shard_map/ppermute | solution.py:52
  22.1 8.0 %collective-permute-start.13 = (bf16[2,32,2048]{2,1,0:T(8,128)(2,1)S(1)}, bf16[2,32,2048]{2,1,0:T(8,128)(2,1)S(1)}, u32[]{:S(2)}, u32[]{:S(2)}) collective-permute-start(bf16[2,32,2048]{2,1,0:T(8,128)(2,1)S(1)} %get-tuple-element.66.first), channel_id=1, source_target_pairs={{0,33},{1,32},{2,35},{3,34},{4,37},{5,36},{6,39},{7,38},{8,41},{9,... | collective-permute-start | bytes 786440 | tf_op jit(solution)/shard_map/ppermute | solution.py:52
  23.5 10.1 %collective-permute-start.8 = (bf16[2,32,2048]{2,1,0:T(8,128)(2,1)S(1)}, bf16[2,32,2048]{2,1,0:T(8,128)(2,1)S(1)}, u32[]{:S(2)}, u32[]{:S(2)}) collective-permute-start(bf16[2,32,2048]{2,1,0:T(8,128)(2,1)S(1)} %get-tuple-element.68.first), channel_id=1, source_target_pairs={{0,24},{1,25},{2,26},{3,27},{4,28},{5,29},{6,30},{7,31},{8,16},{9,... | collective-permute-start | bytes 786440 | tf_op jit(solution)/shard_map/ppermute | solution.py:52
  28.2 10.7 %collective-permute-start.12 = (bf16[2,64,2048]{2,1,0:T(8,128)(2,1)S(1)}, bf16[2,64,2048]{2,1,0:T(8,128)(2,1)S(1)}, u32[]{:S(2)}, u32[]{:S(2)}) collective-permute-start(bf16[2,64,2048]{2,1,0:T(8,128)(2,1)S(1)} %shard_map.104.first), channel_id=1, source_target_pairs={{0,33},{1,32},{2,35},{3,34},{4,37},{5,36},{6,39},{7,38},{8,41},{9,... | collective-permute-start | bytes 1572872 | tf_op jit(solution)/shard_map/ppermute | solution.py:52
  30.2 10.9 %collective-permute-start.14 = (bf16[2,64,2048]{2,1,0:T(8,128)(2,1)S(1)}, bf16[2,64,2048]{2,1,0:T(8,128)(2,1)S(1)}, u32[]{:S(2)}, u32[]{:S(2)}) collective-permute-start(bf16[2,64,2048]{2,1,0:T(8,128)(2,1)S(1)} %shard_map.106.first), channel_id=1, source_target_pairs={{0,24},{1,25},{2,26},{3,27},{4,28},{5,29},{6,30},{7,31},{8,16},{9,... | collective-permute-start | bytes 1572872 | tf_op jit(solution)/shard_map/ppermute | solution.py:52
  33.6 10.5 %collective-permute-start.9 = (bf16[2,64,2048]{2,1,0:T(8,128)(2,1)S(1)}, bf16[2,64,2048]{2,1,0:T(8,128)(2,1)S(1)}, u32[]{:S(2)}, u32[]{:S(2)}) collective-permute-start(bf16[2,64,2048]{2,1,0:T(8,128)(2,1)S(1)} %shard_map.102.first), channel_id=1, source_target_pairs={{0,6},{1,7},{2,4},{3,5},{4,2},{5,3},{6,0},{7,1},{8,14},{9,15},{10,... | collective-permute-start | bytes 1572872 | tf_op jit(solution)/shard_map/ppermute | solution.py:52
  39.0 16.1 %collective-permute-start.16 = (bf16[2,128,2048]{2,1,0:T(8,128)(2,1)S(1)}, bf16[2,128,2048]{2,1,0:T(8,128)(2,1)S(1)}, u32[]{:S(2)}, u32[]{:S(2)}) collective-permute-start(bf16[2,128,2048]{2,1,0:T(8,128)(2,1)S(1)} %shard_map.108.refs_0_), channel_id=1, source_target_pairs={{0,24},{1,25},{2,26},{3,27},{4,28},{5,29},{6,30},{7,31},{8,16},{9,... | collective-permute-start | bytes 3145736 | tf_op jit(solution)/shard_map/ppermute | solution.py:52
  41.2 16.1 %collective-permute-start.15 = (bf16[2,128,2048]{2,1,0:T(8,128)(2,1)S(1)}, bf16[2,128,2048]{2,1,0:T(8,128)(2,1)S(1)}, u32[]{:S(2)}, u32[]{:S(2)}) collective-permute-start(bf16[2,128,2048]{2,1,0:T(8,128)(2,1)S(1)} %shard_map.107.refs_1_.refs_2_), channel_id=1, source_target_pairs={{0,6},{1,7},{2,4},{3,5},{4,2},{5,3},{6,0},{7,1},{8,14},{9,15},{10,... | collective-permute-start | bytes 3145736 | tf_op jit(solution)/shard_map/ppermute | solution.py:52
  44.1 16.1 %collective-permute-start.10 = (bf16[2,128,2048]{2,1,0:T(8,128)(2,1)S(1)}, bf16[2,128,2048]{2,1,0:T(8,128)(2,1)S(1)}, u32[]{:S(2)}, u32[]{:S(2)}) collective-permute-start(bf16[2,128,2048]{2,1,0:T(8,128)(2,1)S(1)} %shard_map.103.refs_2_.refs_4_), channel_id=1, source_target_pairs={{0,33},{1,32},{2,35},{3,34},{4,37},{5,36},{6,39},{7,38},{8,41},{9,... | collective-permute-start | bytes 3145736 | tf_op jit(solution)/shard_map/ppermute | solution.py:52
  58.3 5.3 %copy-start = (bf16[256,256]{1,0:T(8,128)(2,1)S(1)}, bf16[256,256]{1,0:T(8,128)(2,1)}, u32[]{:S(2)}) copy-start(bf16[256,256]{1,0:T(8,128)(2,1)} %constant.13.clone.refs_3_) | copy-start | bytes 393220
  58.4 5.3 %copy-start.1 = (bf16[256,256]{1,0:T(8,128)(2,1)S(1)}, bf16[256,256]{1,0:T(8,128)(2,1)}, u32[]{:S(2)}) copy-start(bf16[256,256]{1,0:T(8,128)(2,1)} %constant.12.clone.refs_2_) | copy-start | bytes 393220
  61.3 2.4 %collective-permute-start.17 = (f32[256,768]{1,0:T(8,128)S(1)}, f32[256,768]{1,0:T(8,128)S(1)}, u32[]{:S(2)}, u32[]{:S(2)}) collective-permute-start(f32[256,768]{1,0:T(8,128)S(1)} %shard_map.112.refs_0_), channel_id=1, source_target_pairs={{0,64},{1,65},{2,66},{3,67},{4,68},{5,69},{6,70},{7,71},{8,72},{9,... | collective-permute-start | bytes 2359304 | tf_op jit(solution)/shard_map/ppermute | solution.py:52
  65.6 9.3 %collective-permute-start.18 = (bf16[128,2048]{1,0:T(8,128)(2,1)S(1)}, bf16[128,2048]{1,0:T(8,128)(2,1)S(1)}, u32[]{:S(2)}, u32[]{:S(2)}) collective-permute-start(bf16[128,2048]{1,0:T(8,128)(2,1)S(1)} %get-tuple-element.43), channel_id=1, source_target_pairs={{0,8},{1,9},{2,10},{3,11},{4,12},{5,13},{6,14},{7,15},{8,0},{9,1},... | collective-permute-start | bytes 1572872 | tf_op jit(solution)/shard_map/ppermute | solution.py:52
  65.7 11.3 %collective-permute-start.21 = (bf16[128,2048]{1,0:T(8,128)(2,1)S(1)}, bf16[128,2048]{1,0:T(8,128)(2,1)S(1)}, u32[]{:S(2)}, u32[]{:S(2)}) collective-permute-start(bf16[128,2048]{1,0:T(8,128)(2,1)S(1)} %get-tuple-element.45), channel_id=1, source_target_pairs={{0,6},{1,7},{2,4},{3,5},{4,2},{5,3},{6,0},{7,1},{8,14},{9,15},{10,... | collective-permute-start | bytes 1572872 | tf_op jit(solution)/shard_map/ppermute | solution.py:52
  67.8 10.6 %collective-permute-start.24 = (bf16[128,2048]{1,0:T(8,128)(2,1)S(1)}, bf16[128,2048]{1,0:T(8,128)(2,1)S(1)}, u32[]{:S(2)}, u32[]{:S(2)}) collective-permute-start(bf16[128,2048]{1,0:T(8,128)(2,1)S(1)} %get-tuple-element.47), channel_id=1, source_target_pairs={{0,33},{1,32},{2,35},{3,34},{4,37},{5,36},{6,39},{7,38},{8,41},{9,... | collective-permute-start | bytes 1572872 | tf_op jit(solution)/shard_map/ppermute | solution.py:52
  75.0 7.7 %collective-permute-start.19 = (bf16[64,2048]{1,0:T(8,128)(2,1)S(1)}, bf16[64,2048]{1,0:T(8,128)(2,1)S(1)}, u32[]{:S(2)}, u32[]{:S(2)}) collective-permute-start(bf16[64,2048]{1,0:T(8,128)(2,1)S(1)} %slice.174), channel_id=1, source_target_pairs={{0,33},{1,32},{2,35},{3,34},{4,37},{5,36},{6,39},{7,38},{8,41},{9,... | collective-permute-start | bytes 786440 | tf_op jit(solution)/shard_map/ppermute | solution.py:52
  77.1 7.5 %collective-permute-start.22 = (bf16[64,2048]{1,0:T(8,128)(2,1)S(1)}, bf16[64,2048]{1,0:T(8,128)(2,1)S(1)}, u32[]{:S(2)}, u32[]{:S(2)}) collective-permute-start(bf16[64,2048]{1,0:T(8,128)(2,1)S(1)} %slice.173), channel_id=1, source_target_pairs={{0,8},{1,9},{2,10},{3,11},{4,12},{5,13},{6,14},{7,15},{8,0},{9,1},... | collective-permute-start | bytes 786440 | tf_op jit(solution)/shard_map/ppermute | solution.py:52
  78.5 7.8 %collective-permute-start.25 = (bf16[64,2048]{1,0:T(8,128)(2,1)S(1)}, bf16[64,2048]{1,0:T(8,128)(2,1)S(1)}, u32[]{:S(2)}, u32[]{:S(2)}) collective-permute-start(bf16[64,2048]{1,0:T(8,128)(2,1)S(1)} %slice.172), channel_id=1, source_target_pairs={{0,6},{1,7},{2,4},{3,5},{4,2},{5,3},{6,0},{7,1},{8,14},{9,15},{10,... | collective-permute-start | bytes 786440 | tf_op jit(solution)/shard_map/ppermute | solution.py:52
  82.8 6.3 %collective-permute-start.20 = (bf16[32,2048]{1,0:T(8,128)(2,1)S(1)}, bf16[32,2048]{1,0:T(8,128)(2,1)S(1)}, u32[]{:S(2)}, u32[]{:S(2)}) collective-permute-start(bf16[32,2048]{1,0:T(8,128)(2,1)S(1)} %slice.178), channel_id=1, source_target_pairs={{0,6},{1,7},{2,4},{3,5},{4,2},{5,3},{6,0},{7,1},{8,14},{9,15},{10,... | collective-permute-start | bytes 393224 | tf_op jit(solution)/shard_map/ppermute | solution.py:52
  84.7 6.3 %collective-permute-start.23 = (bf16[32,2048]{1,0:T(8,128)(2,1)S(1)}, bf16[32,2048]{1,0:T(8,128)(2,1)S(1)}, u32[]{:S(2)}, u32[]{:S(2)}) collective-permute-start(bf16[32,2048]{1,0:T(8,128)(2,1)S(1)} %slice.177), channel_id=1, source_target_pairs={{0,33},{1,32},{2,35},{3,34},{4,37},{5,36},{6,39},{7,38},{8,41},{9,... | collective-permute-start | bytes 393224 | tf_op jit(solution)/shard_map/ppermute | solution.py:52
  86.4 5.0 %collective-permute-start.26 = (bf16[32,2048]{1,0:T(8,128)(2,1)S(1)}, bf16[32,2048]{1,0:T(8,128)(2,1)S(1)}, u32[]{:S(2)}, u32[]{:S(2)}) collective-permute-start(bf16[32,2048]{1,0:T(8,128)(2,1)S(1)} %slice.176), channel_id=1, source_target_pairs={{0,8},{1,9},{2,10},{3,11},{4,12},{5,13},{6,14},{7,15},{8,0},{9,1},... | collective-permute-start | bytes 393224 | tf_op jit(solution)/shard_map/ppermute | solution.py:52
  91.5 7.0 %collective-permute-start.27 = (bf16[16,6144]{1,0:T(8,128)(2,1)S(1)}, bf16[16,6144]{1,0:T(8,128)(2,1)S(1)}, u32[]{:S(2)}, u32[]{:S(2)}) collective-permute-start(bf16[16,6144]{1,0:T(8,128)(2,1)S(1)} %slice.175), channel_id=1, source_target_pairs={{0,24},{1,25},{2,26},{3,27},{4,28},{5,29},{6,30},{7,31},{8,16},{9,... | collective-permute-start | bytes 589832 | tf_op jit(solution)/shard_map/ppermute | solution.py:52
  98.6 4.2 %collective-permute-start.28 = (bf16[4,6144]{1,0:T(4,128)(2,1)S(1)}, bf16[4,6144]{1,0:T(4,128)(2,1)S(1)}, u32[]{:S(2)}, u32[]{:S(2)}) collective-permute-start(bf16[4,6144]{1,0:T(4,128)(2,1)S(1)} %get-tuple-element.69), channel_id=1, source_target_pairs={{0,2},{1,3},{2,0},{3,1},{4,6},{5,7},{6,4},{7,5},{8,10},{9,11},{10,... | collective-permute-start | bytes 147464 | tf_op jit(solution)/shard_map/ppermute | solution.py:52
  98.7 5.1 %collective-permute-start.30 = (bf16[4,6144]{1,0:T(4,128)(2,1)S(1)}, bf16[4,6144]{1,0:T(4,128)(2,1)S(1)}, u32[]{:S(2)}, u32[]{:S(2)}) collective-permute-start(bf16[4,6144]{1,0:T(4,128)(2,1)S(1)} %get-tuple-element.70), channel_id=1, source_target_pairs={{0,34},{1,35},{2,32},{3,33},{4,38},{5,39},{6,36},{7,37},{8,42},{9,... | collective-permute-start | bytes 147464 | tf_op jit(solution)/shard_map/ppermute | solution.py:52
  98.8 5.5 %collective-permute-start.29 = (bf16[4,6144]{1,0:T(4,128)(2,1)S(1)}, bf16[4,6144]{1,0:T(4,128)(2,1)S(1)}, u32[]{:S(2)}, u32[]{:S(2)}) collective-permute-start(bf16[4,6144]{1,0:T(4,128)(2,1)S(1)} %get-tuple-element.71), channel_id=1, source_target_pairs={{0,32},{1,33},{2,34},{3,35},{4,36},{5,37},{6,38},{7,39},{8,40},{9,... | collective-permute-start | bytes 147464 | tf_op jit(solution)/shard_map/ppermute | solution.py:52
  104.4 1.3 %collective-permute-start.31 = (bf16[2,6144]{1,0:T(2,128)(2,1)S(1)}, bf16[2,6144]{1,0:T(2,128)(2,1)S(1)}, u32[]{:S(2)}, u32[]{:S(2)}) collective-permute-start(bf16[2,6144]{1,0:T(2,128)(2,1)S(1)} %broadcast_select_fusion.6), channel_id=1, source_target_pairs={{0,64},{1,65},{2,66},{3,67},{4,68},{5,69},{6,70},{7,71},{8,72},{9,... | collective-permute-start | bytes 73736 | tf_op jit(solution)/shard_map/ppermute | solution.py:52

commit v4 on v3

--- a/solution.py
+++ b/solution.py
@@ -60,7 +60,7 @@
     ]
 
 
-def call(kernel, operands, outs, scratch=(), limit=16, flops=0, megabytes=0):
+def call(kernel, operands, outs, scratch=(), limit=16, flops=0, megabytes=0, aliases=None):
     places = [place for place, _ in operands]
     values = [
         pltpu.with_memory_space_constraint(value, pltpu.VMEM if place == "vmem" else pltpu.HBM)
@@ -79,6 +79,7 @@
         in_specs=[spec[place] for place in places],
         out_specs=[spec[place] for place, _, _ in outs],
         scratch_shapes=list(scratch),
+        input_output_aliases=aliases or {},
         compiler_params=pltpu.CompilerParams(vmem_limit_bytes=limit * 2**20),
         cost_estimate=pl.CostEstimate(
             flops=flops, bytes_accessed=megabytes * 2**20, transcendentals=0
@@ -142,8 +143,7 @@
 
 
 def late_kernel(third, k, *refs):
-    piece, weights, acc, out = refs[0], refs[1:4], refs[4], refs[5]
-    out[...] = acc[...]
+    piece, weights, out = refs[0], refs[1:4], refs[5]
     add_products(third, k, 4, piece, weights, out)
 
 
@@ -247,13 +247,11 @@
     half, third = width // 2, width // 6
     micro = inputs.shape[0]
 
-    rows = jnp.stack([inputs[:, 0], cotangent[:, 0]])
-    low, high = rows[:, :, :half], rows[:, :, half:]
-    mine = jnp.where(core == 0, low, high)
-    theirs = send(jnp.where(core == 0, high, low), OTHER_CORE)
-    block = jnp.concatenate(
-        [jnp.where(core == 0, mine, theirs), jnp.where(core == 0, theirs, mine)], axis=1
-    )
+    mine = jnp.stack([inputs[:, 0], cotangent[:, 0]])
+    theirs = jnp.stack([send(inputs, OTHER_CORE)[:, 0], send(cotangent, OTHER_CORE)[:, 0]])
+    first = jnp.concatenate([mine[:, :, :half], theirs[:, :, :half]], axis=1)
+    second = jnp.concatenate([theirs[:, :, half:], mine[:, :, half:]], axis=1)
+    block = jnp.where(core == 0, first, second)
     block = jnp.concatenate(
         [block] + [send(block, neighbour(axes, 0)) for axes in CUBE], axis=1
     )
@@ -288,6 +286,7 @@
             [("vmem", (rows, 3 * LANES), jnp.float32)],
             flops=rows * local_ff * half,
             megabytes=5,
+            aliases={4: 0},
         )
     other = send(part, OTHER_CORE)
     small = ("vmem", (rows, local_ff), jnp.bfloat16)

time: 108 us -> 108 us (level)
    ppermute x32 -> x33, starting transfers between devices: 48.9 us -> 48.1 us  [send(): return lax.ppermute(value, AXES, route)]
    ppermute x32 -> x33, waiting for transfers between devices: 35.6 us -> 36.3 us  [send(): return lax.ppermute(value, AXES, route)]
  transfers between devices with their start and end apart: 32 -> 33, of which waited for: 22 -> 23; matrix products, arithmetic and copies ran while one was open for 1% -> 1% of each run, Pallas kernels for 13% -> 13%
where the time goes in v4:
time: 108 us; the launch traced here: 106 us
  starting transfers between devices  48.1 us (45%)
  waiting for transfers between devices  36.3 us (34%)
  Pallas kernels  16.5 us (15%)
  other arithmetic  3.33 us (3%)
    ppermute x33, starting transfers between devices, send(): return lax.ppermute(value, AXES, route)  48.1 us
    ppermute x33, waiting for transfers between devices, send(): return lax.ppermute(value, AXES, route)  36.3 us
    pallas_call x14, Pallas kernels, call(): pl.pallas_call(kernel, out_shape=[pltpu.VMEM(shape, dtype) if place == 'v...  16.5 us
  transfers between devices with their start and end apart: 33, of which 23 were waited for; matrix products, arithmetic and copies ran while one was open for 1% of the time, Pallas kernels for 13%

profile of v4, /device:TPU:0, one launch (start us, length us, event | category | flops | bytes accessed | tf_op | source)
XLA Modules:
  0.0 106.3 jit_solution(3609206936166414912)
XLA Ops:
  1.2 0.8 fusion.4
  2.4 1.0 fusion.2
  3.4 4.0 %collective-permute-start.8 = (bf16[2,4,6144]{2,1,0:T(4,128)(2,1)S(1)}, bf16[2,4,6144]{2,1,0:T(4,128)(2,1)S(1)}, u32[]{:S(2)}, u32[]{:S(2)}) collective-permute-start(bf16[2,4,6144]{2,1,0:T(4,128)(2,1)S(1)} %fusion.2), channel_id=1, source_target_pairs={{0,42},{1,43},{2,40},{3,41},{4,46},{5,47},{6,44},{7,45},{8,34},{9,... | collective-permute-start | bytes 294920 | tf_op jit(solution)/shard_map/ppermute | solution.py:52
  7.4 1.9 %collective-permute-start.6 = (bf16[2,4,6144]{2,1,0:T(4,128)(2,1)S(1)}, bf16[2,4,6144]{2,1,0:T(4,128)(2,1)S(1)}, u32[]{:S(2)}, u32[]{:S(2)}) collective-permute-start(bf16[2,4,6144]{2,1,0:T(4,128)(2,1)S(1)} %fusion.2), channel_id=1, source_target_pairs={{0,10},{1,11},{2,8},{3,9},{4,14},{5,15},{6,12},{7,13},{8,2},{9,3},... | collective-permute-start | bytes 294920 | tf_op jit(solution)/shard_map/ppermute | solution.py:52
  9.5 2.4 %collective-permute-start.4 = (bf16[2,4,6144]{2,1,0:T(4,128)(2,1)S(1)}, bf16[2,4,6144]{2,1,0:T(4,128)(2,1)S(1)}, u32[]{:S(2)}, u32[]{:S(2)}) collective-permute-start(bf16[2,4,6144]{2,1,0:T(4,128)(2,1)S(1)} %fusion.2), channel_id=1, source_target_pairs={{0,34},{1,35},{2,32},{3,33},{4,38},{5,39},{6,36},{7,37},{8,42},{9,... | collective-permute-start | bytes 294920 | tf_op jit(solution)/shard_map/ppermute | solution.py:52
  12.3 1.7 %collective-permute-done.7 = bf16[2,4,6144]{2,1,0:T(4,128)(2,1)S(1)} collective-permute-done((bf16[2,4,6144]{2,1,0:T(4,128)(2,1)S(1)}, bf16[2,4,6144]{2,1,0:T(4,128)(2,1)S(1)}, u32[]{:S(2)}, u32[]{:S(2)}) %collective-permute-start.7) | collective-permute-done | bytes 98336 | tf_op jit(solution)/shard_map/ppermute | solution.py:52
  15.5 1.1 collective-permute-done.3
  16.5 2.1 %collective-permute-done.2 = bf16[2,4,6144]{2,1,0:T(4,128)(2,1)S(1)} collective-permute-done((bf16[2,4,6144]{2,1,0:T(4,128)(2,1)S(1)}, bf16[2,4,6144]{2,1,0:T(4,128)(2,1)S(1)}, u32[]{:S(2)}, u32[]{:S(2)}) %collective-permute-start.2) | collective-permute-done | bytes 98336 | tf_op jit(solution)/shard_map/ppermute | solution.py:52
  19.5 2.1 %collective-permute-start.12 = (bf16[2,32,2048]{2,1,0:T(8,128)(2,1)S(1)}, bf16[2,32,2048]{2,1,0:T(8,128)(2,1)S(1)}, u32[]{:S(2)}, u32[]{:S(2)}) collective-permute-start(bf16[2,32,2048]{2,1,0:T(8,128)(2,1)S(1)} %get-tuple-element.65.first), channel_id=1, source_target_pairs={{0,6},{1,7},{2,4},{3,5},{4,2},{5,3},{6,0},{7,1},{8,14},{9,15},{10,... | collective-permute-start | bytes 786440 | tf_op jit(solution)/shard_map/ppermute | solution.py:52
  21.6 1.4 %collective-permute-start.14 = (bf16[2,32,2048]{2,1,0:T(8,128)(2,1)S(1)}, bf16[2,32,2048]{2,1,0:T(8,128)(2,1)S(1)}, u32[]{:S(2)}, u32[]{:S(2)}) collective-permute-start(bf16[2,32,2048]{2,1,0:T(8,128)(2,1)S(1)} %get-tuple-element.64.first), channel_id=1, source_target_pairs={{0,33},{1,32},{2,35},{3,34},{4,37},{5,36},{6,39},{7,38},{8,41},{9,... | collective-permute-start | bytes 786440 | tf_op jit(solution)/shard_map/ppermute | solution.py:52
  23.0 4.0 %collective-permute-start.9 = (bf16[2,32,2048]{2,1,0:T(8,128)(2,1)S(1)}, bf16[2,32,2048]{2,1,0:T(8,128)(2,1)S(1)}, u32[]{:S(2)}, u32[]{:S(2)}) collective-permute-start(bf16[2,32,2048]{2,1,0:T(8,128)(2,1)S(1)} %get-tuple-element.66.first), channel_id=1, source_target_pairs={{0,24},{1,25},{2,26},{3,27},{4,28},{5,29},{6,30},{7,31},{8,16},{9,... | collective-permute-start | bytes 786440 | tf_op jit(solution)/shard_map/ppermute | solution.py:52
  27.0 0.9 collective-permute-done.12.second
  27.9 1.7 %collective-permute-start.13 = (bf16[2,64,2048]{2,1,0:T(8,128)(2,1)S(1)}, bf16[2,64,2048]{2,1,0:T(8,128)(2,1)S(1)}, u32[]{:S(2)}, u32[]{:S(2)}) collective-permute-start(bf16[2,64,2048]{2,1,0:T(8,128)(2,1)S(1)} %shard_map.104.first), channel_id=1, source_target_pairs={{0,33},{1,32},{2,35},{3,34},{4,37},{5,36},{6,39},{7,38},{8,41},{9,... | collective-permute-start | bytes 1572872 | tf_op jit(solution)/shard_map/ppermute | solution.py:52
  29.7 3.6 %collective-permute-start.15 = (bf16[2,64,2048]{2,1,0:T(8,128)(2,1)S(1)}, bf16[2,64,2048]{2,1,0:T(8,128)(2,1)S(1)}, u32[]{:S(2)}, u32[]{:S(2)}) collective-permute-start(bf16[2,64,2048]{2,1,0:T(8,128)(2,1)S(1)} %shard_map.106.first), channel_id=1, source_target_pairs={{0,24},{1,25},{2,26},{3,27},{4,28},{5,29},{6,30},{7,31},{8,16},{9,... | collective-permute-start | bytes 1572872 | tf_op jit(solution)/shard_map/ppermute | solution.py:52
  33.3 1.6 %collective-permute-start.10 = (bf16[2,64,2048]{2,1,0:T(8,128)(2,1)S(1)}, bf16[2,64,2048]{2,1,0:T(8,128)(2,1)S(1)}, u32[]{:S(2)}, u32[]{:S(2)}) collective-permute-start(bf16[2,64,2048]{2,1,0:T(8,128)(2,1)S(1)} %shard_map.102.first), channel_id=1, source_target_pairs={{0,6},{1,7},{2,4},{3,5},{4,2},{5,3},{6,0},{7,1},{8,14},{9,15},{10,... | collective-permute-start | bytes 1572872 | tf_op jit(solution)/shard_map/ppermute | solution.py:52
  34.9 3.5 %shard_map.105 = (bf16[224,6144]{1,0:T(8,128)(2,1)S(1)}, bf16[224,6144]{1,0:T(8,128)(2,1)S(1)}, bf16[224,6144]{1,0:T(8,128)(2,1)S(1)}) custom-call(bf16[224,12288]{1,0:T(8,128)(2,1)} %refs_0_.1, bf16[224,12288]{1,0:T(8,128)(2,1)} %refs_1_.1, bf16[224,12288]{1,0:T(8,128)(2,1)} %refs_2_.2), custom_call_target="tpu_custom_call" | custom-call | bytes 16777216 | tf_op jit(solution)/shard_map/pallas_call | solution.py:73
  38.5 2.3 %collective-permute-start.17 = (bf16[2,128,2048]{2,1,0:T(8,128)(2,1)S(1)}, bf16[2,128,2048]{2,1,0:T(8,128)(2,1)S(1)}, u32[]{:S(2)}, u32[]{:S(2)}) collective-permute-start(bf16[2,128,2048]{2,1,0:T(8,128)(2,1)S(1)} %shard_map.108.refs_0_), channel_id=1, source_target_pairs={{0,24},{1,25},{2,26},{3,27},{4,28},{5,29},{6,30},{7,31},{8,16},{9,... | collective-permute-start | bytes 3145736 | tf_op jit(solution)/shard_map/ppermute | solution.py:52
  40.9 1.5 %collective-permute-start.16 = (bf16[2,128,2048]{2,1,0:T(8,128)(2,1)S(1)}, bf16[2,128,2048]{2,1,0:T(8,128)(2,1)S(1)}, u32[]{:S(2)}, u32[]{:S(2)}) collective-permute-start(bf16[2,128,2048]{2,1,0:T(8,128)(2,1)S(1)} %shard_map.107.refs_1_.refs_2_), channel_id=1, source_target_pairs={{0,6},{1,7},{2,4},{3,5},{4,2},{5,3},{6,0},{7,1},{8,14},{9,15},{10,... | collective-permute-start | bytes 3145736 | tf_op jit(solution)/shard_map/ppermute | solution.py:52
  42.4 1.4 %collective-permute-done.10.second = bf16[2,64,2048]{2,1,0:T(8,128)(2,1)S(1)} collective-permute-done((bf16[2,64,2048]{2,1,0:T(8,128)(2,1)S(1)}, bf16[2,64,2048]{2,1,0:T(8,128)(2,1)S(1)}, u32[]{:S(2)}, u32[]{:S(2)}) %collective-permute-start.10) | collective-permute-done | bytes 524320 | tf_op jit(solution)/shard_map/ppermute | solution.py:52
  43.9 1.7 %collective-permute-start.11 = (bf16[2,128,2048]{2,1,0:T(8,128)(2,1)S(1)}, bf16[2,128,2048]{2,1,0:T(8,128)(2,1)S(1)}, u32[]{:S(2)}, u32[]{:S(2)}) collective-permute-start(bf16[2,128,2048]{2,1,0:T(8,128)(2,1)S(1)} %shard_map.103.refs_2_.refs_4_), channel_id=1, source_target_pairs={{0,33},{1,32},{2,35},{3,34},{4,37},{5,36},{6,39},{7,38},{8,41},{9,... | collective-permute-start | bytes 3145736 | tf_op jit(solution)/shard_map/ppermute | solution.py:52
  45.5 2.9 %shard_map.109.refs_4_ = f32[256,768]{1,0:T(8,128)S(1)} custom-call(bf16[2,128,2048]{2,1,0:T(8,128)(2,1)S(1)} %shard_map.108.refs_0_, bf16[2,128,2048]{2,1,0:T(8,128)(2,1)S(1)} %shard_map.107.refs_1_.refs_2_, bf16[2,128,2048]{2,1,0:T(8,128)(2,1)S(1)} %shard_map.103.refs_2_.refs_4_, bf16[224,6144]{1,0:T(8,128)(2,1)S(1)} %get-tuple-element.36.refs_3_.refs_1_.refs_4_.gate, ...), custom_call_target="tpu_custom_call" | custom-call | flops 1056964608 | bytes 14680064 | tf_op jit(solution)/shard_map/pallas_call | solution.py:73
  48.5 6.1 %collective-permute-done.17.refs_0_.refs_1_ = bf16[2,128,2048]{2,1,0:T(8,128)(2,1)S(1)} collective-permute-done((bf16[2,128,2048]{2,1,0:T(8,128)(2,1)S(1)}, bf16[2,128,2048]{2,1,0:T(8,128)(2,1)S(1)}, u32[]{:S(2)}, u32[]{:S(2)}) %collective-permute-start.17) | collective-permute-done | bytes 1048608 | tf_op jit(solution)/shard_map/ppermute | solution.py:52
  54.6 1.1 shard_map.110.refs_4_
  55.6 1.4 %collective-permute-done.16.refs_0_.refs_3_ = bf16[2,128,2048]{2,1,0:T(8,128)(2,1)S(1)} collective-permute-done((bf16[2,128,2048]{2,1,0:T(8,128)(2,1)S(1)}, bf16[2,128,2048]{2,1,0:T(8,128)(2,1)S(1)}, u32[]{:S(2)}, u32[]{:S(2)}) %collective-permute-start.16) | collective-permute-done | bytes 1048608 | tf_op jit(solution)/shard_map/ppermute | solution.py:52
  57.0 1.1 shard_map.111.refs_4_
  58.1 1.9 %collective-permute-done.11.refs_0_.refs_5_ = bf16[2,128,2048]{2,1,0:T(8,128)(2,1)S(1)} collective-permute-done((bf16[2,128,2048]{2,1,0:T(8,128)(2,1)S(1)}, bf16[2,128,2048]{2,1,0:T(8,128)(2,1)S(1)}, u32[]{:S(2)}, u32[]{:S(2)}) %collective-permute-start.11) | collective-permute-done | bytes 1048608 | tf_op jit(solution)/shard_map/ppermute | solution.py:52
  60.0 1.1 shard_map.112.refs_0_
  61.1 2.3 %collective-permute-done.18.refs_1_ = f32[256,768]{1,0:T(8,128)S(1)} collective-permute-done((f32[256,768]{1,0:T(8,128)S(1)}, f32[256,768]{1,0:T(8,128)S(1)}, u32[]{:S(2)}, u32[]{:S(2)}) %collective-permute-start.18) | collective-permute-done | bytes 786464 | tf_op jit(solution)/shard_map/ppermute | solution.py:52
  63.4 1.9 %shard_map.113 = (bf16[128,2048]{1,0:T(8,128)(2,1)S(1)}, bf16[128,2048]{1,0:T(8,128)(2,1)S(1)}, bf16[128,2048]{1,0:T(8,128)(2,1)S(1)}, bf16[256,224]{1,0:T(8,128...) custom-call(f32[256,768]{1,0:T(8,128)S(1)} %shard_map.112.refs_0_, ...), custom_call_target="tpu_custom_call" | custom-call | flops 704643072 | bytes 8388608 | tf_op jit(solution)/shard_map/pallas_call | solution.py:73
  65.6 1.6 %collective-permute-start.22 = (bf16[128,2048]{1,0:T(8,128)(2,1)S(1)}, bf16[128,2048]{1,0:T(8,128)(2,1)S(1)}, u32[]{:S(2)}, u32[]{:S(2)}) collective-permute-start(bf16[128,2048]{1,0:T(8,128)(2,1)S(1)} %get-tuple-element.45), channel_id=1, source_target_pairs={{0,6},{1,7},{2,4},{3,5},{4,2},{5,3},{6,0},{7,1},{8,14},{9,15},{10,... | collective-permute-start | bytes 1572872 | tf_op jit(solution)/shard_map/ppermute | solution.py:52
  67.2 1.8 %collective-permute-start.25 = (bf16[128,2048]{1,0:T(8,128)(2,1)S(1)}, bf16[128,2048]{1,0:T(8,128)(2,1)S(1)}, u32[]{:S(2)}, u32[]{:S(2)}) collective-permute-start(bf16[128,2048]{1,0:T(8,128)(2,1)S(1)} %get-tuple-element.47), channel_id=1, source_target_pairs={{0,33},{1,32},{2,35},{3,34},{4,37},{5,36},{6,39},{7,38},{8,41},{9,... | collective-permute-start | bytes 1572872 | tf_op jit(solution)/shard_map/ppermute | solution.py:52
  69.0 1.0 shard_map.114
  70.0 4.8 %collective-permute-done.19 = bf16[128,2048]{1,0:T(8,128)(2,1)S(1)} collective-permute-done((bf16[128,2048]{1,0:T(8,128)(2,1)S(1)}, bf16[128,2048]{1,0:T(8,128)(2,1)S(1)}, u32[]{:S(2)}, u32[]{:S(2)}) %collective-permute-start.19) | collective-permute-done | bytes 524320 | tf_op jit(solution)/shard_map/ppermute | solution.py:52
  74.9 1.7 %collective-permute-start.20 = (bf16[64,2048]{1,0:T(8,128)(2,1)S(1)}, bf16[64,2048]{1,0:T(8,128)(2,1)S(1)}, u32[]{:S(2)}, u32[]{:S(2)}) collective-permute-start(bf16[64,2048]{1,0:T(8,128)(2,1)S(1)} %slice.190), channel_id=1, source_target_pairs={{0,33},{1,32},{2,35},{3,34},{4,37},{5,36},{6,39},{7,38},{8,41},{9,... | collective-permute-start | bytes 786440 | tf_op jit(solution)/shard_map/ppermute | solution.py:52
  76.8 1.5 %collective-permute-start.23 = (bf16[64,2048]{1,0:T(8,128)(2,1)S(1)}, bf16[64,2048]{1,0:T(8,128)(2,1)S(1)}, u32[]{:S(2)}, u32[]{:S(2)}) collective-permute-start(bf16[64,2048]{1,0:T(8,128)(2,1)S(1)} %slice.189), channel_id=1, source_target_pairs={{0,8},{1,9},{2,10},{3,11},{4,12},{5,13},{6,14},{7,15},{8,0},{9,1},... | collective-permute-start | bytes 786440 | tf_op jit(solution)/shard_map/ppermute | solution.py:52
  78.4 1.6 %collective-permute-start.26 = (bf16[64,2048]{1,0:T(8,128)(2,1)S(1)}, bf16[64,2048]{1,0:T(8,128)(2,1)S(1)}, u32[]{:S(2)}, u32[]{:S(2)}) collective-permute-start(bf16[64,2048]{1,0:T(8,128)(2,1)S(1)} %slice.188), channel_id=1, source_target_pairs={{0,6},{1,7},{2,4},{3,5},{4,2},{5,3},{6,0},{7,1},{8,14},{9,15},{10,... | collective-permute-start | bytes 786440 | tf_op jit(solution)/shard_map/ppermute | solution.py:52
  80.0 2.6 %collective-permute-done.20 = bf16[64,2048]{1,0:T(8,128)(2,1)S(1)} collective-permute-done((bf16[64,2048]{1,0:T(8,128)(2,1)S(1)}, bf16[64,2048]{1,0:T(8,128)(2,1)S(1)}, u32[]{:S(2)}, u32[]{:S(2)}) %collective-permute-start.20) | collective-permute-done | bytes 262176 | tf_op jit(solution)/shard_map/ppermute | solution.py:52
  82.7 1.6 %collective-permute-start.21 = (bf16[32,2048]{1,0:T(8,128)(2,1)S(1)}, bf16[32,2048]{1,0:T(8,128)(2,1)S(1)}, u32[]{:S(2)}, u32[]{:S(2)}) collective-permute-start(bf16[32,2048]{1,0:T(8,128)(2,1)S(1)} %slice.194), channel_id=1, source_target_pairs={{0,6},{1,7},{2,4},{3,5},{4,2},{5,3},{6,0},{7,1},{8,14},{9,15},{10,... | collective-permute-start | bytes 393224 | tf_op jit(solution)/shard_map/ppermute | solution.py:52
  84.3 1.8 %collective-permute-start.24 = (bf16[32,2048]{1,0:T(8,128)(2,1)S(1)}, bf16[32,2048]{1,0:T(8,128)(2,1)S(1)}, u32[]{:S(2)}, u32[]{:S(2)}) collective-permute-start(bf16[32,2048]{1,0:T(8,128)(2,1)S(1)} %slice.193), channel_id=1, source_target_pairs={{0,33},{1,32},{2,35},{3,34},{4,37},{5,36},{6,39},{7,38},{8,41},{9,... | collective-permute-start | bytes 393224 | tf_op jit(solution)/shard_map/ppermute | solution.py:52
  86.3 1.2 %collective-permute-start.27 = (bf16[32,2048]{1,0:T(8,128)(2,1)S(1)}, bf16[32,2048]{1,0:T(8,128)(2,1)S(1)}, u32[]{:S(2)}, u32[]{:S(2)}) collective-permute-start(bf16[32,2048]{1,0:T(8,128)(2,1)S(1)} %slice.192), channel_id=1, source_target_pairs={{0,8},{1,9},{2,10},{3,11},{4,12},{5,13},{6,14},{7,15},{8,0},{9,1},... | collective-permute-start | bytes 393224 | tf_op jit(solution)/shard_map/ppermute | solution.py:52
  87.5 1.4 %collective-permute-done.21 = bf16[32,2048]{1,0:T(8,128)(2,1)S(1)} collective-permute-done((bf16[32,2048]{1,0:T(8,128)(2,1)S(1)}, bf16[32,2048]{1,0:T(8,128)(2,1)S(1)}, u32[]{:S(2)}, u32[]{:S(2)}) %collective-permute-start.21) | collective-permute-done | bytes 131104 | tf_op jit(solution)/shard_map/ppermute | solution.py:52
  88.9 1.7 %collective-permute-done.24 = bf16[32,2048]{1,0:T(8,128)(2,1)S(1)} collective-permute-done((bf16[32,2048]{1,0:T(8,128)(2,1)S(1)}, bf16[32,2048]{1,0:T(8,128)(2,1)S(1)}, u32[]{:S(2)}, u32[]{:S(2)}) %collective-permute-start.24) | collective-permute-done | bytes 131104 | tf_op jit(solution)/shard_map/ppermute | solution.py:52
  91.4 1.5 %collective-permute-start.28 = (bf16[16,6144]{1,0:T(8,128)(2,1)S(1)}, bf16[16,6144]{1,0:T(8,128)(2,1)S(1)}, u32[]{:S(2)}, u32[]{:S(2)}) collective-permute-start(bf16[16,6144]{1,0:T(8,128)(2,1)S(1)} %slice.191), channel_id=1, source_target_pairs={{0,24},{1,25},{2,26},{3,27},{4,28},{5,29},{6,30},{7,31},{8,16},{9,... | collective-permute-start | bytes 589832 | tf_op jit(solution)/shard_map/ppermute | solution.py:52
  92.9 3.8 %shard_map.115 = (bf16[224,6144]{1,0:T(8,128)(2,1)}, bf16[224,6144]{1,0:T(8,128)(2,1)}, bf16[224,6144]{1,0:T(8,128)(2,1)}) custom-call(bf16[2,128,2048]{2,1,0:T(8,128)(2,1)S(1)} %shard_map.108.refs_0_, bf16[2,128,2048]{2,1,0:T(8,128)(2,1)S(1)} %collective-permute-done.17.refs_0_.refs_1_, bf16[2,128,2048]{2,1,0:T(8,128)(2,1)S(1)} %shard_map.107.refs_1_.refs_2_, ...), custom_call_target="tpu_custom_call" | custom-call | flops 2113929216 | bytes 25165824 | tf_op jit(solution)/shard_map/pallas_call | solution.py:73
  96.7 1.7 %collective-permute-done.28 = bf16[16,6144]{1,0:T(8,128)(2,1)S(1)} collective-permute-done((bf16[16,6144]{1,0:T(8,128)(2,1)S(1)}, bf16[16,6144]{1,0:T(8,128)(2,1)S(1)}, u32[]{:S(2)}, u32[]{:S(2)}) %collective-permute-start.28) | collective-permute-done | bytes 196640 | tf_op jit(solution)/shard_map/ppermute | solution.py:52
  98.7 3.4 %collective-permute-start.30 = (bf16[4,6144]{1,0:T(4,128)(2,1)S(1)}, bf16[4,6144]{1,0:T(4,128)(2,1)S(1)}, u32[]{:S(2)}, u32[]{:S(2)}) collective-permute-start(bf16[4,6144]{1,0:T(4,128)(2,1)S(1)} %get-tuple-element.69), channel_id=1, source_target_pairs={{0,32},{1,33},{2,34},{3,35},{4,36},{5,37},{6,38},{7,39},{8,40},{9,... | collective-permute-start | bytes 147464 | tf_op jit(solution)/shard_map/ppermute | solution.py:52
  102.7 1.0 collective-permute-done.31
  104.4 1.2 %collective-permute-done.32 = bf16[2,6144]{1,0:T(2,128)(2,1)S(1)} collective-permute-done((bf16[2,6144]{1,0:T(2,128)(2,1)S(1)}, bf16[2,6144]{1,0:T(2,128)(2,1)S(1)}, u32[]{:S(2)}, u32[]{:S(2)}) %collective-permute-start.32) | collective-permute-done | bytes 24608 | tf_op jit(solution)/shard_map/ppermute | solution.py:52
  (64 shorter events, 8.3 us)
Async XLA Ops:
  0.6 1.5 %collective-permute-start = (bf16[2,1,12288]{2,0,1:T(2,128)(2,1)}, bf16[2,1,12288]{2,0,1:T(2,128)(2,1)S(1)}, u32[]{:S(2)}, u32[]{:S(2)}) collective-permute-start(bf16[2,1,12288]{2,0,1:T(2,128)(2,1)} %param.7), channel_id=1, source_target_pairs={{0,64},{1,65},{2,66},{3,67},{4,68},{5,69},{6,70},{7,71},{8,72},{9,... | collective-permute-start | bytes 147464 | tf_op jit(solution)/shard_map/ppermute | solution.py:52
  0.7 1.6 %collective-permute-start.1 = (bf16[2,1,12288]{2,0,1:T(2,128)(2,1)}, bf16[2,1,12288]{2,0,1:T(2,128)(2,1)S(1)}, u32[]{:S(2)}, u32[]{:S(2)}) collective-permute-start(bf16[2,1,12288]{2,0,1:T(2,128)(2,1)} %param.8), channel_id=1, source_target_pairs={{0,64},{1,65},{2,66},{3,67},{4,68},{5,69},{6,70},{7,71},{8,72},{9,... | collective-permute-start | bytes 147464 | tf_op jit(solution)/shard_map/ppermute | solution.py:52
  3.4 8.5 %collective-permute-start.8 = (bf16[2,4,6144]{2,1,0:T(4,128)(2,1)S(1)}, bf16[2,4,6144]{2,1,0:T(4,128)(2,1)S(1)}, u32[]{:S(2)}, u32[]{:S(2)}) collective-permute-start(bf16[2,4,6144]{2,1,0:T(4,128)(2,1)S(1)} %fusion.2), channel_id=1, source_target_pairs={{0,42},{1,43},{2,40},{3,41},{4,46},{5,47},{6,44},{7,45},{8,34},{9,... | collective-permute-start | bytes 294920 | tf_op jit(solution)/shard_map/ppermute | solution.py:52
  7.4 6.7 %collective-permute-start.7 = (bf16[2,4,6144]{2,1,0:T(4,128)(2,1)S(1)}, bf16[2,4,6144]{2,1,0:T(4,128)(2,1)S(1)}, u32[]{:S(2)}, u32[]{:S(2)}) collective-permute-start(bf16[2,4,6144]{2,1,0:T(4,128)(2,1)S(1)} %fusion.2), channel_id=1, source_target_pairs={{0,40},{1,41},{2,42},{3,43},{4,44},{5,45},{6,46},{7,47},{8,32},{9,... | collective-permute-start | bytes 294920 | tf_op jit(solution)/shard_map/ppermute | solution.py:52
  7.4 7.0 %collective-permute-start.6 = (bf16[2,4,6144]{2,1,0:T(4,128)(2,1)S(1)}, bf16[2,4,6144]{2,1,0:T(4,128)(2,1)S(1)}, u32[]{:S(2)}, u32[]{:S(2)}) collective-permute-start(bf16[2,4,6144]{2,1,0:T(4,128)(2,1)S(1)} %fusion.2), channel_id=1, source_target_pairs={{0,10},{1,11},{2,8},{3,9},{4,14},{5,15},{6,12},{7,13},{8,2},{9,3},... | collective-permute-start | bytes 294920 | tf_op jit(solution)/shard_map/ppermute | solution.py:52
  9.3 5.7 %collective-permute-start.5 = (bf16[2,4,6144]{2,1,0:T(4,128)(2,1)S(1)}, bf16[2,4,6144]{2,1,0:T(4,128)(2,1)S(1)}, u32[]{:S(2)}, u32[]{:S(2)}) collective-permute-start(bf16[2,4,6144]{2,1,0:T(4,128)(2,1)S(1)} %fusion.2), channel_id=1, source_target_pairs={{0,8},{1,9},{2,10},{3,11},{4,12},{5,13},{6,14},{7,15},{8,0},{9,1},... | collective-permute-start | bytes 294920 | tf_op jit(solution)/shard_map/ppermute | solution.py:52
  9.5 6.0 %collective-permute-start.4 = (bf16[2,4,6144]{2,1,0:T(4,128)(2,1)S(1)}, bf16[2,4,6144]{2,1,0:T(4,128)(2,1)S(1)}, u32[]{:S(2)}, u32[]{:S(2)}) collective-permute-start(bf16[2,4,6144]{2,1,0:T(4,128)(2,1)S(1)} %fusion.2), channel_id=1, source_target_pairs={{0,34},{1,35},{2,32},{3,33},{4,38},{5,39},{6,36},{7,37},{8,42},{9,... | collective-permute-start | bytes 294920 | tf_op jit(solution)/shard_map/ppermute | solution.py:52
  11.9 4.6 %collective-permute-start.3 = (bf16[2,4,6144]{2,1,0:T(4,128)(2,1)S(1)}, bf16[2,4,6144]{2,1,0:T(4,128)(2,1)S(1)}, u32[]{:S(2)}, u32[]{:S(2)}) collective-permute-start(bf16[2,4,6144]{2,1,0:T(4,128)(2,1)S(1)} %fusion.2), channel_id=1, source_target_pairs={{0,32},{1,33},{2,34},{3,35},{4,36},{5,37},{6,38},{7,39},{8,40},{9,... | collective-permute-start | bytes 294920 | tf_op jit(solution)/shard_map/ppermute | solution.py:52
  14.0 4.6 %collective-permute-start.2 = (bf16[2,4,6144]{2,1,0:T(4,128)(2,1)S(1)}, bf16[2,4,6144]{2,1,0:T(4,128)(2,1)S(1)}, u32[]{:S(2)}, u32[]{:S(2)}) collective-permute-start(bf16[2,4,6144]{2,1,0:T(4,128)(2,1)S(1)} %fusion.2), channel_id=1, source_target_pairs={{0,2},{1,3},{2,0},{3,1},{4,6},{5,7},{6,4},{7,5},{8,10},{9,11},{10,... | collective-permute-start | bytes 294920 | tf_op jit(solution)/shard_map/ppermute | solution.py:52
  19.5 8.4 %collective-permute-start.12 = (bf16[2,32,2048]{2,1,0:T(8,128)(2,1)S(1)}, bf16[2,32,2048]{2,1,0:T(8,128)(2,1)S(1)}, u32[]{:S(2)}, u32[]{:S(2)}) collective-permute-start(bf16[2,32,2048]{2,1,0:T(8,128)(2,1)S(1)} %get-tuple-element.65.first), channel_id=1, source_target_pairs={{0,6},{1,7},{2,4},{3,5},{4,2},{5,3},{6,0},{7,1},{8,14},{9,15},{10,... | collective-permute-start | bytes 786440 | tf_op jit(solution)/shard_map/ppermute | solution.py:52
  21.6 8.0 %collective-permute-start.14 = (bf16[2,32,2048]{2,1,0:T(8,128)(2,1)S(1)}, bf16[2,32,2048]{2,1,0:T(8,128)(2,1)S(1)}, u32[]{:S(2)}, u32[]{:S(2)}) collective-permute-start(bf16[2,32,2048]{2,1,0:T(8,128)(2,1)S(1)} %get-tuple-element.64.first), channel_id=1, source_target_pairs={{0,33},{1,32},{2,35},{3,34},{4,37},{5,36},{6,39},{7,38},{8,41},{9,... | collective-permute-start | bytes 786440 | tf_op jit(solution)/shard_map/ppermute | solution.py:52
  23.0 10.3 %collective-permute-start.9 = (bf16[2,32,2048]{2,1,0:T(8,128)(2,1)S(1)}, bf16[2,32,2048]{2,1,0:T(8,128)(2,1)S(1)}, u32[]{:S(2)}, u32[]{:S(2)}) collective-permute-start(bf16[2,32,2048]{2,1,0:T(8,128)(2,1)S(1)} %get-tuple-element.66.first), channel_id=1, source_target_pairs={{0,24},{1,25},{2,26},{3,27},{4,28},{5,29},{6,30},{7,31},{8,16},{9,... | collective-permute-start | bytes 786440 | tf_op jit(solution)/shard_map/ppermute | solution.py:52
  27.9 10.5 %collective-permute-start.13 = (bf16[2,64,2048]{2,1,0:T(8,128)(2,1)S(1)}, bf16[2,64,2048]{2,1,0:T(8,128)(2,1)S(1)}, u32[]{:S(2)}, u32[]{:S(2)}) collective-permute-start(bf16[2,64,2048]{2,1,0:T(8,128)(2,1)S(1)} %shard_map.104.first), channel_id=1, source_target_pairs={{0,33},{1,32},{2,35},{3,34},{4,37},{5,36},{6,39},{7,38},{8,41},{9,... | collective-permute-start | bytes 1572872 | tf_op jit(solution)/shard_map/ppermute | solution.py:52
  29.7 11.2 %collective-permute-start.15 = (bf16[2,64,2048]{2,1,0:T(8,128)(2,1)S(1)}, bf16[2,64,2048]{2,1,0:T(8,128)(2,1)S(1)}, u32[]{:S(2)}, u32[]{:S(2)}) collective-permute-start(bf16[2,64,2048]{2,1,0:T(8,128)(2,1)S(1)} %shard_map.106.first), channel_id=1, source_target_pairs={{0,24},{1,25},{2,26},{3,27},{4,28},{5,29},{6,30},{7,31},{8,16},{9,... | collective-permute-start | bytes 1572872 | tf_op jit(solution)/shard_map/ppermute | solution.py:52
  33.3 10.5 %collective-permute-start.10 = (bf16[2,64,2048]{2,1,0:T(8,128)(2,1)S(1)}, bf16[2,64,2048]{2,1,0:T(8,128)(2,1)S(1)}, u32[]{:S(2)}, u32[]{:S(2)}) collective-permute-start(bf16[2,64,2048]{2,1,0:T(8,128)(2,1)S(1)} %shard_map.102.first), channel_id=1, source_target_pairs={{0,6},{1,7},{2,4},{3,5},{4,2},{5,3},{6,0},{7,1},{8,14},{9,15},{10,... | collective-permute-start | bytes 1572872 | tf_op jit(solution)/shard_map/ppermute | solution.py:52
  38.5 16.1 %collective-permute-start.17 = (bf16[2,128,2048]{2,1,0:T(8,128)(2,1)S(1)}, bf16[2,128,2048]{2,1,0:T(8,128)(2,1)S(1)}, u32[]{:S(2)}, u32[]{:S(2)}) collective-permute-start(bf16[2,128,2048]{2,1,0:T(8,128)(2,1)S(1)} %shard_map.108.refs_0_), channel_id=1, source_target_pairs={{0,24},{1,25},{2,26},{3,27},{4,28},{5,29},{6,30},{7,31},{8,16},{9,... | collective-permute-start | bytes 3145736 | tf_op jit(solution)/shard_map/ppermute | solution.py:52
  40.9 16.1 %collective-permute-start.16 = (bf16[2,128,2048]{2,1,0:T(8,128)(2,1)S(1)}, bf16[2,128,2048]{2,1,0:T(8,128)(2,1)S(1)}, u32[]{:S(2)}, u32[]{:S(2)}) collective-permute-start(bf16[2,128,2048]{2,1,0:T(8,128)(2,1)S(1)} %shard_map.107.refs_1_.refs_2_), channel_id=1, source_target_pairs={{0,6},{1,7},{2,4},{3,5},{4,2},{5,3},{6,0},{7,1},{8,14},{9,15},{10,... | collective-permute-start | bytes 3145736 | tf_op jit(solution)/shard_map/ppermute | solution.py:52
  43.9 16.1 %collective-permute-start.11 = (bf16[2,128,2048]{2,1,0:T(8,128)(2,1)S(1)}, bf16[2,128,2048]{2,1,0:T(8,128)(2,1)S(1)}, u32[]{:S(2)}, u32[]{:S(2)}) collective-permute-start(bf16[2,128,2048]{2,1,0:T(8,128)(2,1)S(1)} %shard_map.103.refs_2_.refs_4_), channel_id=1, source_target_pairs={{0,33},{1,32},{2,35},{3,34},{4,37},{5,36},{6,39},{7,38},{8,41},{9,... | collective-permute-start | bytes 3145736 | tf_op jit(solution)/shard_map/ppermute | solution.py:52
  58.1 5.3 %copy-start = (bf16[256,256]{1,0:T(8,128)(2,1)S(1)}, bf16[256,256]{1,0:T(8,128)(2,1)}, u32[]{:S(2)}) copy-start(bf16[256,256]{1,0:T(8,128)(2,1)} %constant.13.clone.refs_3_) | copy-start | bytes 393220
  58.1 5.3 %copy-start.1 = (bf16[256,256]{1,0:T(8,128)(2,1)S(1)}, bf16[256,256]{1,0:T(8,128)(2,1)}, u32[]{:S(2)}) copy-start(bf16[256,256]{1,0:T(8,128)(2,1)} %constant.12.clone.refs_2_) | copy-start | bytes 393220
  61.0 2.4 %collective-permute-start.18 = (f32[256,768]{1,0:T(8,128)S(1)}, f32[256,768]{1,0:T(8,128)S(1)}, u32[]{:S(2)}, u32[]{:S(2)}) collective-permute-start(f32[256,768]{1,0:T(8,128)S(1)} %shard_map.112.refs_0_), channel_id=1, source_target_pairs={{0,64},{1,65},{2,66},{3,67},{4,68},{5,69},{6,70},{7,71},{8,72},{9,... | collective-permute-start | bytes 2359304 | tf_op jit(solution)/shard_map/ppermute | solution.py:52
  65.3 9.4 %collective-permute-start.19 = (bf16[128,2048]{1,0:T(8,128)(2,1)S(1)}, bf16[128,2048]{1,0:T(8,128)(2,1)S(1)}, u32[]{:S(2)}, u32[]{:S(2)}) collective-permute-start(bf16[128,2048]{1,0:T(8,128)(2,1)S(1)} %get-tuple-element.43), channel_id=1, source_target_pairs={{0,8},{1,9},{2,10},{3,11},{4,12},{5,13},{6,14},{7,15},{8,0},{9,1},... | collective-permute-start | bytes 1572872 | tf_op jit(solution)/shard_map/ppermute | solution.py:52
  65.6 11.0 %collective-permute-start.22 = (bf16[128,2048]{1,0:T(8,128)(2,1)S(1)}, bf16[128,2048]{1,0:T(8,128)(2,1)S(1)}, u32[]{:S(2)}, u32[]{:S(2)}) collective-permute-start(bf16[128,2048]{1,0:T(8,128)(2,1)S(1)} %get-tuple-element.45), channel_id=1, source_target_pairs={{0,6},{1,7},{2,4},{3,5},{4,2},{5,3},{6,0},{7,1},{8,14},{9,15},{10,... | collective-permute-start | bytes 1572872 | tf_op jit(solution)/shard_map/ppermute | solution.py:52
  67.2 11.0 %collective-permute-start.25 = (bf16[128,2048]{1,0:T(8,128)(2,1)S(1)}, bf16[128,2048]{1,0:T(8,128)(2,1)S(1)}, u32[]{:S(2)}, u32[]{:S(2)}) collective-permute-start(bf16[128,2048]{1,0:T(8,128)(2,1)S(1)} %get-tuple-element.47), channel_id=1, source_target_pairs={{0,33},{1,32},{2,35},{3,34},{4,37},{5,36},{6,39},{7,38},{8,41},{9,... | collective-permute-start | bytes 1572872 | tf_op jit(solution)/shard_map/ppermute | solution.py:52
  74.9 7.7 %collective-permute-start.20 = (bf16[64,2048]{1,0:T(8,128)(2,1)S(1)}, bf16[64,2048]{1,0:T(8,128)(2,1)S(1)}, u32[]{:S(2)}, u32[]{:S(2)}) collective-permute-start(bf16[64,2048]{1,0:T(8,128)(2,1)S(1)} %slice.190), channel_id=1, source_target_pairs={{0,33},{1,32},{2,35},{3,34},{4,37},{5,36},{6,39},{7,38},{8,41},{9,... | collective-permute-start | bytes 786440 | tf_op jit(solution)/shard_map/ppermute | solution.py:52
  76.8 7.5 %collective-permute-start.23 = (bf16[64,2048]{1,0:T(8,128)(2,1)S(1)}, bf16[64,2048]{1,0:T(8,128)(2,1)S(1)}, u32[]{:S(2)}, u32[]{:S(2)}) collective-permute-start(bf16[64,2048]{1,0:T(8,128)(2,1)S(1)} %slice.189), channel_id=1, source_target_pairs={{0,8},{1,9},{2,10},{3,11},{4,12},{5,13},{6,14},{7,15},{8,0},{9,1},... | collective-permute-start | bytes 786440 | tf_op jit(solution)/shard_map/ppermute | solution.py:52
  78.4 7.8 %collective-permute-start.26 = (bf16[64,2048]{1,0:T(8,128)(2,1)S(1)}, bf16[64,2048]{1,0:T(8,128)(2,1)S(1)}, u32[]{:S(2)}, u32[]{:S(2)}) collective-permute-start(bf16[64,2048]{1,0:T(8,128)(2,1)S(1)} %slice.188), channel_id=1, source_target_pairs={{0,6},{1,7},{2,4},{3,5},{4,2},{5,3},{6,0},{7,1},{8,14},{9,15},{10,... | collective-permute-start | bytes 786440 | tf_op jit(solution)/shard_map/ppermute | solution.py:52
  82.7 6.3 %collective-permute-start.21 = (bf16[32,2048]{1,0:T(8,128)(2,1)S(1)}, bf16[32,2048]{1,0:T(8,128)(2,1)S(1)}, u32[]{:S(2)}, u32[]{:S(2)}) collective-permute-start(bf16[32,2048]{1,0:T(8,128)(2,1)S(1)} %slice.194), channel_id=1, source_target_pairs={{0,6},{1,7},{2,4},{3,5},{4,2},{5,3},{6,0},{7,1},{8,14},{9,15},{10,... | collective-permute-start | bytes 393224 | tf_op jit(solution)/shard_map/ppermute | solution.py:52
  84.3 6.3 %collective-permute-start.24 = (bf16[32,2048]{1,0:T(8,128)(2,1)S(1)}, bf16[32,2048]{1,0:T(8,128)(2,1)S(1)}, u32[]{:S(2)}, u32[]{:S(2)}) collective-permute-start(bf16[32,2048]{1,0:T(8,128)(2,1)S(1)} %slice.193), channel_id=1, source_target_pairs={{0,33},{1,32},{2,35},{3,34},{4,37},{5,36},{6,39},{7,38},{8,41},{9,... | collective-permute-start | bytes 393224 | tf_op jit(solution)/shard_map/ppermute | solution.py:52
  86.3 5.0 %collective-permute-start.27 = (bf16[32,2048]{1,0:T(8,128)(2,1)S(1)}, bf16[32,2048]{1,0:T(8,128)(2,1)S(1)}, u32[]{:S(2)}, u32[]{:S(2)}) collective-permute-start(bf16[32,2048]{1,0:T(8,128)(2,1)S(1)} %slice.192), channel_id=1, source_target_pairs={{0,8},{1,9},{2,10},{3,11},{4,12},{5,13},{6,14},{7,15},{8,0},{9,1},... | collective-permute-start | bytes 393224 | tf_op jit(solution)/shard_map/ppermute | solution.py:52
  91.4 7.0 %collective-permute-start.28 = (bf16[16,6144]{1,0:T(8,128)(2,1)S(1)}, bf16[16,6144]{1,0:T(8,128)(2,1)S(1)}, u32[]{:S(2)}, u32[]{:S(2)}) collective-permute-start(bf16[16,6144]{1,0:T(8,128)(2,1)S(1)} %slice.191), channel_id=1, source_target_pairs={{0,24},{1,25},{2,26},{3,27},{4,28},{5,29},{6,30},{7,31},{8,16},{9,... | collective-permute-start | bytes 589832 | tf_op jit(solution)/shard_map/ppermute | solution.py:52
  98.5 4.2 %collective-permute-start.29 = (bf16[4,6144]{1,0:T(4,128)(2,1)S(1)}, bf16[4,6144]{1,0:T(4,128)(2,1)S(1)}, u32[]{:S(2)}, u32[]{:S(2)}) collective-permute-start(bf16[4,6144]{1,0:T(4,128)(2,1)S(1)} %get-tuple-element.67), channel_id=1, source_target_pairs={{0,2},{1,3},{2,0},{3,1},{4,6},{5,7},{6,4},{7,5},{8,10},{9,11},{10,... | collective-permute-start | bytes 147464 | tf_op jit(solution)/shard_map/ppermute | solution.py:52
  98.6 5.1 %collective-permute-start.31 = (bf16[4,6144]{1,0:T(4,128)(2,1)S(1)}, bf16[4,6144]{1,0:T(4,128)(2,1)S(1)}, u32[]{:S(2)}, u32[]{:S(2)}) collective-permute-start(bf16[4,6144]{1,0:T(4,128)(2,1)S(1)} %get-tuple-element.68), channel_id=1, source_target_pairs={{0,34},{1,35},{2,32},{3,33},{4,38},{5,39},{6,36},{7,37},{8,42},{9,... | collective-permute-start | bytes 147464 | tf_op jit(solution)/shard_map/ppermute | solution.py:52
  98.7 5.5 %collective-permute-start.30 = (bf16[4,6144]{1,0:T(4,128)(2,1)S(1)}, bf16[4,6144]{1,0:T(4,128)(2,1)S(1)}, u32[]{:S(2)}, u32[]{:S(2)}) collective-permute-start(bf16[4,6144]{1,0:T(4,128)(2,1)S(1)} %get-tuple-element.69), channel_id=1, source_target_pairs={{0,32},{1,33},{2,34},{3,35},{4,36},{5,37},{6,38},{7,39},{8,40},{9,... | collective-permute-start | bytes 147464 | tf_op jit(solution)/shard_map/ppermute | solution.py:52
  104.3 1.3 %collective-permute-start.32 = (bf16[2,6144]{1,0:T(2,128)(2,1)S(1)}, bf16[2,6144]{1,0:T(2,128)(2,1)S(1)}, u32[]{:S(2)}, u32[]{:S(2)}) collective-permute-start(bf16[2,6144]{1,0:T(2,128)(2,1)S(1)} %broadcast_select_fusion.2), channel_id=1, source_target_pairs={{0,64},{1,65},{2,66},{3,67},{4,68},{5,69},{6,70},{7,71},{8,72},{9,... | collective-permute-start | bytes 73736 | tf_op jit(solution)/shard_map/ppermute | solution.py:52
